TPU v7x, 32 devices: a whole 2x2x4 slice. The times are simulated.
32 devices in a mesh: fsdp: 4 (over y, x), ctx: 2 (over core), tp: 4 (over z).
Axes of the slice: x: 2, y: 2, z: 4, core: 2. Of those that a mesh axis runs over, the one named last changes fastest.
Arguments:
- inputs: bfloat16 [4, 1500, 1280], P('fsdp', 'ctx'), may hold values from -6 to 6
- lengths: int32 [4], P('fsdp'), may hold values from 375 to 1500, as said below
- cotangent: bfloat16 [4, 1500, 1280], P('fsdp', 'ctx'), may hold values from -6 to 6
- norm_gains: float32 [2, 2, 1280], replicated, may hold values from 0.5 to 1.5
- norm_shifts: float32 [2, 2, 1280], replicated, may hold values from -1 to 1
- qkv_weight: bfloat16 [2, 1280, 3, 1280], P(None, 'fsdp', None, 'tp'), may hold values from -0.15625 to 0.15625
- qv_bias: float32 [2, 2, 1280], P(None, None, 'tp'), may hold values from -1.5 to 1.5
- out_weight: bfloat16 [2, 1280, 1280], P(None, 'fsdp', 'tp'), may hold values from -0.625 to 0.625
- out_bias: float32 [2, 1280], replicated, may hold values from -1.5 to 1.5
- up_weight: bfloat16 [2, 1280, 5120], P(None, 'fsdp', 'tp'), may hold values from -0.15625 to 0.15625
- up_bias: float32 [2, 5120], P(None, 'tp'), may hold values from -1.5 to 1.5
- down_weight: bfloat16 [2, 1280, 5120], P(None, 'fsdp', 'tp'), may hold values from -0.125 to 0.125
- down_bias: float32 [2, 1280], replicated, may hold values from -1.5 to 1.5
Outputs:
- outputs: bfloat16 [4, 1500, 1280], P('fsdp', 'ctx')
- input_grad: float32 [4, 1500, 1280], P('fsdp', 'ctx')
- grad_norm_gains: float32 [2, 2, 1280], replicated
- grad_norm_shifts: float32 [2, 2, 1280], replicated
- grad_qkv: float32 [2, 1280, 3, 1280], P(None, 'fsdp', None, 'tp')
- grad_qv_bias: float32 [2, 2, 1280], P(None, None, 'tp')
- grad_out_weight: float32 [2, 1280, 1280], P(None, 'fsdp', 'tp')
- grad_out_bias: float32 [2, 1280], replicated
- grad_up_weight: float32 [2, 1280, 5120], P(None, 'fsdp', 'tp')
- grad_up_bias: float32 [2, 5120], P(None, 'tp')
- grad_down_weight: float32 [2, 1280, 5120], P(None, 'fsdp', 'tp')
- grad_down_bias: float32 [2, 1280], replicated
Inputs may be any that keep to these rules, and one draw needn't show every extreme that they name: `lengths`: every clip has a length over 750, and some clip has length exactly 1500.
All inputs are finite; a program needn't handle non-finite values.
Results may differ from a plain program's by a relative error of at most 0.018.
Values may be sent and summed in bfloat16 or wider, within the bound.
No kernel may reach another device: no remote copies, remote signals or barrier semaphores. Data moves between devices by JAX's collectives and lax.ppermute only.
A program may use at most 256 MiB of HBM per device.

v0:
```python
import jax
import jax.numpy as jnp
from jax import lax
from jax.sharding import PartitionSpec as P

HEAD_DIM = 80


epsilon = 1e-05


def normalize(rows, gain, shift):
    center = jnp.mean(rows, axis=-1, keepdims=True)
    centred = rows - center
    spread = jnp.mean(centred * centred, axis=-1, keepdims=True)
    return centred * lax.rsqrt(spread + epsilon) * gain + shift


def gelu_exact(values):
    return jax.nn.gelu(values, approximate=False)


def masked_scores(queries, pairs, key_valid, local_heads):
    clips, rows = (queries.shape[0], queries.shape[1])
    span = pairs.shape[2]
    head_q = queries.reshape(clips, rows, local_heads, HEAD_DIM)
    head_k = pairs[0].reshape(clips, span, local_heads, HEAD_DIM)
    scores = jnp.einsum(
        "crhe,cshe->chrs", head_q, head_k, preferred_element_type=jnp.float32
    ) * HEAD_DIM ** (-0.5)
    return jnp.where(key_valid[:, None, None, :], scores, -1e30)


def per_device(
    inputs,
    lengths,
    cotangent,
    norm_gains,
    norm_shifts,
    qkv_weight,
    qv_bias,
    out_weight,
    out_bias,
    up_weight,
    up_bias,
    down_weight,
    down_bias,
):
    clips, rows, width = inputs.shape
    local_width = qkv_weight.shape[-1]
    local_heads = local_width // HEAD_DIM
    span = rows * lax.axis_size("ctx")
    offset = lax.axis_index("ctx") * rows
    scale = HEAD_DIM ** (-0.5)
    key_valid = jnp.arange(span)[None, :] < lengths[:, None]
    row_live = (offset + jnp.arange(rows))[None, :] < lengths[:, None]
    hidden = inputs.astype(jnp.float32)
    layers = norm_gains.shape[0]
    saved = []
    for layer in range(layers):
        weights = (
            lax.all_gather(qkv_weight[layer], "fsdp", axis=0, tiled=True),
            lax.all_gather(out_weight[layer], "fsdp", axis=0, tiled=True),
            lax.all_gather(up_weight[layer], "fsdp", axis=0, tiled=True),
            lax.all_gather(down_weight[layer], "fsdp", axis=0, tiled=True),
        )
        w_qkv, w_out, w_up, w_down = weights
        normed = normalize(hidden, norm_gains[layer, 0], norm_shifts[layer, 0]).astype(jnp.bfloat16)
        mixed = jnp.einsum("crd,dte->tcre", normed, w_qkv, preferred_element_type=jnp.float32)
        queries = (mixed[0] + qv_bias[layer, 0]).astype(jnp.bfloat16)
        own_pairs = jnp.stack(
            [mixed[1].astype(jnp.bfloat16), (mixed[2] + qv_bias[layer, 1]).astype(jnp.bfloat16)]
        )
        pairs = lax.all_gather(own_pairs, "ctx", axis=2, tiled=True)
        scores = masked_scores(queries, pairs, key_valid, local_heads)
        top = jnp.max(scores, axis=-1, keepdims=True)
        expon = jnp.exp(scores - top)
        total = jnp.sum(expon, axis=-1, keepdims=True)
        probs = (expon / total).astype(jnp.bfloat16)
        head_v = pairs[1].reshape(clips, span, local_heads, HEAD_DIM)
        attended = jnp.einsum("chrs,cshe->crhe", probs, head_v, preferred_element_type=jnp.float32)
        attended = attended.reshape(clips, rows, local_width).astype(jnp.bfloat16)
        partial_value = jnp.einsum(
            "cre,de->crd", attended, w_out, preferred_element_type=jnp.float32
        )
        middle = (
            hidden
            + lax.psum(partial_value.astype(jnp.bfloat16), "tp").astype(jnp.float32)
            + out_bias[layer]
        )
        normed2 = normalize(middle, norm_gains[layer, 1], norm_shifts[layer, 1]).astype(
            jnp.bfloat16
        )
        upper = (
            jnp.einsum("crd,df->crf", normed2, w_up, preferred_element_type=jnp.float32)
            + up_bias[layer]
        )
        active = gelu_exact(upper).astype(jnp.bfloat16)
        partial_value = jnp.einsum(
            "crf,df->crd", active, w_down, preferred_element_type=jnp.float32
        )
        new_hidden = (
            middle
            + lax.psum(partial_value.astype(jnp.bfloat16), "tp").astype(jnp.float32)
            + down_bias[layer]
        )
        kept_pairs = pairs
        saved.append(
            (
                hidden,
                normed,
                queries,
                kept_pairs,
                top,
                total,
                attended,
                middle,
                normed2,
                upper,
                active,
                weights,
            )
        )
        hidden = new_hidden
    outputs = hidden.astype(jnp.bfloat16)
    grad = cotangent.astype(jnp.float32) * row_live[:, :, None].astype(jnp.float32)
    results = [None] * layers
    for layer in reversed(range(layers)):
        (
            hidden,
            normed,
            queries,
            kept_pairs,
            top,
            total,
            attended,
            middle,
            normed2,
            upper,
            active,
            weights,
        ) = saved[layer]
        w_qkv, w_out, w_up, w_down = weights
        grad_down_bias = jnp.sum(grad, axis=(0, 1))
        grad_low = grad.astype(jnp.bfloat16)
        grad_down = jnp.einsum("crd,crf->df", grad_low, active, preferred_element_type=jnp.float32)
        d_active = jnp.einsum("crd,df->crf", grad_low, w_down, preferred_element_type=jnp.float32)
        unused, gelu_back = jax.vjp(gelu_exact, upper)
        d_upper = gelu_back(d_active)[0].astype(jnp.bfloat16)
        grad_up_bias = jnp.sum(d_upper.astype(jnp.float32), axis=(0, 1))
        grad_up = jnp.einsum("crd,crf->df", normed2, d_upper, preferred_element_type=jnp.float32)
        partial_value = jnp.einsum("crf,df->crd", d_upper, w_up, preferred_element_type=jnp.float32)
        d_normed2 = lax.psum(partial_value.astype(jnp.bfloat16), "tp").astype(jnp.float32)
        unused, norm_back = jax.vjp(normalize, middle, norm_gains[layer, 1], norm_shifts[layer, 1])
        d_middle, gain_second, shift_second = norm_back(d_normed2)
        grad = grad + d_middle
        grad_out_bias = jnp.sum(grad, axis=(0, 1))
        grad_low = grad.astype(jnp.bfloat16)
        grad_out = jnp.einsum("crd,cre->de", grad_low, attended, preferred_element_type=jnp.float32)
        d_attended = jnp.einsum("crd,de->cre", grad_low, w_out, preferred_element_type=jnp.float32)
        d_attended = d_attended.astype(jnp.bfloat16).reshape(clips, rows, local_heads, HEAD_DIM)
        pairs = kept_pairs
        scores = masked_scores(queries, pairs, key_valid, local_heads)
        probs = jnp.exp(scores - top) / total
        probs_low = probs.astype(jnp.bfloat16)
        head_k = pairs[0].reshape(clips, span, local_heads, HEAD_DIM)
        head_v = pairs[1].reshape(clips, span, local_heads, HEAD_DIM)
        head_q = queries.reshape(clips, rows, local_heads, HEAD_DIM)
        d_values = jnp.einsum(
            "chrs,crhe->cshe", probs_low, d_attended, preferred_element_type=jnp.float32
        )
        d_probs = jnp.einsum(
            "crhe,cshe->chrs", d_attended, head_v, preferred_element_type=jnp.float32
        )
        d_scores = probs * (d_probs - jnp.sum(probs * d_probs, axis=-1, keepdims=True))
        d_scores = d_scores.astype(jnp.bfloat16)
        d_queries = (
            jnp.einsum("chrs,cshe->crhe", d_scores, head_k, preferred_element_type=jnp.float32)
            * scale
        )
        d_keys = (
            jnp.einsum("chrs,crhe->cshe", d_scores, head_q, preferred_element_type=jnp.float32)
            * scale
        )
        both = jnp.stack([d_keys, d_values]).reshape(2, clips, span, local_width)
        d_pairs = lax.psum_scatter(
            both.astype(jnp.bfloat16), "ctx", scatter_dimension=2, tiled=True
        ).astype(jnp.float32)
        d_mixed = jnp.stack([d_queries.reshape(clips, rows, local_width), d_pairs[0], d_pairs[1]])
        d_mixed = d_mixed.astype(jnp.bfloat16)
        grad_qv = jnp.stack(
            [
                jnp.sum(d_mixed[0].astype(jnp.float32), axis=(0, 1)),
                jnp.sum(d_mixed[2].astype(jnp.float32), axis=(0, 1)),
            ]
        )
        grad_qkv = jnp.einsum("crd,tcre->dte", normed, d_mixed, preferred_element_type=jnp.float32)
        partial_value = jnp.einsum(
            "tcre,dte->crd", d_mixed, w_qkv, preferred_element_type=jnp.float32
        )
        d_normed = lax.psum(partial_value.astype(jnp.bfloat16), "tp").astype(jnp.float32)
        unused, norm_back = jax.vjp(normalize, hidden, norm_gains[layer, 0], norm_shifts[layer, 0])
        d_hidden, gain_first, shift_first = norm_back(d_normed)
        grad = grad + d_hidden
        matrices = (grad_qkv, grad_out, grad_up, grad_down)
        owned = (
            lax.psum_scatter(
                matrices[0].astype(jnp.bfloat16), "fsdp", scatter_dimension=0, tiled=True
            ).astype(jnp.float32),
            lax.psum_scatter(
                matrices[1].astype(jnp.bfloat16), "fsdp", scatter_dimension=0, tiled=True
            ).astype(jnp.float32),
            lax.psum_scatter(
                matrices[2].astype(jnp.bfloat16), "fsdp", scatter_dimension=0, tiled=True
            ).astype(jnp.float32),
            lax.psum_scatter(
                matrices[3].astype(jnp.bfloat16), "fsdp", scatter_dimension=0, tiled=True
            ).astype(jnp.float32),
        )
        owned = (
            lax.psum(owned[0].astype(jnp.bfloat16), "ctx").astype(jnp.float32),
            lax.psum(owned[1].astype(jnp.bfloat16), "ctx").astype(jnp.float32),
            lax.psum(owned[2].astype(jnp.bfloat16), "ctx").astype(jnp.float32),
            lax.psum(owned[3].astype(jnp.bfloat16), "ctx").astype(jnp.float32),
        )
        gains_both = jnp.stack([gain_first, gain_second])
        shifts_both = jnp.stack([shift_first, shift_second])
        vectors = lax.psum(
            (gains_both, shifts_both, grad_qv, grad_out_bias, grad_up_bias, grad_down_bias),
            ("fsdp", "ctx"),
        )
        results[layer] = (owned, vectors)

    def stacked(outer, inner):
        return jnp.stack([results[layer][outer][inner] for layer in range(layers)])

    return (
        outputs,
        grad,
        stacked(1, 0),
        stacked(1, 1),
        stacked(0, 0),
        stacked(1, 2),
        stacked(0, 1),
        stacked(1, 3),
        stacked(0, 2),
        stacked(1, 4),
        stacked(0, 3),
        stacked(1, 5),
    )


def solution(mesh):
    in_specs = (
        P("fsdp", "ctx", None),
        P("fsdp"),
        P("fsdp", "ctx", None),
        P(),
        P(),
        P(None, "fsdp", None, "tp"),
        P(None, None, "tp"),
        P(None, "fsdp", "tp"),
        P(),
        P(None, "fsdp", "tp"),
        P(None, "tp"),
        P(None, "fsdp", "tp"),
        P(),
    )
    out_specs = (
        P("fsdp", "ctx", None),
        P("fsdp", "ctx", None),
        P(),
        P(),
        P(None, "fsdp", None, "tp"),
        P(None, None, "tp"),
        P(None, "fsdp", "tp"),
        P(),
        P(None, "fsdp", "tp"),
        P(None, "tp"),
        P(None, "fsdp", "tp"),
        P(),
    )
    return jax.shard_map(
        per_device, mesh=mesh, in_specs=in_specs, out_specs=out_specs, check_vma=False
    )
```

profile of v0, /device:TPU:1, one launch (start us, length us, event | category | flops | bytes accessed | tf_op | source)
XLA Modules:
  0.0 1727.7 jit_solution(15113540060973155712)
XLA Ops:
  13.8 50.3 %all-gather.21.cloned.1.call-done = bf16[1,1280,3,320]{3,2,0,1:T(4,128)(2,1)} async-done(((bf16[1,320,3,320]{3,2,0,1:T(4,128)(2,1)}), bf16[1,1280,3,320]{3,2,0,1:T(4,128)(2,1)}) %all-gather.21.cloned.1.call-update) | async-done | bytes 2457616 | tf_op jit(solution)/shard_map/all_gather | solution.py:62
  64.1 7.4 copy.33
  76.9 4.7 copy.34
  83.5 12.3 all-gather.1
  95.8 7.3 fusion.190
  103.1 6.4 copy.36
  109.5 6.4 copy.35
  115.9 10.9 fusion.195
  126.8 9.5 fusion.134
  147.1 74.2 %all-reduce.17.cloned.1.call-done = bf16[1,750,1280]{2,1,0:T(8,128)(2,1)} async-done(((bf16[1,750,1280]{2,1,0:T(8,128)(2,1)}), bf16[1,750,1280]{2,1,0:T(8,128)(2,1)}) %all-reduce.17.cloned.1.call-update) | async-done | bytes 1920016 | tf_op jit(solution)/shard_map/psum | solution.py:88
  224.7 43.1 %all-gather.23.cloned.1.call-done = bf16[1,1280,1280]{2,1,0:T(8,128)(2,1)} async-done(((bf16[1,320,1280]{2,1,0:T(8,128)(2,1)}), bf16[1,1280,1280]{2,1,0:T(8,128)(2,1)}) %all-gather.23.cloned.1.call-update) | async-done | bytes 3276816 | tf_op jit(solution)/shard_map/all_gather | solution.py:64
  267.8 15.7 multiply_convert_fusion.3
  283.5 31.1 %all-gather.25.cloned.1.call-done = bf16[1,1280,1280]{2,1,0:T(8,128)(2,1)} async-done(((bf16[1,320,1280]{2,1,0:T(8,128)(2,1)}), bf16[1,1280,1280]{2,1,0:T(8,128)(2,1)}) %all-gather.25.cloned.1.call-update) | async-done | bytes 3276816 | tf_op jit(solution)/shard_map/all_gather | solution.py:65
  314.6 6.5 fusion.70
  322.2 45.2 %all-gather.27.cloned.1.call-done = bf16[1,1280,3,320]{3,2,0,1:T(4,128)(2,1)} async-done(((bf16[1,320,3,320]{3,2,0,1:T(4,128)(2,1)}), bf16[1,1280,3,320]{3,2,0,1:T(4,128)(2,1)}) %all-gather.27.cloned.1.call-update) | async-done | bytes 2457616 | tf_op jit(solution)/shard_map/all_gather | solution.py:62
  367.4 7.4 copy.38
  374.9 76.3 %all-reduce.19.cloned.1.call-done = bf16[1,750,1280]{2,1,0:T(8,128)(2,1)} async-done(((bf16[1,750,1280]{2,1,0:T(8,128)(2,1)}), bf16[1,750,1280]{2,1,0:T(8,128)(2,1)}) %all-reduce.19.cloned.1.call-update) | async-done | bytes 1920016 | tf_op jit(solution)/shard_map/psum | solution.py:104
  463.1 12.9 all-gather.5
  476.1 6.9 fusion.189
  483.0 6.4 copy.41
  489.4 5.2 copy.40
  494.6 10.9 fusion.196
  505.5 9.3 fusion.137
  519.6 79.1 %all-reduce.21.cloned.1.call-done = bf16[1,750,1280]{2,1,0:T(8,128)(2,1)} async-done(((bf16[1,750,1280]{2,1,0:T(8,128)(2,1)}), bf16[1,750,1280]{2,1,0:T(8,128)(2,1)}) %all-reduce.21.cloned.1.call-update) | async-done | bytes 1920016 | tf_op jit(solution)/shard_map/psum | solution.py:88
  604.4 40.7 %all-gather.29.cloned.1.call-done = bf16[1,1280,1280]{2,1,0:T(8,128)(2,1)} async-done(((bf16[1,320,1280]{2,1,0:T(8,128)(2,1)}), bf16[1,1280,1280]{2,1,0:T(8,128)(2,1)}) %all-gather.29.cloned.1.call-update) | async-done | bytes 3276816 | tf_op jit(solution)/shard_map/all_gather | solution.py:64
  645.1 15.2 multiply_convert_fusion.2
  660.3 31.8 %all-gather.31.cloned.1.call-done = bf16[1,1280,1280]{2,1,0:T(8,128)(2,1)} async-done(((bf16[1,320,1280]{2,1,0:T(8,128)(2,1)}), bf16[1,1280,1280]{2,1,0:T(8,128)(2,1)}) %all-gather.31.cloned.1.call-update) | async-done | bytes 3276816 | tf_op jit(solution)/shard_map/all_gather | solution.py:65
  692.1 9.1 convert_reduce_fusion.5
  706.6 80.6 %all-reduce.23.cloned.1.call-done = bf16[1,750,1280]{2,1,0:T(8,128)(2,1)} async-done(((bf16[1,750,1280]{2,1,0:T(8,128)(2,1)}), bf16[1,750,1280]{2,1,0:T(8,128)(2,1)}) %all-reduce.23.cloned.1.call-update) | async-done | bytes 1920016 | tf_op jit(solution)/shard_map/psum | solution.py:153
  787.2 4.6 convert_reduce_fusion.3
  799.8 7.5 fusion.93
  807.4 11.6 multiply_reduce_fusion.1
  818.9 12.4 multiply_convert_fusion.1
  838.3 7.4 convert_reduce_fusion.7
  845.7 11.4 all-reduce.29.cloned.1.call-done
  859.8 4.5 fusion.84
  864.4 81.6 %all-reduce.25.cloned.1.call-done = bf16[1,750,1280]{2,1,0:T(8,128)(2,1)} async-done(((bf16[1,750,1280]{2,1,0:T(8,128)(2,1)}), bf16[1,750,1280]{2,1,0:T(8,128)(2,1)}) %all-reduce.25.cloned.1.call-update) | async-done | bytes 1920016 | tf_op jit(solution)/shard_map/psum | solution.py:201
  967.3 79.8 %all-reduce.27.cloned.1.call-done = bf16[1,750,1280]{2,1,0:T(8,128)(2,1)} async-done(((bf16[1,750,1280]{2,1,0:T(8,128)(2,1)}), bf16[1,750,1280]{2,1,0:T(8,128)(2,1)}) %all-reduce.27.cloned.1.call-update) | async-done | bytes 1920016 | tf_op jit(solution)/shard_map/psum | solution.py:153
  1058.8 7.6 fusion.90
  1066.4 11.5 multiply_reduce_fusion
  1077.9 12.7 multiply_convert_fusion
  1095.9 6.6 fusion.73
  1102.5 6.9 convert_reduce_fusion.8
  1109.4 6.9 all-reduce.31.cloned.1.call-done
  1119.0 5.2 fusion.85
  1129.6 8.1 convolution_convert_fusion.2
  1138.2 6.7 convolution_convert_fusion
  1145.0 7.0 convolution_convert_fusion.4
  1156.6 7.4 convolution_convert_fusion.1
  1164.2 7.1 convolution_convert_fusion.3
  1171.6 4.9 convolution_convert_fusion.5
  1185.7 83.9 %all-reduce.35.cloned.1.call-done = (bf16[1,750,1280]{2,1,0:T(8,128)(2,1)}, bf16[1,750,1280]{2,1,0:T(8,128)(2,1)}) async-done(((bf16[1,750,1280]{2,1,0:T(8,128)(2,1)}, bf16[1,750,1280]{2,1,0:T(8,128)(2,1)}), (bf16[1,750,1280]{2,1,0:T(8,128)(2,1)}, bf16[1,750,1280]{2,1,0:T(8,128)(2,1)})) %all-reduce.35.cloned.1.call-update) | async-done | bytes 3840016 | tf_op jit(solution)/shard_map/psum | solution.py:104
  1276.3 22.7 %reduce-scatter.17.cloned.1.call-done = bf16[320,320]{1,0:T(8,128)(2,1)} async-done(((bf16[1280,320]{1,0:T(8,128)(2,1)}), bf16[320,320]{1,0:T(8,128)(2,1)}) %reduce-scatter.17.cloned.1.call-update) | async-done | bytes 204816 | tf_op jit(solution)/shard_map/reduce_scatter | solution.py:210
  1298.9 49.0 %reduce-scatter.21.cloned.1.call-done = bf16[320,1280]{1,0:T(8,128)(2,1)} async-done(((bf16[1280,1280]{1,0:T(8,128)(2,1)}), bf16[320,1280]{1,0:T(8,128)(2,1)}) %reduce-scatter.21.cloned.1.call-update) | async-done | bytes 819216 | tf_op jit(solution)/shard_map/reduce_scatter | solution.py:213
  1347.9 48.8 %reduce-scatter.25.cloned.1.call-done = bf16[320,1280]{1,0:T(8,128)(2,1)} async-done(((bf16[1280,1280]{1,0:T(8,128)(2,1)}), bf16[320,1280]{1,0:T(8,128)(2,1)}) %reduce-scatter.25.cloned.1.call-update) | async-done | bytes 819216 | tf_op jit(solution)/shard_map/reduce_scatter | solution.py:216
  1396.7 46.2 %reduce-scatter.13.cloned.1.call-done = bf16[320,3,320]{2,0,1:T(8,128)(2,1)} async-done(((bf16[1280,3,320]{2,0,1:T(8,128)(2,1)}), bf16[320,3,320]{2,0,1:T(8,128)(2,1)}) %reduce-scatter.13.cloned.1.call-update) | async-done | bytes 614416 | tf_op jit(solution)/shard_map/reduce_scatter | solution.py:207
  1442.9 30.5 %reduce-scatter.15.cloned.1.call-done = bf16[320,320]{1,0:T(8,128)(2,1)} async-done(((bf16[1280,320]{1,0:T(8,128)(2,1)}), bf16[320,320]{1,0:T(8,128)(2,1)}) %reduce-scatter.15.cloned.1.call-update) | async-done | bytes 204816 | tf_op jit(solution)/shard_map/reduce_scatter | solution.py:210
  1473.4 48.4 %reduce-scatter.23.cloned.1.call-done = bf16[320,1280]{1,0:T(8,128)(2,1)} async-done(((bf16[1280,1280]{1,0:T(8,128)(2,1)}), bf16[320,1280]{1,0:T(8,128)(2,1)}) %reduce-scatter.23.cloned.1.call-update) | async-done | bytes 819216 | tf_op jit(solution)/shard_map/reduce_scatter | solution.py:216
  1521.8 48.8 %reduce-scatter.19.cloned.1.call-done = bf16[320,1280]{1,0:T(8,128)(2,1)} async-done(((bf16[1280,1280]{1,0:T(8,128)(2,1)}), bf16[320,1280]{1,0:T(8,128)(2,1)}) %reduce-scatter.19.cloned.1.call-update) | async-done | bytes 819216 | tf_op jit(solution)/shard_map/reduce_scatter | solution.py:213
  1570.6 45.6 %reduce-scatter.11.cloned.1.call-done = bf16[320,3,320]{2,0,1:T(8,128)(2,1)} async-done(((bf16[1280,3,320]{2,0,1:T(8,128)(2,1)}), bf16[320,3,320]{2,0,1:T(8,128)(2,1)}) %reduce-scatter.11.cloned.1.call-update) | async-done | bytes 614416 | tf_op jit(solution)/shard_map/reduce_scatter | solution.py:207
  1616.3 4.7 add_add_fusion.4
  1621.0 8.1 copy.46
  1630.9 46.8 %all-reduce.33.cloned.1.call-done = (f32[1,2,1280]{2,1,0:T(2,128)}, f32[1,2,1280]{2,1,0:T(2,128)}, f32[1,2,1280]{2,1,0:T(2,128)}, f32[1,2,1280]{2,1,0:T(2,128)},...) async-done(((f32[1,2,1280]{2,1,0:T(2,128)}, ...) | async-done | bytes 76816 | tf_op jit(solution)/shard_map/psum | solution.py:228
  1683.1 28.8 %all-reduce.37.cloned.1.call-done = (bf16[1,320,3,320]{3,1,2,0:T(8,128)(2,1)}, bf16[1,320,3,320]{3,1,2,0:T(8,128)(2,1)}, bf16[1,320,320]{2,1,0:T(8,128)(2,1)}, b...) async-done(((bf16[1,320,3,320]{3,1,2,0:T(8,128)(2,1)}, ...) | async-done | bytes 4915216 | tf_op jit(solution)/shard_map/psum | solution.py:221
  (403 shorter events, 155.6 us)
Async XLA Ops:
  7.2 56.9 %all-gather.21.cloned.1.call-start = ((), (), s32[]{:S(2)}) async-start(), calls=%async_computation.24 | async-start | bytes 4915200 | tf_op jit(solution)/shard_map/all_gather | solution.py:62
  11.4 84.4 %all-gather.17.cloned.1.call-start = ((), (), s32[]{:S(2)}) async-start(), calls=%async_computation.8 | async-start | bytes 3456000 | tf_op jit(solution)/shard_map/all_gather | solution.py:74
  12.1 59.5 %copy-start.50 = (f32[1280]{0:T(1024)}, f32[1280]{0:T(1024)S(1)}, u32[]{:S(2)}) copy-start(f32[1280]{0:T(1024)S(1)} %get-tuple-element.54) | copy-start | bytes 15364
  12.1 255.7 %copy-start.52 = (f32[1280]{0:T(1024)}, f32[1280]{0:T(1024)S(1)}, u32[]{:S(2)}) copy-start(f32[1280]{0:T(1024)S(1)} %get-tuple-element.53) | copy-start | bytes 15364
  12.1 442.8 %copy-start.56 = (f32[1280]{0:T(1024)}, f32[1280]{0:T(1024)S(1)}, u32[]{:S(2)}) copy-start(f32[1280]{0:T(1024)S(1)} %get-tuple-element.55) | copy-start | bytes 15364
  12.1 782.4 %copy-start.54 = (f32[1280]{0:T(1024)}, f32[1280]{0:T(1024)S(1)}, u32[]{:S(2)}) copy-start(f32[1280]{0:T(1024)S(1)} %get-tuple-element.52) | copy-start | bytes 15364
  12.8 58.8 %copy-start.100 = (f32[1280]{0:T(1024)}, f32[1280]{0:T(1024)S(1)}, u32[]{:S(2)}) copy-start(f32[1280]{0:T(1024)S(1)} %get-tuple-element.58) | copy-start | bytes 15364
  12.8 255.0 %copy-start.102 = (f32[1280]{0:T(1024)}, f32[1280]{0:T(1024)S(1)}, u32[]{:S(2)}) copy-start(f32[1280]{0:T(1024)S(1)} %get-tuple-element.57) | copy-start | bytes 15364
  12.8 442.2 %copy-start.104 = (f32[1280]{0:T(1024)}, f32[1280]{0:T(1024)S(1)}, u32[]{:S(2)}) copy-start(f32[1280]{0:T(1024)S(1)} %get-tuple-element.59) | copy-start | bytes 15364
  13.1 58.5 %copy-start.58 = (f32[750]{0:T(1024)}, f32[750]{0:T(1024)S(1)}, u32[]{:S(2)}) copy-start(f32[750]{0:T(1024)S(1)} %broadcast_multiply_fusion.3) | copy-start | bytes 9004
  13.8 61.8 %copy-start.72 = (f32[750]{0:T(1024)}, f32[750]{0:T(1024)S(1)}, u32[]{:S(2)}) copy-start(f32[750]{0:T(1024)S(1)} %fusion.35) | copy-start | bytes 9004
  13.8 61.8 %copy-start.68 = (f32[750]{0:T(1024)}, f32[750]{0:T(1024)S(1)}, u32[]{:S(2)}) copy-start(f32[750]{0:T(1024)S(1)} %fusion.155) | copy-start | bytes 9004
  75.8 40.1 %copy-start.20 = (f32[1,1,750,320]{2,3,0,1:T(8,128)}, f32[1,1,750,320]{2,3,0,1:T(8,128)S(1)}, u32[]{:S(2)}) copy-start(f32[1,1,750,320]{2,3,0,1:T(8,128)S(1)} %get-tuple-element.108) | copy-start | bytes 2880004
  81.6 139.7 %all-reduce.17.cloned.1.call-start = ((), (), s32[]{:S(2)}) async-start(), calls=%async_computation.9 | async-start | bytes 3850240 | tf_op jit(solution)/shard_map/psum | solution.py:88
  82.4 33.5 %copy-start.66 = (f32[4,80]{1,0:T(4,128)}, f32[4,80]{1,0:T(4,128)S(1)}, u32[]{:S(2)}) copy-start(f32[4,80]{1,0:T(4,128)S(1)} %add.325) | copy-start | bytes 3844
  82.4 33.5 %copy-start.109 = (pred[1500]{0:T(1024)(128)(4,1)}, pred[1500]{0:T(1024)(128)(4,1)S(1)}, u32[]{:S(2)}) copy-start(pred[1500]{0:T(1024)(128)(4,1)S(1)} %iota_compare_fusion) | copy-start | bytes 4504
  138.9 128.9 %all-gather.23.cloned.1.call-start = ((), (), s32[]{:S(2)}) async-start(), calls=%async_computation.25 | async-start | bytes 4096000 | tf_op jit(solution)/shard_map/all_gather | solution.py:64
  141.7 172.9 %all-gather.25.cloned.1.call-start = ((), (), s32[]{:S(2)}) async-start(), calls=%async_computation.26 | async-start | bytes 4096000 | tf_op jit(solution)/shard_map/all_gather | solution.py:65
  144.4 223.0 %all-gather.27.cloned.1.call-start = ((), (), s32[]{:S(2)}) async-start(), calls=%async_computation.27 | async-start | bytes 4915200 | tf_op jit(solution)/shard_map/all_gather | solution.py:62
  146.1 305.1 %all-reduce.19.cloned.1.call-start = ((), (), s32[]{:S(2)}) async-start(), calls=%async_computation.10 | async-start | bytes 3850240 | tf_op jit(solution)/shard_map/psum | solution.py:104
  146.4 304.7 %copy-start.48 = (f32[1280]{0:T(1024)}, f32[1280]{0:T(1024)S(1)}, u32[]{:S(2)}) copy-start(f32[1280]{0:T(1024)S(1)} %get-tuple-element.65) | copy-start | bytes 15364
  223.7 59.8 %copy-start.60 = (f32[750]{0:T(1024)}, f32[750]{0:T(1024)S(1)}, u32[]{:S(2)}) copy-start(f32[750]{0:T(1024)S(1)} %broadcast_multiply_fusion.2) | copy-start | bytes 9004
  224.7 58.8 %copy-start.78 = (f32[750]{0:T(1024)}, f32[750]{0:T(1024)S(1)}, u32[]{:S(2)}) copy-start(f32[750]{0:T(1024)S(1)} %multiply_reduce_fusion.4) | copy-start | bytes 9004
  224.7 58.8 %copy-start.70 = (f32[750]{0:T(1024)}, f32[750]{0:T(1024)S(1)}, u32[]{:S(2)}) copy-start(f32[750]{0:T(1024)S(1)} %fusion.156) | copy-start | bytes 9004
  321.1 155.0 %all-gather.19.cloned.1.call-start = ((), (), s32[]{:S(2)}) async-start(), calls=%async_computation.11 | async-start | bytes 3456000 | tf_op jit(solution)/shard_map/all_gather | solution.py:74
  463.0 135.7 %all-reduce.21.cloned.1.call-start = ((), (), s32[]{:S(2)}) async-start(), calls=%async_computation.12 | async-start | bytes 3850240 | tf_op jit(solution)/shard_map/psum | solution.py:88
  518.1 127.1 %all-gather.29.cloned.1.call-start = ((), (), s32[]{:S(2)}) async-start(), calls=%async_computation.28 | async-start | bytes 4096000 | tf_op jit(solution)/shard_map/all_gather | solution.py:64
  518.6 173.4 %all-gather.31.cloned.1.call-start = ((), (), s32[]{:S(2)}) async-start(), calls=%async_computation.29 | async-start | bytes 4096000 | tf_op jit(solution)/shard_map/all_gather | solution.py:65
  519.4 267.8 %all-reduce.23.cloned.1.call-start = ((), (), s32[]{:S(2)}) async-start(), calls=%async_computation.13 | async-start | bytes 3850240 | tf_op jit(solution)/shard_map/psum | solution.py:153
  519.6 274.9 %copy-start.89 = (f32[750]{0:T(1024)}, f32[750]{0:T(1024)S(1)}, u32[]{:S(2)}) copy-start(f32[750]{0:T(1024)S(1)} %fusion.154) | copy-start | bytes 9004
  602.0 43.2 %copy-start.98 = (f32[1280]{0:T(1024)S(1)}, f32[1280]{0:T(1024)}, u32[]{:S(2)}) copy-start(f32[1280]{0:T(1024)} %get-tuple-element.62) | copy-start | bytes 15364
  602.0 43.2 %copy-start.106 = (f32[1280]{0:T(1024)S(1)}, f32[1280]{0:T(1024)}, u32[]{:S(2)}) copy-start(f32[1280]{0:T(1024)} %get-tuple-element.56) | copy-start | bytes 15364
  602.0 192.5 %copy-start.64 = (f32[750]{0:T(1024)}, f32[750]{0:T(1024)S(1)}, u32[]{:S(2)}) copy-start(f32[750]{0:T(1024)S(1)} %broadcast_multiply_fusion) | copy-start | bytes 9004
  604.4 190.2 %copy-start.76 = (f32[750]{0:T(1024)}, f32[750]{0:T(1024)S(1)}, u32[]{:S(2)}) copy-start(f32[750]{0:T(1024)S(1)} %fusion.158) | copy-start | bytes 9004
  706.3 150.8 %all-reduce.29.cloned.1.call-start = ((), (), s32[]{:S(2)}) async-start(), calls=%async_computation.30 | async-start | bytes 3932160
  836.5 109.6 %all-reduce.25.cloned.1.call-start = ((), (), s32[]{:S(2)}) async-start(), calls=%async_computation.14 | async-start | bytes 3850240 | tf_op jit(solution)/shard_map/psum | solution.py:201
  838.3 21.5 %copy-start.29 = (bf16[1,1280,3,320]{1,3,2,0:T(8,128)(2,1)S(1)}, bf16[1,1280,3,320]{1,3,2,0:T(8,128)(2,1)}, u32[]{:S(2)}) copy-start(bf16[1,1280,3,320]{1,3,2,0:T(8,128)(2,1)} %copy.38) | copy-start | bytes 7372804
  859.8 86.3 %copy-start.57 = (f32[1280]{0:T(1024)S(1)}, f32[1280]{0:T(1024)}, u32[]{:S(2)}) copy-start(f32[1280]{0:T(1024)} %copy-done.56) | copy-start | bytes 15364
  859.8 86.3 %copy-start.63 = (f32[750]{0:T(1024)S(1)}, f32[750]{0:T(1024)}, u32[]{:S(2)}) copy-start(f32[750]{0:T(1024)} %copy-done.62) | copy-start | bytes 9004
  864.3 85.7 %copy-start.81 = (f32[750]{0:T(1024)S(1)}, f32[750]{0:T(1024)}, u32[]{:S(2)}) copy-start(f32[750]{0:T(1024)} %copy-done.80) | copy-start | bytes 9004
  864.3 85.7 %copy-start.75 = (f32[750]{0:T(1024)S(1)}, f32[750]{0:T(1024)}, u32[]{:S(2)}) copy-start(f32[750]{0:T(1024)} %copy-done.74) | copy-start | bytes 9004
  864.3 182.8 %all-reduce.27.cloned.1.call-start = ((), (), s32[]{:S(2)}) async-start(), calls=%async_computation.15 | async-start | bytes 3850240 | tf_op jit(solution)/shard_map/psum | solution.py:153
  963.2 83.9 %copy-start.1 = (bf16[1,750,1280]{2,1,0:T(8,128)(2,1)S(1)}, bf16[1,750,1280]{2,1,0:T(8,128)(2,1)}, u32[]{:S(2)}) copy-start(bf16[1,750,1280]{2,1,0:T(8,128)(2,1)} %param.13) | copy-start | bytes 5760004
  963.2 83.9 %copy-start.49 = (f32[1280]{0:T(1024)S(1)}, f32[1280]{0:T(1024)}, u32[]{:S(2)}) copy-start(f32[1280]{0:T(1024)} %copy-done.48) | copy-start | bytes 15364
  963.2 83.9 %copy-start.53 = (f32[1280]{0:T(1024)S(1)}, f32[1280]{0:T(1024)}, u32[]{:S(2)}) copy-start(f32[1280]{0:T(1024)} %copy-done.52) | copy-start | bytes 15364
  963.2 83.9 %copy-start.61 = (f32[750]{0:T(1024)S(1)}, f32[750]{0:T(1024)}, u32[]{:S(2)}) copy-start(f32[750]{0:T(1024)} %copy-done.60) | copy-start | bytes 9004
  967.1 83.9 %copy-start.79 = (f32[750]{0:T(1024)S(1)}, f32[750]{0:T(1024)}, u32[]{:S(2)}) copy-start(f32[750]{0:T(1024)} %copy-done.78) | copy-start | bytes 9004
  967.1 83.9 %copy-start.71 = (f32[750]{0:T(1024)S(1)}, f32[750]{0:T(1024)}, u32[]{:S(2)}) copy-start(f32[750]{0:T(1024)} %copy-done.70) | copy-start | bytes 9004
  967.1 149.2 %all-reduce.31.cloned.1.call-start = ((), (), s32[]{:S(2)}) async-start(), calls=%async_computation.31 | async-start | bytes 3932160
  1077.9 12.7 copy-start.21
  1077.9 12.7 copy-start.67
  1095.7 173.9 %all-reduce.35.cloned.1.call-start = ((), (), s32[]{:S(2)}) async-start(), calls=%async_computation.33 | async-start | bytes 7700480 | tf_op jit(solution)/shard_map/psum | solution.py:104
  1109.4 14.8 copy-start.43
  1124.3 174.7 %reduce-scatter.17.cloned.1.call-start = ((), (), s32[]{:S(2)}) async-start(), calls=%async_computation.19 | async-start | bytes 1228800 | tf_op jit(solution)/shard_map/reduce_scatter | solution.py:210
  1129.5 218.4 %reduce-scatter.21.cloned.1.call-start = ((), (), s32[]{:S(2)}) async-start(), calls=%async_computation.21 | async-start | bytes 4096000 | tf_op jit(solution)/shard_map/reduce_scatter | solution.py:213
  1137.8 258.9 %reduce-scatter.25.cloned.1.call-start = ((), (), s32[]{:S(2)}) async-start(), calls=%async_computation.23 | async-start | bytes 4096000 | tf_op jit(solution)/shard_map/reduce_scatter | solution.py:216
  1145.0 298.0 %reduce-scatter.13.cloned.1.call-start = ((), (), s32[]{:S(2)}) async-start(), calls=%async_computation.17 | async-start | bytes 3686400 | tf_op jit(solution)/shard_map/reduce_scatter | solution.py:207
  1152.0 321.4 %reduce-scatter.15.cloned.1.call-start = ((), (), s32[]{:S(2)}) async-start(), calls=%async_computation.18 | async-start | bytes 1228800 | tf_op jit(solution)/shard_map/reduce_scatter | solution.py:210
  1156.5 365.3 %reduce-scatter.23.cloned.1.call-start = ((), (), s32[]{:S(2)}) async-start(), calls=%async_computation.22 | async-start | bytes 4096000 | tf_op jit(solution)/shard_map/reduce_scatter | solution.py:216
  1164.0 406.6 %reduce-scatter.19.cloned.1.call-start = ((), (), s32[]{:S(2)}) async-start(), calls=%async_computation.20 | async-start | bytes 4096000 | tf_op jit(solution)/shard_map/reduce_scatter | solution.py:213
  1171.4 444.8 %reduce-scatter.11.cloned.1.call-start = ((), (), s32[]{:S(2)}) async-start(), calls=%async_computation.16 | async-start | bytes 3686400 | tf_op jit(solution)/shard_map/reduce_scatter | solution.py:207
  1176.5 96.0 %copy-start.73 = (f32[750]{0:T(1024)S(1)}, f32[750]{0:T(1024)}, u32[]{:S(2)}) copy-start(f32[750]{0:T(1024)} %copy-done.72) | copy-start | bytes 9004
  1176.5 501.2 %all-reduce.33.cloned.1.call-start = ((), (), s32[]{:S(2)}) async-start(), calls=%async_computation.32 | async-start | bytes 155648 | tf_op jit(solution)/shard_map/psum | solution.py:228
  1276.0 435.9 %all-reduce.37.cloned.1.call-start = ((), (), s32[]{:S(2)}) async-start(), calls=%async_computation.34 | async-start | bytes 10485760 | tf_op jit(solution)/shard_map/psum | solution.py:221
  (82 other events, 424.0 us)
Sparse Core Ops, SparseCore 0:
  11.5 52.5 all-gather.20
  81.7 11.2 all-gather.16
  139.0 82.2 all-reduce.16
  223.6 44.1 all-gather.22
  269.5 45.0 all-gather.24
  316.9 50.5 all-gather.26
  370.4 80.7 all-reduce.18
  463.1 10.3 all-gather.18
  518.2 80.4 all-reduce.20
  600.9 44.1 all-gather.28
  647.0 45.0 all-gather.30
  706.4 80.7 all-reduce.22
  836.6 20.4 all-reduce.28
  864.5 81.5 all-reduce.24
  967.2 79.8 all-reduce.26
  1095.8 20.4 all-reduce.30
  1124.3 145.1 all-reduce.34
  1272.6 26.2 reduce-scatter.16
  1302.8 45.0 reduce-scatter.20
  1351.6 45.0 reduce-scatter.24
  1400.6 42.2 reduce-scatter.12
  1446.2 27.2 reduce-scatter.14
  1476.7 45.0 reduce-scatter.22
  1525.6 45.0 reduce-scatter.18
  1574.0 42.2 reduce-scatter.10
  1622.6 55.0 all-reduce.32
  1680.9 30.9 all-reduce.36
where the time goes:
time: 1730 us
  waiting for transfers between devices  1230 us (71%)
  matrix products  234 us (14%)
  local copies, waits for them, and re-layouts  114 us (7%)
  other arithmetic  99.8 us (6%)
  blocking collectives  25.2 us (1%)
  between operations  17.5 us (1%)
    psum x7, waiting for transfers between devices, per_device(): lax.psum(partial_value.astype(jnp.bfloat16), 'tp').astype(jnp.float32)  556 us
    reduce_scatter x2, waiting for transfers between devices, per_device(): lax.psum_scatter(matrices[2].astype(jnp.bfloat16), 'fsdp', scatter_dimens...  97.8 us
    reduce_scatter x2, waiting for transfers between devices, per_device(): lax.psum_scatter(matrices[3].astype(jnp.bfloat16), 'fsdp', scatter_dimens...  97.2 us
    all_gather x2, waiting for transfers between devices, per_device(): lax.all_gather(qkv_weight[layer], 'fsdp', axis=0, tiled=True)  95.5 us
    reduce_scatter x2, waiting for transfers between devices, per_device(): lax.psum_scatter(matrices[0].astype(jnp.bfloat16), 'fsdp', scatter_dimens...  91.9 us
    all_gather x2, waiting for transfers between devices, per_device(): lax.all_gather(up_weight[layer], 'fsdp', axis=0, tiled=True)  83.8 us
    all_gather x2, waiting for transfers between devices, per_device(): lax.all_gather(down_weight[layer], 'fsdp', axis=0, tiled=True)  62.8 us
    reduce_scatter x2, waiting for transfers between devices, per_device(): lax.psum_scatter(matrices[1].astype(jnp.bfloat16), 'fsdp', scatter_dimens...  53.2 us
  transfers between devices with their start and end apart: 27, of which 25 were waited for; matrix products, arithmetic and copies ran while one was open for 10% of the time, Pallas kernels for 0%

commit v1 on v0

v1 whole, which is shorter than its diff:
```python
import functools

import jax
import jax.numpy as jnp
import numpy as np
from jax import lax
from jax.experimental import pallas as pl
from jax.experimental.pallas import tpu as pltpu
from jax.sharding import PartitionSpec as P

HEAD_DIM = 80
LANES = 128
EPSILON = 1e-05
NEG = -1e30
CHUNKS = 3
SCALE = HEAD_DIM**-0.5
SCALE2 = SCALE * float(np.log2(np.e))
BF = jnp.bfloat16
F32 = jnp.float32
NT = (((1,), (1,)), ((), ()))
NN = (((1,), (0,)), ((), ()))


def mm(a, b, dims=NN):
    return lax.dot_general(a, b, dims, preferred_element_type=F32)


def lane_iota(shape):
    return lax.broadcasted_iota(jnp.int32, shape, 1)


def split3(v):
    hi = v.astype(BF).astype(F32)
    mid = (v - hi).astype(BF).astype(F32)
    return hi, mid, v - hi - mid


def attn_fwd_kernel(q_ref, k0_ref, v0_ref, k1_ref, v1_ref, o_ref, qa_ref):
    q = q_ref[...]
    s0 = mm(q, k0_ref[0], NT)
    s1 = mm(q, k1_ref[0], NT)
    top = jnp.maximum(jnp.max(s0, axis=1, keepdims=True), jnp.max(s1, axis=1, keepdims=True))
    p0 = jnp.exp2((s0 - top) * SCALE2).astype(BF)
    p1 = jnp.exp2((s1 - top) * SCALE2).astype(BF)
    o = mm(p0, v0_ref[0]) + mm(p1, v1_ref[0])
    lane = lane_iota(o.shape)
    total = jnp.sum(jnp.where(lane == HEAD_DIM, o, 0.0), axis=1, keepdims=True)
    o_ref[...] = jnp.where(lane < HEAD_DIM, o / total, 0.0).astype(BF)
    lse = top + jnp.log2(total) * (1.0 / SCALE2)
    hi, mid, lo = split3(-lse)
    qa = jnp.where(lane == HEAD_DIM + 1, hi, q.astype(F32))
    qa = jnp.where(lane == HEAD_DIM + 2, mid, qa)
    qa = jnp.where(lane == HEAD_DIM + 3, lo, qa)
    qa_ref[...] = qa.astype(BF)


def attn_fwd(q, kv0, kv1):
    rows, width = q.shape
    span = kv0.shape[1]
    heads = width // LANES
    qspec = pl.BlockSpec((rows, LANES), lambda h: (0, h))
    kspec = pl.BlockSpec((1, span, LANES), lambda h: (0, 0, h))
    vspec = pl.BlockSpec((1, span, LANES), lambda h: (1, 0, h))
    return pl.pallas_call(
        attn_fwd_kernel,
        grid=(heads,),
        in_specs=[qspec, kspec, vspec, kspec, vspec],
        out_specs=[qspec, qspec],
        out_shape=[jax.ShapeDtypeStruct((rows, width), BF)] * 2,
        compiler_params=pltpu.CompilerParams(vmem_limit_bytes=32 * 1024 * 1024),
        cost_estimate=pl.CostEstimate(
            flops=8 * rows * span * width, bytes_accessed=8 * span * width, transcendentals=2 * rows * span * heads
        ),
        name="attn_fwd",
    )(q, kv0, kv0, kv1, kv1)


def attn_bwd_kernel(first, qa_ref, o_ref, do_ref, k0_ref, v0_ref, k1_ref, v1_ref, *refs):
    if first:
        dq_ref, dk0_ref, dv0_ref, dk1_ref, dv1_ref = refs
        olds = (None,) * 4
    else:
        olds = refs[:4]
        dq_ref, dk0_ref, dv0_ref, dk1_ref, dv1_ref = refs[4:]
    qa = qa_ref[...]
    o = o_ref[...].astype(F32)
    do = do_ref[...].astype(F32)
    lane = lane_iota(do.shape)
    delta = -jnp.sum(o * do, axis=1, keepdims=True)
    hi = delta.astype(BF).astype(F32)
    doa = jnp.where(lane == HEAD_DIM, hi, do)
    doa = jnp.where(lane == HEAD_DIM + 1, delta - hi, doa).astype(BF)
    dqt = None
    for k_ref, v_ref, dk_ref, dv_ref, dk_old, dv_old in (
        (k0_ref, v0_ref, dk0_ref, dv0_ref, olds[0], olds[1]),
        (k1_ref, v1_ref, dk1_ref, dv1_ref, olds[2], olds[3]),
    ):
        k = k_ref[0]
        st = mm(k, qa, NT)
        pt = jnp.exp2(st * SCALE2)
        dpt = mm(v_ref[0], doa, NT)
        dst = (pt * dpt).astype(BF)
        dv = mm(pt.astype(BF), doa)
        dk = mm(dst, qa)
        dv_ref[...] = dv if first else dv_old[...] + dv
        dk_ref[...] = dk if first else dk_old[...] + dk
        part = mm(k.T, dst)
        dqt = part if dqt is None else dqt + part
    dq_ref[...] = (dqt.T * SCALE).astype(BF)


def attn_bwd(qa, o, do, kv0, kv1, sums):
    rows, width = qa.shape
    span = kv0.shape[1]
    heads = width // LANES
    qspec = pl.BlockSpec((rows, LANES), lambda h: (0, h))
    kspec = pl.BlockSpec((1, span, LANES), lambda h: (0, 0, h))
    vspec = pl.BlockSpec((1, span, LANES), lambda h: (1, 0, h))
    aspec = pl.BlockSpec((span, LANES), lambda h: (0, h))
    first = sums is None
    extra = () if first else tuple(sums)
    out = pl.pallas_call(
        functools.partial(attn_bwd_kernel, first),
        grid=(heads,),
        in_specs=[qspec] * 3 + [kspec, vspec, kspec, vspec] + [aspec] * len(extra),
        out_specs=[qspec] + [aspec] * 4,
        out_shape=[jax.ShapeDtypeStruct((rows, width), BF)] + [jax.ShapeDtypeStruct((span, width), F32)] * 4,
        input_output_aliases={} if first else {7 + i: 1 + i for i in range(4)},
        compiler_params=pltpu.CompilerParams(vmem_limit_bytes=48 * 1024 * 1024),
        cost_estimate=pl.CostEstimate(
            flops=20 * rows * span * width, bytes_accessed=40 * span * width, transcendentals=2 * rows * span * heads
        ),
        name="attn_bwd",
    )(qa, o, do, kv0, kv0, kv1, kv1, *extra)
    return out[0], out[1:]


def swap(n, step):
    return [(i, i ^ step) for i in range(n)]


def tp_sum(part, tp):
    if tp != 4:
        return lax.psum(part, "tp")
    index = lax.axis_index("tp")
    edge = (index == 0) | (index == 3)
    pair = part + lax.ppermute(part, "tp", [(0, 1), (3, 2)])
    total = pair + lax.ppermute(pair, "tp", [(1, 2), (2, 1)])
    back = lax.ppermute(total, "tp", [(1, 0), (2, 3)])
    return jnp.where(edge, back, total)


def group_sum(v, fsdp):
    v = v + lax.ppermute(v, "ctx", swap(2, 1))
    step = 1
    while step < fsdp:
        v = v + lax.ppermute(v, "fsdp", swap(fsdp, step))
        step *= 2
    return v


def norm_stats(v):
    center = jnp.mean(v, axis=-1, keepdims=True)
    centred = v - center
    spread = jnp.mean(centred * centred, axis=-1, keepdims=True)
    r = lax.rsqrt(spread + EPSILON)
    return centred * r, r


def norm_back(v, gain, dn):
    xhat, r = norm_stats(v)
    dx = dn * gain
    back = r * (dx - jnp.mean(dx, axis=-1, keepdims=True) - xhat * jnp.mean(dx * xhat, axis=-1, keepdims=True))
    return back, jnp.sum(dn * xhat, axis=0), jnp.sum(dn, axis=0)


def gelu_pair(u):
    cdf = 0.5 * (1.0 + lax.erf(u * float(np.sqrt(0.5))))
    pdf = jnp.exp(-0.5 * u * u) * float(1.0 / np.sqrt(2 * np.pi))
    return u * cdf, cdf + u * pdf


def pad_rows(v, rows):
    return jnp.pad(v, ((0, rows - v.shape[0]), (0, 0))) if rows > v.shape[0] else v


def up_to(n, m):
    return -(-n // m) * m


def per_device(
    sizes,
    inputs,
    lengths,
    cotangent,
    norm_gains,
    norm_shifts,
    qkv_weight,
    qv_bias,
    out_weight,
    out_bias,
    up_weight,
    up_bias,
    down_weight,
    down_bias,
):
    fsdp, tp = sizes
    clips, rows, width = inputs.shape
    assert clips == 1
    local = qkv_weight.shape[-1]
    units = up_weight.shape[-1]
    heads = local // HEAD_DIM
    wide = heads * LANES
    layers = norm_gains.shape[0]
    me = lax.axis_index("ctx")
    full = up_to(rows, 16)
    span = up_to(rows, LANES)
    tile = up_to(-(-full // CHUNKS), LANES)
    cuts = [(a, min(full, a + tile)) for a in range(0, full, tile)]
    qrows = [up_to(b - a, LANES) for a, b in cuts]
    length = lengths[0]

    spread = np.zeros((local, wide), np.float32)
    for f in range(local):
        spread[f, f // HEAD_DIM * LANES + f % HEAD_DIM] = 1.0
    spread = jnp.asarray(spread, BF)
    gather = spread.T
    head_lane = np.arange(wide) % LANES
    q_extra = jnp.asarray((head_lane == HEAD_DIM)[None, :], F32)
    k_ones = jnp.asarray(((head_lane > HEAD_DIM) & (head_lane <= HEAD_DIM + 3))[None, :], F32)
    v_ones = jnp.asarray(((head_lane >= HEAD_DIM) & (head_lane <= HEAD_DIM + 1))[None, :], F32)
    row = jnp.arange(span)[:, None]
    live_key = (row < rows) & (row + me * rows < length)
    k_extra = k_ones + jnp.where(live_key, 0.0, NEG) * q_extra
    live_row = live_key[:full].astype(F32)

    half = qkv_weight.shape[1] // 2

    def mine(w):
        return lax.dynamic_slice_in_dim(w, me * half, half, axis=0)

    def fetch(w):
        return lax.all_gather(w, ("fsdp", "ctx"), axis=0, tiled=True)

    weights = []
    for layer in range(layers):
        q3 = mine(qkv_weight[layer]).reshape(half, 3 * local)
        attn = fetch(jnp.concatenate([q3, mine(out_weight[layer])], axis=1))
        weights.append((attn, fetch(mine(up_weight[layer])), fetch(mine(down_weight[layer]))))

    def pieces(v):
        v = jnp.pad(v[0].astype(F32), ((0, full - rows), (0, 0)))
        return [v[a:b] for a, b in cuts]

    hidden = pieces(inputs)
    saved = []
    for layer in range(layers):
        w_attn, w_up, w_down = weights[layer]
        w_qkv, w_out = w_attn[:, : 3 * local], w_attn[:, 3 * local :]
        qb, vb = qv_bias[layer, 0], qv_bias[layer, 1]
        bias3 = jnp.concatenate([qb, jnp.zeros_like(qb), vb])
        normed, mixed = [], []
        for h in hidden:
            xhat, _ = norm_stats(h)
            normed.append((xhat * norm_gains[layer, 0] + norm_shifts[layer, 0]).astype(BF))
            mixed.append((mm(normed[-1], w_qkv) + bias3).astype(BF))
        tall = pad_rows(jnp.concatenate(mixed), span)
        keys = (mm(tall[:, local : 2 * local], spread) + k_extra).astype(BF)
        values = (mm(tall[:, 2 * local :], spread) + v_ones).astype(BF)
        kv0 = jnp.stack([keys, values])
        kv1 = lax.ppermute(kv0, "ctx", swap(2, 1))
        out_chunks, qas, mids, normed2, actives, slopes, nexts = [], [], [], [], [], [], []
        attended = []
        for (a, b), qr, h, m in zip(cuts, qrows, hidden, mixed):
            q = (mm(pad_rows(m[:, :local], qr), spread) + q_extra).astype(BF)
            o, qa = attn_fwd(q, kv0, kv1)
            out_chunks.append(o)
            qas.append(qa)
            att = mm(o[: b - a], gather).astype(BF)
            attended.append(att)
            part = mm(att, w_out, NT).astype(BF)
            mids.append(h + tp_sum(part, tp).astype(F32) + out_bias[layer])
        for mid in mids:
            xhat, _ = norm_stats(mid)
            n2 = (xhat * norm_gains[layer, 1] + norm_shifts[layer, 1]).astype(BF)
            normed2.append(n2)
            act, slope = gelu_pair(mm(n2, w_up) + up_bias[layer])
            actives.append(act.astype(BF))
            slopes.append(slope.astype(BF))
            part = mm(actives[-1], w_down, NT).astype(BF)
            nexts.append(mid + tp_sum(part, tp).astype(F32) + down_bias[layer])
        saved.append((hidden, normed, qas, out_chunks, attended, kv0, kv1, mids, normed2, actives, slopes))
        hidden = nexts
    outputs = jnp.concatenate([h.astype(BF) for h in hidden])[None, :rows]

    grad = [g * live_row[a:b] for g, (a, b) in zip(pieces(cotangent), cuts)]
    owned, vectors = [None] * layers, [None] * layers

    def total(parts):
        return functools.reduce(jnp.add, parts)

    def col_sum(parts):
        return total([jnp.sum(p.astype(F32), axis=0) for p in parts])

    def weight_grad(left, right):
        return lax.dot_general(left, right, (((0,), (0,)), ((), ())), preferred_element_type=F32).astype(BF)

    def give(g):
        part = lax.psum_scatter(g, ("fsdp", "ctx"), scatter_dimension=0, tiled=True)
        other = lax.ppermute(part, "ctx", swap(2, 1))
        low = jnp.where(me == 0, part, other)
        high = jnp.where(me == 0, other, part)
        return jnp.concatenate([low, high]).astype(F32)

    for layer in reversed(range(layers)):
        hidden, normed, qas, out_chunks, attended, kv0, kv1, mids, normed2, actives, slopes = saved[layer]
        w_attn, w_up, w_down = weights[layer]
        w_qkv, w_out = w_attn[:, : 3 * local], w_attn[:, 3 * local :]
        down_bias_grad = col_sum(grad)
        lows = [g.astype(BF) for g in grad]
        d_upper, dn2 = [], []
        for gl, slope in zip(lows, slopes):
            d_upper.append((mm(gl, w_down) * slope.astype(F32)).astype(BF))
            dn2.append(tp_sum(mm(d_upper[-1], w_up, NT).astype(BF), tp).astype(F32))
        up_bias_grad = col_sum(d_upper)
        d_up_all, low_all = jnp.concatenate(d_upper), jnp.concatenate(lows)
        grad_down = give(weight_grad(low_all, jnp.concatenate(actives)))
        grad_up = give(weight_grad(jnp.concatenate(normed2), d_up_all))
        gains2, shifts2, mid_grad = [], [], []
        for g, d, mid in zip(grad, dn2, mids):
            back, gg, ss = norm_back(mid, norm_gains[layer, 1], d)
            gains2.append(gg)
            shifts2.append(ss)
            mid_grad.append(g + back)
        out_bias_grad = col_sum(mid_grad)
        lows = [g.astype(BF) for g in mid_grad]
        dqs, sums = [], None
        for (a, b), qr, gl, qa, o in zip(cuts, qrows, lows, qas, out_chunks):
            d_att = mm(gl, w_out).astype(BF)
            do = mm(pad_rows(d_att, qr), spread).astype(BF)
            dq, sums = attn_bwd(qa, o, do, kv0, kv1, sums)
            dqs.append(mm(dq[: b - a], gather).astype(BF))
        dk0, dv0, dk1, dv1 = sums
        theirs = jnp.stack([dk1 * SCALE, dv1]).astype(BF)
        got = lax.ppermute(theirs, "ctx", swap(2, 1)).astype(F32)
        dk = mm((dk0 * SCALE + got[0]).astype(BF), gather).astype(BF)[:full]
        dv = mm((dv0 + got[1]).astype(BF), gather).astype(BF)[:full]
        d_mixed = [jnp.concatenate([q, dk[a:b], dv[a:b]], axis=1) for q, (a, b) in zip(dqs, cuts)]
        grad_out_low = weight_grad(jnp.concatenate(lows), jnp.concatenate(attended))
        d_all = jnp.concatenate(d_mixed)
        grad_attn = give(jnp.concatenate([weight_grad(jnp.concatenate(normed), d_all), grad_out_low], axis=1))
        q_sum = jnp.sum(d_all[:, :local].astype(F32), axis=0)
        v_sum = jnp.sum(d_all[:, 2 * local :].astype(F32), axis=0)
        gains1, shifts1, grad = [], [], []
        for g, h, d in zip(mid_grad, hidden, d_mixed):
            dn = tp_sum(mm(d, w_qkv, NT).astype(BF), tp).astype(F32)
            back, gg, ss = norm_back(h, norm_gains[layer, 0], dn)
            gains1.append(gg)
            shifts1.append(ss)
            grad.append(g + back)
        grad_qkv = grad_attn[:, : 3 * local].reshape(-1, 3, local)
        owned[layer] = (grad_qkv, grad_attn[:, 3 * local :], grad_up, grad_down)
        flat = jnp.concatenate(
            [
                total(gains1),
                total(gains2),
                total(shifts1),
                total(shifts2),
                q_sum,
                v_sum,
                out_bias_grad,
                up_bias_grad,
                down_bias_grad,
            ]
        )
        size = flat.shape[0]
        flat = jnp.pad(flat, (0, up_to(size, 1024) - size)).reshape(-1, LANES)
        flat = group_sum(flat, fsdp).reshape(-1)
        ends = np.cumsum([width] * 4 + [local] * 2 + [width, units, width])[:-1]
        vectors[layer] = jnp.split(flat[:size], ends)

    def stack(group, index):
        return jnp.stack([group[layer][index] for layer in range(layers)])

    def both(index):
        return jnp.stack([jnp.stack([v[index], v[index + 1]]) for v in vectors])

    return (
        outputs,
        jnp.concatenate(grad)[None, :rows],
        both(0),
        both(2),
        stack(owned, 0),
        both(4),
        stack(owned, 1),
        stack(vectors, 6),
        stack(owned, 2),
        stack(vectors, 7),
        stack(owned, 3),
        stack(vectors, 8),
    )


def solution(mesh):
    in_specs = (
        P("fsdp", "ctx", None),
        P("fsdp"),
        P("fsdp", "ctx", None),
        P(),
        P(),
        P(None, "fsdp", None, "tp"),
        P(None, None, "tp"),
        P(None, "fsdp", "tp"),
        P(),
        P(None, "fsdp", "tp"),
        P(None, "tp"),
        P(None, "fsdp", "tp"),
        P(),
    )
    out_specs = (
        P("fsdp", "ctx", None),
        P("fsdp", "ctx", None),
        P(),
        P(),
        P(None, "fsdp", None, "tp"),
        P(None, None, "tp"),
        P(None, "fsdp", "tp"),
        P(),
        P(None, "fsdp", "tp"),
        P(None, "tp"),
        P(None, "fsdp", "tp"),
        P(),
    )
    sizes = (mesh.shape["fsdp"], mesh.shape["tp"])
    return jax.shard_map(
        functools.partial(per_device, sizes), mesh=mesh, in_specs=in_specs, out_specs=out_specs, check_vma=False
    )
```

time: 1730 us -> 1010 us (0.58)
  waiting for transfers between devices: 1230 us -> 387 us
  starting transfers between devices: 3.8 us -> 137 us
  matrix products: 234 us -> 136 us
  Pallas kernels: 0 us -> 73.9 us
  other arithmetic: 99.8 us -> 142 us
  blocking collectives: 25.2 us -> 0 us
    psum x9 -> x0, waiting for transfers between devices: 631 us -> none  [the longest x7 556 us: per_device(): lax.psum(partial_value.astype(jnp.bfloat16), 'tp').astype(jnp.float32)]
    ppermute x0 -> x88, waiting for transfers between devices: none -> 364 us  [the longest x24 189 us: tp_sum(): back = lax.ppermute(total, 'tp', [(1, 0), (2, 3)])]
    reduce_scatter x8 -> x6, waiting for transfers between devices: 340 us -> 0.05 us  [give(): part = lax.psum_scatter(g, ('fsdp', 'ctx'), scatter_dimension=0, tiled=True)]
    all_gather x8 -> x6, waiting for transfers between devices: 242 us -> 22.1 us  [fetch(): return lax.all_gather(w, ('fsdp', 'ctx'), axis=0, tiled=True)]
    ppermute x0 -> x88, starting transfers between devices: none -> 136 us  [the longest x24 45.8 us: tp_sum(): pair = part + lax.ppermute(part, 'tp', [(0, 1), (3, 2)])]
    dot_general x34 -> x84, matrix products: 212 us -> 136 us  [the longest x76 105 us: mm(): return lax.dot_general(a, b, dims, preferred_element_type=F32)]
    pallas_call x0 -> x12, Pallas kernels: none -> 73.9 us  [the longest x6 49.1 us: attn_bwd(): pl.pallas_call(functools.partial(attn_bwd_kernel, first), grid=(heads,),...]
    add x1 -> x70, other arithmetic: 4.71 us -> 51.5 us  [the longest x24 27.1 us: tp_sum(): total = pair + lax.ppermute(pair, 'tp', [(1, 2), (2, 1)])]
  transfers between devices with their start and end apart: 27 -> 100, of which waited for: 25 -> 41; matrix products, arithmetic and copies ran while one was open for 10% -> 32% of each run, Pallas kernels for 0% -> 7%
where the time goes in v1:
time: 1010 us; the launch traced here: 1000 us
  waiting for transfers between devices  387 us (38%)
  other arithmetic  142 us (14%)
  starting transfers between devices  137 us (14%)
  matrix products  136 us (13%)
  local copies, waits for them, and re-layouts  103 us (10%)
  Pallas kernels  73.9 us (7%)
  between operations  20.5 us (2%)
    ppermute x24, waiting for transfers between devices, tp_sum(): back = lax.ppermute(total, 'tp', [(1, 0), (2, 3)])  189 us
    ppermute x24, waiting for transfers between devices, tp_sum(): pair = part + lax.ppermute(part, 'tp', [(0, 1), (3, 2)])  167 us
    dot_general x76, matrix products, mm(): return lax.dot_general(a, b, dims, preferred_element_type=F32)  105 us
    unnamed x630, local copies, waits for them, and re-layouts  79 us
    pallas_call x6, Pallas kernels, attn_bwd(): pl.pallas_call(functools.partial(attn_bwd_kernel, first), grid=(heads,),...  49.1 us
    ppermute x24, starting transfers between devices, tp_sum(): pair = part + lax.ppermute(part, 'tp', [(0, 1), (3, 2)])  45.8 us
    ppermute x24, starting transfers between devices, tp_sum(): back = lax.ppermute(total, 'tp', [(1, 0), (2, 3)])  41.3 us
    dot_general x8, matrix products, weight_grad(): lax.dot_general(left, right, (((0,), (0,)), ((), ())), preferred_element_...  31.1 us
  transfers between devices with their start and end apart: 100, of which 41 were waited for; matrix products, arithmetic and copies ran while one was open for 32% of the time, Pallas kernels for 7%

profile of v1, /device:TPU:1, one launch (start us, length us, event | category | flops | bytes accessed | tf_op | source)
XLA Modules:
  0.0 999.6 jit_solution(14026419955705848712)
XLA Ops:
  25.7 22.1 %all-gather.11.cloned.1.call-done = bf16[1280,1280]{1,0:T(8,128)(2,1)} async-done(((bf16[160,1280]{1,0:T(8,128)(2,1)}), bf16[1280,1280]{1,0:T(8,128)(2,1)}) %all-gather.11.cloned.1.call-update) | async-done | bytes 3276816 | tf_op jit(solution)/shard_map/all_gather | solution.py:243
  59.0 4.1 attn_fwd.8
  67.7 4.1 attn_fwd.6
  75.0 4.1 attn_fwd.7
  82.5 11.9 %collective-permute-done.1 = bf16[256,1280]{1,0:T(8,128)(2,1)S(1)} collective-permute-done((bf16[256,1280]{1,0:T(8,128)(2,1)S(1)}, bf16[256,1280]{1,0:T(8,128)(2,1)S(1)}, u32[]{:S(2)}, u32[]{:S(2)}) %collective-permute-start.1) | collective-permute-done | bytes 655392 | tf_op jit(solution)/shard_map/ppermute | solution.py:147
  96.1 12.4 %collective-permute-done.7 = bf16[256,1280]{1,0:T(8,128)(2,1)S(1)} collective-permute-done((bf16[256,1280]{1,0:T(8,128)(2,1)S(1)}, bf16[256,1280]{1,0:T(8,128)(2,1)S(1)}, u32[]{:S(2)}, u32[]{:S(2)}) %collective-permute-start.7) | collective-permute-done | bytes 655392 | tf_op jit(solution)/shard_map/ppermute | solution.py:147
  118.8 9.9 collective-permute-done.15
  131.5 4.2 multiply_convert_fusion.7
  139.0 4.0 collective-permute-start.16
  143.0 13.8 %collective-permute-done.9 = bf16[256,1280]{1,0:T(8,128)(2,1)} collective-permute-done((bf16[256,1280]{1,0:T(8,128)(2,1)S(1)}, bf16[256,1280]{1,0:T(8,128)(2,1)}, u32[]{:S(2)}, u32[]{:S(2)}) %collective-permute-start.9) | collective-permute-done | bytes 655392 | tf_op jit(solution)/shard_map/ppermute | solution.py:149
  172.9 6.9 collective-permute-done.4
  182.3 11.5 %collective-permute-done.10 = bf16[256,1280]{1,0:T(8,128)(2,1)S(1)} collective-permute-done((bf16[256,1280]{1,0:T(8,128)(2,1)S(1)}, bf16[256,1280]{1,0:T(8,128)(2,1)S(1)}, u32[]{:S(2)}, u32[]{:S(2)}) %collective-permute-start.10) | collective-permute-done | bytes 655392 | tf_op jit(solution)/shard_map/ppermute | solution.py:147
  205.7 9.8 collective-permute-start.12
  222.2 5.4 collective-permute-done.6
  227.5 14.0 %collective-permute-done.12 = bf16[256,1280]{1,0:T(8,128)(2,1)} collective-permute-done((bf16[256,1280]{1,0:T(8,128)(2,1)}, bf16[256,1280]{1,0:T(8,128)(2,1)}, u32[]{:S(2)}, u32[]{:S(2)}) %collective-permute-start.12) | collective-permute-done | bytes 655392 | tf_op jit(solution)/shard_map/ppermute | solution.py:149
  260.5 4.1 attn_fwd.11
  267.1 4.1 attn_fwd.9
  274.0 4.1 attn_fwd.10
  282.0 11.2 %collective-permute-done.20 = bf16[256,1280]{1,0:T(8,128)(2,1)S(1)} collective-permute-done((bf16[256,1280]{1,0:T(8,128)(2,1)S(1)}, bf16[256,1280]{1,0:T(8,128)(2,1)S(1)}, u32[]{:S(2)}, u32[]{:S(2)}) %collective-permute-start.20) | collective-permute-done | bytes 655392 | tf_op jit(solution)/shard_map/ppermute | solution.py:147
  294.2 13.2 %collective-permute-done.26 = bf16[256,1280]{1,0:T(8,128)(2,1)S(1)} collective-permute-done((bf16[256,1280]{1,0:T(8,128)(2,1)S(1)}, bf16[256,1280]{1,0:T(8,128)(2,1)S(1)}, u32[]{:S(2)}, u32[]{:S(2)}) %collective-permute-start.26) | collective-permute-done | bytes 655392 | tf_op jit(solution)/shard_map/ppermute | solution.py:147
  314.3 12.0 %collective-permute-done.34 = bf16[240,1280]{1,0:T(8,128)(2,1)S(1)} collective-permute-done((bf16[240,1280]{1,0:T(8,128)(2,1)S(1)}, bf16[240,1280]{1,0:T(8,128)(2,1)S(1)}, u32[]{:S(2)}, u32[]{:S(2)}) %collective-permute-start.34) | collective-permute-done | bytes 614432 | tf_op jit(solution)/shard_map/ppermute | solution.py:149
  328.0 4.4 multiply_convert_fusion.6
  332.4 4.1 convert_reduce_fusion.16
  337.6 4.1 collective-permute-start.41
  345.6 8.9 collective-permute-done.28
  374.9 4.3 collective-permute-done.44
  380.9 12.4 %collective-permute-done.29 = bf16[256,1280]{1,0:T(8,128)(2,1)S(1)} collective-permute-done((bf16[256,1280]{1,0:T(8,128)(2,1)S(1)}, bf16[256,1280]{1,0:T(8,128)(2,1)S(1)}, u32[]{:S(2)}, u32[]{:S(2)}) %collective-permute-start.29) | collective-permute-done | bytes 655392 | tf_op jit(solution)/shard_map/ppermute | solution.py:147
  395.8 11.5 %collective-permute-done.23 = bf16[256,1280]{1,0:T(8,128)(2,1)S(1)} collective-permute-done((bf16[256,1280]{1,0:T(8,128)(2,1)S(1)}, bf16[256,1280]{1,0:T(8,128)(2,1)S(1)}, u32[]{:S(2)}, u32[]{:S(2)}) %collective-permute-start.23) | collective-permute-done | bytes 655392 | tf_op jit(solution)/shard_map/ppermute | solution.py:147
  409.9 11.5 %collective-permute-done.38 = bf16[256,1280]{1,0:T(8,128)(2,1)S(1)} collective-permute-done((bf16[256,1280]{1,0:T(8,128)(2,1)S(1)}, bf16[256,1280]{1,0:T(8,128)(2,1)S(1)}, u32[]{:S(2)}, u32[]{:S(2)}) %collective-permute-start.38) | collective-permute-done | bytes 655392 | tf_op jit(solution)/shard_map/ppermute | solution.py:147
  428.8 4.5 convolution_convert_fusion.2
  449.4 7.1 collective-permute-done.37
  462.7 8.0 collective-permute-done.46
  470.7 14.0 %collective-permute-done.31 = bf16[256,1280]{1,0:T(8,128)(2,1)S(1)} collective-permute-done((bf16[256,1280]{1,0:T(8,128)(2,1)S(1)}, bf16[256,1280]{1,0:T(8,128)(2,1)S(1)}, u32[]{:S(2)}, u32[]{:S(2)}) %collective-permute-start.31) | collective-permute-done | bytes 655392 | tf_op jit(solution)/shard_map/ppermute | solution.py:149
  484.8 13.9 %collective-permute-done.25 = bf16[256,1280]{1,0:T(8,128)(2,1)S(1)} collective-permute-done((bf16[256,1280]{1,0:T(8,128)(2,1)S(1)}, bf16[256,1280]{1,0:T(8,128)(2,1)S(1)}, u32[]{:S(2)}, u32[]{:S(2)}) %collective-permute-start.25) | collective-permute-done | bytes 655392 | tf_op jit(solution)/shard_map/ppermute | solution.py:149
  498.7 14.0 %collective-permute-done.40 = bf16[256,1280]{1,0:T(8,128)(2,1)S(1)} collective-permute-done((bf16[256,1280]{1,0:T(8,128)(2,1)S(1)}, bf16[256,1280]{1,0:T(8,128)(2,1)S(1)}, u32[]{:S(2)}, u32[]{:S(2)}) %collective-permute-start.40) | collective-permute-done | bytes 655392 | tf_op jit(solution)/shard_map/ppermute | solution.py:149
  512.7 3.7 fusion.331
  526.8 7.8 attn_bwd.6
  543.2 8.4 attn_bwd.7
  551.6 8.3 attn_bwd.8
  563.6 4.8 collective-permute-start.47
  568.4 4.4 convolution_convert_fusion
  586.5 7.7 collective-permute-done.54
  598.3 9.9 collective-permute-done.48
  609.9 12.3 %collective-permute-done.60 = bf16[256,1280]{1,0:T(8,128)(2,1)S(1)} collective-permute-done((bf16[256,1280]{1,0:T(8,128)(2,1)S(1)}, bf16[256,1280]{1,0:T(8,128)(2,1)S(1)}, u32[]{:S(2)}, u32[]{:S(2)}) %collective-permute-start.60) | collective-permute-done | bytes 655392 | tf_op jit(solution)/shard_map/ppermute | solution.py:147
  627.3 5.6 copy.107
  647.7 7.4 collective-permute-done.50
  656.4 12.8 %collective-permute-done.62 = bf16[256,1280]{1,0:T(8,128)(2,1)S(1)} collective-permute-done((bf16[256,1280]{1,0:T(8,128)(2,1)S(1)}, bf16[256,1280]{1,0:T(8,128)(2,1)S(1)}, u32[]{:S(2)}, u32[]{:S(2)}) %collective-permute-start.62) | collective-permute-done | bytes 655392 | tf_op jit(solution)/shard_map/ppermute | solution.py:149
  679.6 4.5 convolution_convert_fusion.3
  711.2 6.1 convolution_convert_fusion.1
  735.0 11.8 %collective-permute-done.63 = bf16[256,1280]{1,0:T(8,128)(2,1)} collective-permute-done((bf16[256,1280]{1,0:T(8,128)(2,1)S(1)}, bf16[256,1280]{1,0:T(8,128)(2,1)}, u32[]{:S(2)}, u32[]{:S(2)}) %collective-permute-start.63) | collective-permute-done | bytes 655392 | tf_op jit(solution)/shard_map/ppermute | solution.py:147
  754.7 12.4 %collective-permute-done.59 = bf16[240,1280]{1,0:T(8,128)(2,1)S(1)} collective-permute-done((bf16[240,1280]{1,0:T(8,128)(2,1)S(1)}, bf16[240,1280]{1,0:T(8,128)(2,1)S(1)}, u32[]{:S(2)}, u32[]{:S(2)}) %collective-permute-start.59) | collective-permute-done | bytes 614432 | tf_op jit(solution)/shard_map/ppermute | solution.py:149
  771.7 9.5 collective-permute-done.53
  781.9 13.2 %collective-permute-done.65 = bf16[256,1280]{1,0:T(8,128)(2,1)S(1)} collective-permute-done((bf16[256,1280]{1,0:T(8,128)(2,1)S(1)}, bf16[256,1280]{1,0:T(8,128)(2,1)S(1)}, u32[]{:S(2)}, u32[]{:S(2)}) %collective-permute-start.65) | collective-permute-done | bytes 655392 | tf_op jit(solution)/shard_map/ppermute | solution.py:149
  798.2 3.6 convolution_convert_fusion.24.do_ref
  807.8 8.0 attn_bwd.9
  815.8 8.4 attn_bwd.10
  824.2 8.3 attn_bwd.11
  868.7 5.2 convolution_convert_fusion.5
  877.6 7.5 collective-permute-done.67
  888.9 10.1 %collective-permute-done.70 = bf16[256,1280]{1,0:T(8,128)(2,1)} collective-permute-done((bf16[256,1280]{1,0:T(8,128)(2,1)S(1)}, bf16[256,1280]{1,0:T(8,128)(2,1)}, u32[]{:S(2)}, u32[]{:S(2)}) %collective-permute-start.70) | collective-permute-done | bytes 655392 | tf_op jit(solution)/shard_map/ppermute | solution.py:147
  931.9 5.7 copy.101
  940.3 5.5 copy.102
  950.7 10.4 %collective-permute-done.72 = bf16[256,1280]{1,0:T(8,128)(2,1)} collective-permute-done((bf16[256,1280]{1,0:T(8,128)(2,1)}, bf16[256,1280]{1,0:T(8,128)(2,1)}, u32[]{:S(2)}, u32[]{:S(2)}) %collective-permute-start.72) | collective-permute-done | bytes 655392 | tf_op jit(solution)/shard_map/ppermute | solution.py:149
  971.2 5.8 copy.99
  (1154 shorter events, 440.1 us)
Async XLA Ops:
  7.2 40.6 %all-gather.11.cloned.1.call-start = ((), (), s32[]{:S(2)}) async-start(), calls=%async_computation.6 | async-start | bytes 3686400 | tf_op jit(solution)/shard_map/all_gather | solution.py:243
  12.3 119.3 %all-gather.15.cloned.1.call-start = ((), (), s32[]{:S(2)}) async-start(), calls=%async_computation.8 | async-start | bytes 3686400 | tf_op jit(solution)/shard_map/all_gather | solution.py:243
  14.2 121.6 %all-gather.17.cloned.1.call-start = ((), (), s32[]{:S(2)}) async-start(), calls=%async_computation.9 | async-start | bytes 3686400 | tf_op jit(solution)/shard_map/all_gather | solution.py:243
  17.5 201.5 %all-gather.13.cloned.1.call-start = ((), (), s32[]{:S(2)}) async-start(), calls=%async_computation.7 | async-start | bytes 3686400 | tf_op jit(solution)/shard_map/all_gather | solution.py:243
  73.6 20.8 %collective-permute-start.1 = (bf16[256,1280]{1,0:T(8,128)(2,1)S(1)}, bf16[256,1280]{1,0:T(8,128)(2,1)S(1)}, u32[]{:S(2)}, u32[]{:S(2)}) collective-permute-start(bf16[256,1280]{1,0:T(8,128)(2,1)S(1)} %convolution_convert_fusion.15), channel_id=1, source_target_pairs={{0,1},{3,2},{4,5},{7,6},{8,9},{11,10},{12,13},{15,14},{16,17},{19,... | collective-permute-start | bytes 1966088 | tf_op jit(solution)/shard_map/ppermute | solution.py:147
  80.3 28.2 %collective-permute-start.7 = (bf16[256,1280]{1,0:T(8,128)(2,1)S(1)}, bf16[256,1280]{1,0:T(8,128)(2,1)S(1)}, u32[]{:S(2)}, u32[]{:S(2)}) collective-permute-start(bf16[256,1280]{1,0:T(8,128)(2,1)S(1)} %convolution_convert_fusion.14), channel_id=1, source_target_pairs={{0,1},{3,2},{4,5},{7,6},{8,9},{11,10},{12,13},{15,14},{16,17},{19,... | collective-permute-start | bytes 1966088 | tf_op jit(solution)/shard_map/ppermute | solution.py:147
  81.8 28.5 %collective-permute-start.14 = (bf16[240,1280]{1,0:T(8,128)(2,1)S(1)}, bf16[240,1280]{1,0:T(8,128)(2,1)S(1)}, u32[]{:S(2)}, u32[]{:S(2)}) collective-permute-start(bf16[240,1280]{1,0:T(8,128)(2,1)S(1)} %add.964), channel_id=1, source_target_pairs={{1,2},{2,1},{5,6},{6,5},{9,10},{10,9},{13,14},{14,13},{17,18},{18,... | collective-permute-start | bytes 1843208 | tf_op jit(solution)/shard_map/ppermute | solution.py:148
  94.6 18.9 %collective-permute-start.2 = (bf16[256,1280]{1,0:T(8,128)(2,1)S(1)}, bf16[256,1280]{1,0:T(8,128)(2,1)}, u32[]{:S(2)}, u32[]{:S(2)}) collective-permute-start(bf16[256,1280]{1,0:T(8,128)(2,1)S(1)} %add.920), channel_id=1, source_target_pairs={{1,2},{2,1},{5,6},{6,5},{9,10},{10,9},{13,14},{14,13},{17,18},{18,... | collective-permute-start | bytes 1966088 | tf_op jit(solution)/shard_map/ppermute | solution.py:148
  113.3 214.7 %all-gather.19.cloned.1.call-start = ((), (), s32[]{:S(2)}) async-start(), calls=%async_computation.10 | async-start | bytes 3686400 | tf_op jit(solution)/shard_map/all_gather | solution.py:243
  114.9 28.1 %collective-permute-start.3 = (bf16[256,1280]{1,0:T(8,128)(2,1)S(1)}, bf16[256,1280]{1,0:T(8,128)(2,1)}, u32[]{:S(2)}, u32[]{:S(2)}) collective-permute-start(bf16[256,1280]{1,0:T(8,128)(2,1)S(1)} %add.921), channel_id=1, source_target_pairs={{1,0},{2,3},{5,4},{6,7},{9,8},{10,11},{13,12},{14,15},{17,16},{18,... | collective-permute-start | bytes 1966088 | tf_op jit(solution)/shard_map/ppermute | solution.py:149
  117.5 39.3 %collective-permute-start.9 = (bf16[256,1280]{1,0:T(8,128)(2,1)S(1)}, bf16[256,1280]{1,0:T(8,128)(2,1)}, u32[]{:S(2)}, u32[]{:S(2)}) collective-permute-start(bf16[256,1280]{1,0:T(8,128)(2,1)S(1)} %add.949), channel_id=1, source_target_pairs={{1,0},{2,3},{5,4},{6,7},{9,8},{10,11},{13,12},{14,15},{17,16},{18,... | collective-permute-start | bytes 1966088 | tf_op jit(solution)/shard_map/ppermute | solution.py:149
  139.0 33.0 %collective-permute-start.16 = (bf16[240,1280]{1,0:T(8,128)(2,1)S(1)}, bf16[240,1280]{1,0:T(8,128)(2,1)S(1)}, u32[]{:S(2)}, u32[]{:S(2)}) collective-permute-start(bf16[240,1280]{1,0:T(8,128)(2,1)S(1)} %fusion.130), channel_id=1, source_target_pairs={{0,1},{3,2},{4,5},{7,6},{8,9},{11,10},{12,13},{15,14},{16,17},{19,... | collective-permute-start | bytes 1843208 | tf_op jit(solution)/shard_map/ppermute | solution.py:147
  170.7 23.2 %collective-permute-start.10 = (bf16[256,1280]{1,0:T(8,128)(2,1)S(1)}, bf16[256,1280]{1,0:T(8,128)(2,1)S(1)}, u32[]{:S(2)}, u32[]{:S(2)}) collective-permute-start(bf16[256,1280]{1,0:T(8,128)(2,1)S(1)} %fusion.100), channel_id=1, source_target_pairs={{0,1},{3,2},{4,5},{7,6},{8,9},{11,10},{12,13},{15,14},{16,17},{19,... | collective-permute-start | bytes 1966088 | tf_op jit(solution)/shard_map/ppermute | solution.py:147
  172.2 24.3 %collective-permute-start.17 = (bf16[240,1280]{1,0:T(8,128)(2,1)S(1)}, bf16[240,1280]{1,0:T(8,128)(2,1)S(1)}, u32[]{:S(2)}, u32[]{:S(2)}) collective-permute-start(bf16[240,1280]{1,0:T(8,128)(2,1)S(1)} %add.975), channel_id=1, source_target_pairs={{1,2},{2,1},{5,6},{6,5},{9,10},{10,9},{13,14},{14,13},{17,18},{18,... | collective-permute-start | bytes 1843208 | tf_op jit(solution)/shard_map/ppermute | solution.py:148
  180.8 18.9 %collective-permute-start.5 = (bf16[256,1280]{1,0:T(8,128)(2,1)}, bf16[256,1280]{1,0:T(8,128)(2,1)}, u32[]{:S(2)}, u32[]{:S(2)}) collective-permute-start(bf16[256,1280]{1,0:T(8,128)(2,1)} %add.934), channel_id=1, source_target_pairs={{1,2},{2,1},{5,6},{6,5},{9,10},{10,9},{13,14},{14,13},{17,18},{18,... | collective-permute-start | bytes 1966088 | tf_op jit(solution)/shard_map/ppermute | solution.py:148
  199.6 132.9 %all-gather.21.cloned.1.call-start = ((), (), s32[]{:S(2)}) async-start(), calls=%async_computation.11 | async-start | bytes 3686400 | tf_op jit(solution)/shard_map/all_gather | solution.py:243
  202.0 25.6 %collective-permute-start.6 = (bf16[256,1280]{1,0:T(8,128)(2,1)}, bf16[256,1280]{1,0:T(8,128)(2,1)}, u32[]{:S(2)}, u32[]{:S(2)}) collective-permute-start(bf16[256,1280]{1,0:T(8,128)(2,1)} %add.935), channel_id=1, source_target_pairs={{1,0},{2,3},{5,4},{6,7},{9,8},{10,11},{13,12},{14,15},{17,16},{18,... | collective-permute-start | bytes 1966088 | tf_op jit(solution)/shard_map/ppermute | solution.py:149
  205.7 35.9 %collective-permute-start.12 = (bf16[256,1280]{1,0:T(8,128)(2,1)}, bf16[256,1280]{1,0:T(8,128)(2,1)}, u32[]{:S(2)}, u32[]{:S(2)}) collective-permute-start(bf16[256,1280]{1,0:T(8,128)(2,1)} %add.957), channel_id=1, source_target_pairs={{1,0},{2,3},{5,4},{6,7},{9,8},{10,11},{13,12},{14,15},{17,16},{18,... | collective-permute-start | bytes 1966088 | tf_op jit(solution)/shard_map/ppermute | solution.py:149
  256.2 432.4 %reduce-scatter.25.cloned.1.call-start = ((), (), s32[]{:S(2)}) async-start(), calls=%async_computation.15 | async-start | bytes 3686400 | tf_op jit(solution)/shard_map/reduce_scatter | solution.py:309
  272.4 20.9 %collective-permute-start.20 = (bf16[256,1280]{1,0:T(8,128)(2,1)S(1)}, bf16[256,1280]{1,0:T(8,128)(2,1)S(1)}, u32[]{:S(2)}, u32[]{:S(2)}) collective-permute-start(bf16[256,1280]{1,0:T(8,128)(2,1)S(1)} %convolution_convert_fusion.13), channel_id=1, source_target_pairs={{0,1},{3,2},{4,5},{7,6},{8,9},{11,10},{12,13},{15,14},{16,17},{19,... | collective-permute-start | bytes 1966088 | tf_op jit(solution)/shard_map/ppermute | solution.py:147
  279.2 28.1 %collective-permute-start.26 = (bf16[256,1280]{1,0:T(8,128)(2,1)S(1)}, bf16[256,1280]{1,0:T(8,128)(2,1)S(1)}, u32[]{:S(2)}, u32[]{:S(2)}) collective-permute-start(bf16[256,1280]{1,0:T(8,128)(2,1)S(1)} %convolution_convert_fusion.12), channel_id=1, source_target_pairs={{0,1},{3,2},{4,5},{7,6},{8,9},{11,10},{12,13},{15,14},{16,17},{19,... | collective-permute-start | bytes 1966088 | tf_op jit(solution)/shard_map/ppermute | solution.py:147
  280.8 27.4 %collective-permute-start.33 = (bf16[240,1280]{1,0:T(8,128)(2,1)S(1)}, bf16[240,1280]{1,0:T(8,128)(2,1)S(1)}, u32[]{:S(2)}, u32[]{:S(2)}) collective-permute-start(bf16[240,1280]{1,0:T(8,128)(2,1)S(1)} %add.1021), channel_id=1, source_target_pairs={{1,2},{2,1},{5,6},{6,5},{9,10},{10,9},{13,14},{14,13},{17,18},{18,... | collective-permute-start | bytes 1843208 | tf_op jit(solution)/shard_map/ppermute | solution.py:148
  311.4 33.3 %collective-permute-start.22 = (bf16[256,1280]{1,0:T(8,128)(2,1)S(1)}, bf16[256,1280]{1,0:T(8,128)(2,1)S(1)}, u32[]{:S(2)}, u32[]{:S(2)}) collective-permute-start(bf16[256,1280]{1,0:T(8,128)(2,1)S(1)} %add.988), channel_id=1, source_target_pairs={{1,0},{2,3},{5,4},{6,7},{9,8},{10,11},{13,12},{14,15},{17,16},{18,... | collective-permute-start | bytes 1966088 | tf_op jit(solution)/shard_map/ppermute | solution.py:149
  313.0 41.5 %collective-permute-start.28 = (bf16[256,1280]{1,0:T(8,128)(2,1)S(1)}, bf16[256,1280]{1,0:T(8,128)(2,1)}, u32[]{:S(2)}, u32[]{:S(2)}) collective-permute-start(bf16[256,1280]{1,0:T(8,128)(2,1)S(1)} %add.1009), channel_id=1, source_target_pairs={{1,0},{2,3},{5,4},{6,7},{9,8},{10,11},{13,12},{14,15},{17,16},{18,... | collective-permute-start | bytes 1966088 | tf_op jit(solution)/shard_map/ppermute | solution.py:149
  337.6 34.9 %collective-permute-start.41 = (bf16[240,1280]{1,0:T(8,128)(2,1)S(1)}, bf16[240,1280]{1,0:T(8,128)(2,1)S(1)}, u32[]{:S(2)}, u32[]{:S(2)}) collective-permute-start(bf16[240,1280]{1,0:T(8,128)(2,1)S(1)} %fusion.133), channel_id=1, source_target_pairs={{0,1},{3,2},{4,5},{7,6},{8,9},{11,10},{12,13},{15,14},{16,17},{19,... | collective-permute-start | bytes 1843208 | tf_op jit(solution)/shard_map/ppermute | solution.py:147
  342.8 31.2 %collective-permute-start.35 = (bf16[240,1280]{1,0:T(8,128)(2,1)S(1)}, bf16[240,1280]{1,0:T(8,128)(2,1)S(1)}, u32[]{:S(2)}, u32[]{:S(2)}) collective-permute-start(bf16[240,1280]{1,0:T(8,128)(2,1)S(1)} %fusion.136), channel_id=1, source_target_pairs={{0,1},{3,2},{4,5},{7,6},{8,9},{11,10},{12,13},{15,14},{16,17},{19,... | collective-permute-start | bytes 1843208 | tf_op jit(solution)/shard_map/ppermute | solution.py:147
  363.9 29.4 %collective-permute-start.29 = (bf16[256,1280]{1,0:T(8,128)(2,1)S(1)}, bf16[256,1280]{1,0:T(8,128)(2,1)S(1)}, u32[]{:S(2)}, u32[]{:S(2)}) collective-permute-start(bf16[256,1280]{1,0:T(8,128)(2,1)S(1)} %fusion.112), channel_id=1, source_target_pairs={{0,1},{3,2},{4,5},{7,6},{8,9},{11,10},{12,13},{15,14},{16,17},{19,... | collective-permute-start | bytes 1966088 | tf_op jit(solution)/shard_map/ppermute | solution.py:147
  368.3 39.0 %collective-permute-start.23 = (bf16[256,1280]{1,0:T(8,128)(2,1)S(1)}, bf16[256,1280]{1,0:T(8,128)(2,1)S(1)}, u32[]{:S(2)}, u32[]{:S(2)}) collective-permute-start(bf16[256,1280]{1,0:T(8,128)(2,1)S(1)} %fusion.109), channel_id=1, source_target_pairs={{0,1},{3,2},{4,5},{7,6},{8,9},{11,10},{12,13},{15,14},{16,17},{19,... | collective-permute-start | bytes 1966088 | tf_op jit(solution)/shard_map/ppermute | solution.py:147
  372.5 48.9 %collective-permute-start.38 = (bf16[256,1280]{1,0:T(8,128)(2,1)S(1)}, bf16[256,1280]{1,0:T(8,128)(2,1)S(1)}, u32[]{:S(2)}, u32[]{:S(2)}) collective-permute-start(bf16[256,1280]{1,0:T(8,128)(2,1)S(1)} %fusion.103), channel_id=1, source_target_pairs={{0,1},{3,2},{4,5},{7,6},{8,9},{11,10},{12,13},{15,14},{16,17},{19,... | collective-permute-start | bytes 1966088 | tf_op jit(solution)/shard_map/ppermute | solution.py:147
  374.0 49.9 %collective-permute-start.42 = (bf16[240,1280]{1,0:T(8,128)(2,1)S(1)}, bf16[240,1280]{1,0:T(8,128)(2,1)S(1)}, u32[]{:S(2)}, u32[]{:S(2)}) collective-permute-start(bf16[240,1280]{1,0:T(8,128)(2,1)S(1)} %add.1044), channel_id=1, source_target_pairs={{1,2},{2,1},{5,6},{6,5},{9,10},{10,9},{13,14},{14,13},{17,18},{18,... | collective-permute-start | bytes 1843208 | tf_op jit(solution)/shard_map/ppermute | solution.py:148
  379.2 47.3 %collective-permute-start.36 = (bf16[240,1280]{1,0:T(8,128)(2,1)S(1)}, bf16[240,1280]{1,0:T(8,128)(2,1)S(1)}, u32[]{:S(2)}, u32[]{:S(2)}) collective-permute-start(bf16[240,1280]{1,0:T(8,128)(2,1)S(1)} %add.1032), channel_id=1, source_target_pairs={{1,2},{2,1},{5,6},{6,5},{9,10},{10,9},{13,14},{14,13},{17,18},{18,... | collective-permute-start | bytes 1843208 | tf_op jit(solution)/shard_map/ppermute | solution.py:148
  393.3 41.5 %collective-permute-start.45 = (bf16[256,1280]{1,0:T(8,128)(2,1)}, bf16[256,1280]{1,0:T(8,128)(2,1)}, u32[]{:S(2)}, u32[]{:S(2)}) collective-permute-start(bf16[256,1280]{1,0:T(8,128)(2,1)} %add.1048), channel_id=1, source_target_pairs={{1,2},{2,1},{5,6},{6,5},{9,10},{10,9},{13,14},{14,13},{17,18},{18,... | collective-permute-start | bytes 1966088 | tf_op jit(solution)/shard_map/ppermute | solution.py:148
  407.3 30.2 %collective-permute-start.30 = (bf16[256,1280]{1,0:T(8,128)(2,1)}, bf16[256,1280]{1,0:T(8,128)(2,1)}, u32[]{:S(2)}, u32[]{:S(2)}) collective-permute-start(bf16[256,1280]{1,0:T(8,128)(2,1)} %add.1016), channel_id=1, source_target_pairs={{1,2},{2,1},{5,6},{6,5},{9,10},{10,9},{13,14},{14,13},{17,18},{18,... | collective-permute-start | bytes 1966088 | tf_op jit(solution)/shard_map/ppermute | solution.py:148
  421.4 18.9 %collective-permute-start.24 = (bf16[256,1280]{1,0:T(8,128)(2,1)}, bf16[256,1280]{1,0:T(8,128)(2,1)}, u32[]{:S(2)}, u32[]{:S(2)}) collective-permute-start(bf16[256,1280]{1,0:T(8,128)(2,1)} %add.1001), channel_id=1, source_target_pairs={{1,2},{2,1},{5,6},{6,5},{9,10},{10,9},{13,14},{14,13},{17,18},{18,... | collective-permute-start | bytes 1966088 | tf_op jit(solution)/shard_map/ppermute | solution.py:148
  423.9 19.2 %collective-permute-start.39 = (bf16[256,1280]{1,0:T(8,128)(2,1)}, bf16[256,1280]{1,0:T(8,128)(2,1)}, u32[]{:S(2)}, u32[]{:S(2)}) collective-permute-start(bf16[256,1280]{1,0:T(8,128)(2,1)} %add.1040), channel_id=1, source_target_pairs={{1,2},{2,1},{5,6},{6,5},{9,10},{10,9},{13,14},{14,13},{17,18},{18,... | collective-permute-start | bytes 1966088 | tf_op jit(solution)/shard_map/ppermute | solution.py:148
  433.4 257.6 %reduce-scatter.29.cloned.1.call-start = ((), (), s32[]{:S(2)}) async-start(), calls=%async_computation.17 | async-start | bytes 3686400 | tf_op jit(solution)/shard_map/reduce_scatter | solution.py:309
  434.8 21.7 %collective-permute-start.37 = (bf16[240,1280]{1,0:T(8,128)(2,1)S(1)}, bf16[240,1280]{1,0:T(8,128)(2,1)S(1)}, u32[]{:S(2)}, u32[]{:S(2)}) collective-permute-start(bf16[240,1280]{1,0:T(8,128)(2,1)S(1)} %add.1033), channel_id=1, source_target_pairs={{1,0},{2,3},{5,4},{6,7},{9,8},{10,11},{13,12},{14,15},{17,16},{18,... | collective-permute-start | bytes 1843208 | tf_op jit(solution)/shard_map/ppermute | solution.py:149
  437.6 33.1 %collective-permute-start.46 = (bf16[256,1280]{1,0:T(8,128)(2,1)S(1)}, bf16[256,1280]{1,0:T(8,128)(2,1)S(1)}, u32[]{:S(2)}, u32[]{:S(2)}) collective-permute-start(bf16[256,1280]{1,0:T(8,128)(2,1)S(1)} %add.1049), channel_id=1, source_target_pairs={{1,0},{2,3},{5,4},{6,7},{9,8},{10,11},{13,12},{14,15},{17,16},{18,... | collective-permute-start | bytes 1966088 | tf_op jit(solution)/shard_map/ppermute | solution.py:149
  440.3 44.4 %collective-permute-start.31 = (bf16[256,1280]{1,0:T(8,128)(2,1)S(1)}, bf16[256,1280]{1,0:T(8,128)(2,1)S(1)}, u32[]{:S(2)}, u32[]{:S(2)}) collective-permute-start(bf16[256,1280]{1,0:T(8,128)(2,1)S(1)} %add.1017), channel_id=1, source_target_pairs={{1,0},{2,3},{5,4},{6,7},{9,8},{10,11},{13,12},{14,15},{17,16},{18,... | collective-permute-start | bytes 1966088 | tf_op jit(solution)/shard_map/ppermute | solution.py:149
  443.1 55.6 %collective-permute-start.25 = (bf16[256,1280]{1,0:T(8,128)(2,1)S(1)}, bf16[256,1280]{1,0:T(8,128)(2,1)S(1)}, u32[]{:S(2)}, u32[]{:S(2)}) collective-permute-start(bf16[256,1280]{1,0:T(8,128)(2,1)S(1)} %add.1002), channel_id=1, source_target_pairs={{1,0},{2,3},{5,4},{6,7},{9,8},{10,11},{13,12},{14,15},{17,16},{18,... | collective-permute-start | bytes 1966088 | tf_op jit(solution)/shard_map/ppermute | solution.py:149
  446.1 66.6 %collective-permute-start.40 = (bf16[256,1280]{1,0:T(8,128)(2,1)S(1)}, bf16[256,1280]{1,0:T(8,128)(2,1)S(1)}, u32[]{:S(2)}, u32[]{:S(2)}) collective-permute-start(bf16[256,1280]{1,0:T(8,128)(2,1)S(1)} %add.1041), channel_id=1, source_target_pairs={{1,0},{2,3},{5,4},{6,7},{9,8},{10,11},{13,12},{14,15},{17,16},{18,... | collective-permute-start | bytes 1966088 | tf_op jit(solution)/shard_map/ppermute | solution.py:149
  572.9 266.9 %reduce-scatter.21.cloned.1.call-start = ((), (), s32[]{:S(2)}) async-start(), calls=%async_computation.13 | async-start | bytes 3686400 | tf_op jit(solution)/shard_map/reduce_scatter | solution.py:309
  582.7 25.5 %collective-permute-start.48 = (bf16[256,1280]{1,0:T(8,128)(2,1)S(1)}, bf16[256,1280]{1,0:T(8,128)(2,1)S(1)}, u32[]{:S(2)}, u32[]{:S(2)}) collective-permute-start(bf16[256,1280]{1,0:T(8,128)(2,1)S(1)} %convolution_convert_fusion.11), channel_id=1, source_target_pairs={{0,1},{3,2},{4,5},{7,6},{8,9},{11,10},{12,13},{15,14},{16,17},{19,... | collective-permute-start | bytes 1966088 | tf_op jit(solution)/shard_map/ppermute | solution.py:147
  585.0 37.2 %collective-permute-start.60 = (bf16[256,1280]{1,0:T(8,128)(2,1)S(1)}, bf16[256,1280]{1,0:T(8,128)(2,1)S(1)}, u32[]{:S(2)}, u32[]{:S(2)}) collective-permute-start(bf16[256,1280]{1,0:T(8,128)(2,1)S(1)} %convolution_convert_fusion.10), channel_id=1, source_target_pairs={{0,1},{3,2},{4,5},{7,6},{8,9},{11,10},{12,13},{15,14},{16,17},{19,... | collective-permute-start | bytes 1966088 | tf_op jit(solution)/shard_map/ppermute | solution.py:147
  594.4 29.6 %collective-permute-start.55 = (bf16[240,1280]{1,0:T(8,128)(2,1)S(1)}, bf16[240,1280]{1,0:T(8,128)(2,1)S(1)}, u32[]{:S(2)}, u32[]{:S(2)}) collective-permute-start(bf16[240,1280]{1,0:T(8,128)(2,1)S(1)} %add.1060), channel_id=1, source_target_pairs={{1,2},{2,1},{5,6},{6,5},{9,10},{10,9},{13,14},{14,13},{17,18},{18,... | collective-permute-start | bytes 1843208 | tf_op jit(solution)/shard_map/ppermute | solution.py:148
  608.4 24.7 %collective-permute-start.49 = (bf16[256,1280]{1,0:T(8,128)(2,1)S(1)}, bf16[256,1280]{1,0:T(8,128)(2,1)}, u32[]{:S(2)}, u32[]{:S(2)}) collective-permute-start(bf16[256,1280]{1,0:T(8,128)(2,1)S(1)} %add.1053), channel_id=1, source_target_pairs={{1,2},{2,1},{5,6},{6,5},{9,10},{10,9},{13,14},{14,13},{17,18},{18,... | collective-permute-start | bytes 1966088 | tf_op jit(solution)/shard_map/ppermute | solution.py:148
  633.0 269.7 %reduce-scatter.23.cloned.1.call-start = ((), (), s32[]{:S(2)}) async-start(), calls=%async_computation.14 | async-start | bytes 3686400 | tf_op jit(solution)/shard_map/reduce_scatter | solution.py:309
  634.3 20.8 %collective-permute-start.50 = (bf16[256,1280]{1,0:T(8,128)(2,1)S(1)}, bf16[256,1280]{1,0:T(8,128)(2,1)S(1)}, u32[]{:S(2)}, u32[]{:S(2)}) collective-permute-start(bf16[256,1280]{1,0:T(8,128)(2,1)S(1)} %add.1054), channel_id=1, source_target_pairs={{1,0},{2,3},{5,4},{6,7},{9,8},{10,11},{13,12},{14,15},{17,16},{18,... | collective-permute-start | bytes 1966088 | tf_op jit(solution)/shard_map/ppermute | solution.py:149
  637.0 32.2 %collective-permute-start.62 = (bf16[256,1280]{1,0:T(8,128)(2,1)S(1)}, bf16[256,1280]{1,0:T(8,128)(2,1)S(1)}, u32[]{:S(2)}, u32[]{:S(2)}) collective-permute-start(bf16[256,1280]{1,0:T(8,128)(2,1)S(1)} %add.1068), channel_id=1, source_target_pairs={{1,0},{2,3},{5,4},{6,7},{9,8},{10,11},{13,12},{14,15},{17,16},{18,... | collective-permute-start | bytes 1966088 | tf_op jit(solution)/shard_map/ppermute | solution.py:149
  684.2 238.1 %reduce-scatter.27.cloned.1.call-start = ((), (), s32[]{:S(2)}) async-start(), calls=%async_computation.16 | async-start | bytes 3686400 | tf_op jit(solution)/shard_map/reduce_scatter | solution.py:309
  704.0 25.8 %collective-permute-start.57 = (bf16[240,1280]{1,0:T(8,128)(2,1)}, bf16[240,1280]{1,0:T(8,128)(2,1)}, u32[]{:S(2)}, u32[]{:S(2)}) collective-permute-start(bf16[240,1280]{1,0:T(8,128)(2,1)} %fusion.127), channel_id=1, source_target_pairs={{0,1},{3,2},{4,5},{7,6},{8,9},{11,10},{12,13},{15,14},{16,17},{19,... | collective-permute-start | bytes 1843208 | tf_op jit(solution)/shard_map/ppermute | solution.py:147
  708.3 24.5 %collective-permute-start.51 = (bf16[256,1280]{1,0:T(8,128)(2,1)}, bf16[256,1280]{1,0:T(8,128)(2,1)}, u32[]{:S(2)}, u32[]{:S(2)}) collective-permute-start(bf16[256,1280]{1,0:T(8,128)(2,1)} %fusion.91), channel_id=1, source_target_pairs={{0,1},{3,2},{4,5},{7,6},{8,9},{11,10},{12,13},{15,14},{16,17},{19,... | collective-permute-start | bytes 1966088 | tf_op jit(solution)/shard_map/ppermute | solution.py:147
  720.6 26.1 %collective-permute-start.63 = (bf16[256,1280]{1,0:T(8,128)(2,1)S(1)}, bf16[256,1280]{1,0:T(8,128)(2,1)}, u32[]{:S(2)}, u32[]{:S(2)}) collective-permute-start(bf16[256,1280]{1,0:T(8,128)(2,1)S(1)} %fusion.94), channel_id=1, source_target_pairs={{0,1},{3,2},{4,5},{7,6},{8,9},{11,10},{12,13},{15,14},{16,17},{19,... | collective-permute-start | bytes 1966088 | tf_op jit(solution)/shard_map/ppermute | solution.py:147
  722.9 256.8 %reduce-scatter.19.cloned.1.call-start = ((), (), s32[]{:S(2)}) async-start(), calls=%async_computation.12 | async-start | bytes 3686400 | tf_op jit(solution)/shard_map/reduce_scatter | solution.py:309
  751.2 29.9 %collective-permute-start.53 = (bf16[256,1280]{1,0:T(8,128)(2,1)S(1)}, bf16[256,1280]{1,0:T(8,128)(2,1)S(1)}, u32[]{:S(2)}, u32[]{:S(2)}) collective-permute-start(bf16[256,1280]{1,0:T(8,128)(2,1)S(1)} %add.1058), channel_id=1, source_target_pairs={{1,0},{2,3},{5,4},{6,7},{9,8},{10,11},{13,12},{14,15},{17,16},{18,... | collective-permute-start | bytes 1966088 | tf_op jit(solution)/shard_map/ppermute | solution.py:149
  752.8 42.2 %collective-permute-start.65 = (bf16[256,1280]{1,0:T(8,128)(2,1)S(1)}, bf16[256,1280]{1,0:T(8,128)(2,1)S(1)}, u32[]{:S(2)}, u32[]{:S(2)}) collective-permute-start(bf16[256,1280]{1,0:T(8,128)(2,1)S(1)} %add.1072), channel_id=1, source_target_pairs={{1,0},{2,3},{5,4},{6,7},{9,8},{10,11},{13,12},{14,15},{17,16},{18,... | collective-permute-start | bytes 1966088 | tf_op jit(solution)/shard_map/ppermute | solution.py:149
  860.6 24.6 %collective-permute-start.67 = (bf16[256,1280]{1,0:T(8,128)(2,1)}, bf16[256,1280]{1,0:T(8,128)(2,1)}, u32[]{:S(2)}, u32[]{:S(2)}) collective-permute-start(bf16[256,1280]{1,0:T(8,128)(2,1)} %convolution_convert_fusion.9), channel_id=1, source_target_pairs={{0,1},{3,2},{4,5},{7,6},{8,9},{11,10},{12,13},{15,14},{16,17},{19,... | collective-permute-start | bytes 1966088 | tf_op jit(solution)/shard_map/ppermute | solution.py:147
  863.6 35.4 %collective-permute-start.70 = (bf16[256,1280]{1,0:T(8,128)(2,1)S(1)}, bf16[256,1280]{1,0:T(8,128)(2,1)}, u32[]{:S(2)}, u32[]{:S(2)}) collective-permute-start(bf16[256,1280]{1,0:T(8,128)(2,1)S(1)} %convolution_convert_fusion.8), channel_id=1, source_target_pairs={{0,1},{3,2},{4,5},{7,6},{8,9},{11,10},{12,13},{15,14},{16,17},{19,... | collective-permute-start | bytes 1966088 | tf_op jit(solution)/shard_map/ppermute | solution.py:147
  876.1 35.0 %collective-permute-start.74 = (bf16[240,1280]{1,0:T(8,128)(2,1)}, bf16[240,1280]{1,0:T(8,128)(2,1)}, u32[]{:S(2)}, u32[]{:S(2)}) collective-permute-start(bf16[240,1280]{1,0:T(8,128)(2,1)} %add.1082), channel_id=1, source_target_pairs={{1,2},{2,1},{5,6},{6,5},{9,10},{10,9},{13,14},{14,13},{17,18},{18,... | collective-permute-start | bytes 1843208 | tf_op jit(solution)/shard_map/ppermute | solution.py:148
  887.4 27.2 %collective-permute-start.68 = (bf16[256,1280]{1,0:T(8,128)(2,1)}, bf16[256,1280]{1,0:T(8,128)(2,1)}, u32[]{:S(2)}, u32[]{:S(2)}) collective-permute-start(bf16[256,1280]{1,0:T(8,128)(2,1)} %add.1076), channel_id=1, source_target_pairs={{1,2},{2,1},{5,6},{6,5},{9,10},{10,9},{13,14},{14,13},{17,18},{18,... | collective-permute-start | bytes 1966088 | tf_op jit(solution)/shard_map/ppermute | solution.py:148
  902.7 21.0 %collective-permute-start.84 = (bf16[160,1280]{1,0:T(8,128)(2,1)}, bf16[160,1280]{1,0:T(8,128)(2,1)}, u32[]{:S(2)}, u32[]{:S(2)}) collective-permute-start(bf16[160,1280]{1,0:T(8,128)(2,1)} %reduce-scatter.23.cloned.1.call-done), channel_id=1, source_target_pairs={{0,4},{4,0},{1,5},{5,1},{2,6},{6,2},{3,7},{7,3},{8,12},{12,8},{9,1... | collective-permute-start | bytes 1228808 | tf_op jit(solution)/shard_map/ppermute | solution.py:310
  913.3 32.5 %collective-permute-start.75 = (bf16[240,1280]{1,0:T(8,128)(2,1)}, bf16[240,1280]{1,0:T(8,128)(2,1)}, u32[]{:S(2)}, u32[]{:S(2)}) collective-permute-start(bf16[240,1280]{1,0:T(8,128)(2,1)} %add.1083), channel_id=1, source_target_pairs={{1,0},{2,3},{5,4},{6,7},{9,8},{10,11},{13,12},{14,15},{17,16},{18,... | collective-permute-start | bytes 1843208 | tf_op jit(solution)/shard_map/ppermute | solution.py:149
  916.9 33.8 %collective-permute-start.69 = (bf16[256,1280]{1,0:T(8,128)(2,1)}, bf16[256,1280]{1,0:T(8,128)(2,1)}, u32[]{:S(2)}, u32[]{:S(2)}) collective-permute-start(bf16[256,1280]{1,0:T(8,128)(2,1)} %add.1077), channel_id=1, source_target_pairs={{1,0},{2,3},{5,4},{6,7},{9,8},{10,11},{13,12},{14,15},{17,16},{18,... | collective-permute-start | bytes 1966088 | tf_op jit(solution)/shard_map/ppermute | solution.py:149
  920.7 40.3 %collective-permute-start.72 = (bf16[256,1280]{1,0:T(8,128)(2,1)}, bf16[256,1280]{1,0:T(8,128)(2,1)}, u32[]{:S(2)}, u32[]{:S(2)}) collective-permute-start(bf16[256,1280]{1,0:T(8,128)(2,1)} %add.1080), channel_id=1, source_target_pairs={{1,0},{2,3},{5,4},{6,7},{9,8},{10,11},{13,12},{14,15},{17,16},{18,... | collective-permute-start | bytes 1966088 | tf_op jit(solution)/shard_map/ppermute | solution.py:149
  (338 other events, 2766.8 us)
Sparse Core Ops, SparseCore 0:
  12.4 35.3 all-gather.10
  50.3 32.9 all-gather.14
  85.7 32.8 all-gather.16
  120.3 32.8 all-gather.12
  199.7 36.9 all-gather.18
  256.4 32.7 all-gather.20
  433.5 53.6 reduce-scatter.24
  573.0 46.3 reduce-scatter.28
  633.1 49.5 reduce-scatter.20
  686.6 47.6 reduce-scatter.22
  738.3 46.4 reduce-scatter.26
  909.6 47.9 reduce-scatter.18

commit v2 on v1

v2 whole, which is shorter than its diff:
```python
import functools

import jax
import jax.numpy as jnp
import numpy as np
from jax import lax
from jax.experimental import pallas as pl
from jax.experimental.pallas import tpu as pltpu
from jax.sharding import PartitionSpec as P

HEAD_DIM = 80
LANES = 128
CHUNK = 192
BACK = 384
EPSILON = 1e-05
NEG = -1e30
SCALE = HEAD_DIM**-0.5
SCALE2 = SCALE * float(np.log2(np.e))
BF = jnp.bfloat16
F32 = jnp.float32
NT = (((1,), (1,)), ((), ()))
NN = (((1,), (0,)), ((), ()))
MIB = 1024 * 1024
LIMIT = 20


def mm(a, b, dims=NN):
    return lax.dot_general(a, b, dims, preferred_element_type=F32)


def up_to(n, m):
    return -(-n // m) * m


def block(shape, index):
    return pl.BlockSpec(shape, lambda *grid: index)


def call(kernel, name, grid, ins, outs, scratch=(), flops=0, moved=0, limit=LIMIT):
    olds = [(n, o[0]) for n, o in enumerate(outs) if o[0] is not None]
    specs = [spec for _, spec in ins] + [pl.BlockSpec(memory_space=pl.ANY)] * len(olds)
    live = len(ins)

    def body(*refs):
        kernel(*refs[:live], *refs[live + len(olds) :])

    return pl.pallas_call(
        body,
        grid=grid,
        in_specs=specs,
        out_specs=[o[3] for o in outs],
        out_shape=[jax.ShapeDtypeStruct(o[1], o[2]) for o in outs],
        scratch_shapes=list(scratch),
        input_output_aliases={live + k: n for k, (n, _) in enumerate(olds)},
        compiler_params=pltpu.CompilerParams(vmem_limit_bytes=limit * MIB),
        cost_estimate=pl.CostEstimate(flops=int(flops), bytes_accessed=int(moved), transcendentals=0),
        name=name,
    )(*[a for a, _ in ins], *[o for _, o in olds])


def lane_iota(shape):
    return lax.broadcasted_iota(jnp.int32, shape, 1)


def norm_stats(v):
    center = jnp.mean(v, axis=-1, keepdims=True)
    centred = v - center
    spread = jnp.mean(centred * centred, axis=-1, keepdims=True)
    r = lax.rsqrt(spread + EPSILON)
    return centred * r, r


def norm_back(v, gain, dn):
    xhat, r = norm_stats(v)
    dx = dn * gain
    back = r * (dx - jnp.mean(dx, axis=-1, keepdims=True) - xhat * jnp.mean(dx * xhat, axis=-1, keepdims=True))
    return back, dn * xhat


def gelu_pair(u):
    cdf = 0.5 * (1.0 + lax.erf(u * float(np.sqrt(0.5))))
    pdf = jnp.exp(-0.5 * u * u) * float(1.0 / np.sqrt(2 * np.pi))
    return u * cdf, cdf + u * pdf


def summed(edge_ref, got_ref, part_ref):
    return jnp.where(edge_ref[0] == 1, got_ref[...], part_ref[...]).astype(F32)


def rows_sum(v):
    return jnp.sum(v, axis=0, keepdims=True)


def store_sums(ref, *values):
    ref[...] = jnp.zeros_like(ref)
    for n, v in enumerate(values):
        ref[0, n : n + 1, :] = v


def project_kernel(
    first, local, edge_ref, got_ref, part_ref, base_ref, add_ref, gain_ref, shift_ref, w_ref, bias_ref, spread_ref,
    ke_ref, qe_ref, ve_ref, h_ref, n_ref, q_ref, kv_ref,
):
    h = base_ref[...].astype(F32)
    if not first:
        h = h + summed(edge_ref, got_ref, part_ref) + add_ref[...]
    h_ref[...] = h
    xhat, _ = norm_stats(h)
    n = (xhat * gain_ref[...] + shift_ref[...]).astype(BF)
    n_ref[...] = n
    m = (mm(n, w_ref[...]) + bias_ref[...]).astype(BF)
    spread = spread_ref[...]
    q_ref[...] = (mm(m[:, local : 2 * local], spread) + qe_ref[...]).astype(BF)
    kv_ref[0] = (mm(m[:, 2 * local : 3 * local], spread) + ke_ref[...].astype(F32)).astype(BF)
    kv_ref[1] = (mm(m[:, 3 * local :], spread) + ve_ref[...]).astype(BF)


def split3(v):
    hi = v.astype(BF).astype(F32)
    mid = (v - hi).astype(BF).astype(F32)
    return hi, mid, v - hi - mid


def attend_kernel(
    heads, edge_ref, q_ref, k0_ref, v0_ref, k1_ref, v1_ref, gather_ref, w_ref, o_ref, qa_ref, att_ref, part_ref, acc_ref
):
    q = q_ref[...]
    s0 = mm(q, k0_ref[0], NT)
    s1 = mm(q, k1_ref[0], NT)
    top = jnp.maximum(jnp.max(s0, axis=1, keepdims=True), jnp.max(s1, axis=1, keepdims=True))
    p0 = jnp.exp2((s0 - top) * SCALE2).astype(BF)
    p1 = jnp.exp2((s1 - top) * SCALE2).astype(BF)
    o = mm(p0, v0_ref[0]) + mm(p1, v1_ref[0])
    lane = lane_iota(o.shape)
    total = jnp.sum(jnp.where(lane == HEAD_DIM, o, 0.0), axis=1, keepdims=True)
    o = jnp.where(lane < HEAD_DIM, o / total, 0.0).astype(BF)
    o_ref[...] = o
    hi, mid, lo = split3(-(top + jnp.log2(total) * (1.0 / SCALE2)))
    qa = jnp.where(lane == HEAD_DIM + 1, hi, q.astype(F32))
    qa = jnp.where(lane == HEAD_DIM + 2, mid, qa)
    qa = jnp.where(lane == HEAD_DIM + 3, lo, qa)
    qa_ref[...] = qa.astype(BF)
    head = pl.program_id(0)
    here = mm(o, gather_ref[...])

    @pl.when(head == 0)
    def _():
        acc_ref[...] = here

    @pl.when(head > 0)
    def _():
        acc_ref[...] += here

    @pl.when(head == heads - 1)
    def _():
        att = acc_ref[...].astype(BF)
        att_ref[...] = att
        part_ref[...] = mm(att, w_ref[...], NT).astype(BF)


def feed_kernel(
    back, tiles, edge_ref, got_ref, part_ref, h_ref, add_ref, gain_ref, shift_ref, up_ref, bias_ref, down_ref, *refs
):
    if back:
        (g_ref, mid_ref, n_ref, act_ref, low_ref, d_ref, out_ref, back_ref, sum_ref, usum_ref,
         n_s, acc_s, low_s, acc2_s) = refs
    else:
        mid_ref, n_ref, act_ref, slope_ref, out_ref, n_s, acc_s = refs
    tile = pl.program_id(0)

    @pl.when(tile == 0)
    def _():
        mid = h_ref[...] + summed(edge_ref, got_ref, part_ref) + add_ref[...]
        mid_ref[...] = mid
        xhat, _ = norm_stats(mid)
        n = (xhat * gain_ref[...] + shift_ref[...]).astype(BF)
        n_ref[...] = n
        n_s[...] = n
        if back:
            g = g_ref[...]
            low = g.astype(BF)
            low_ref[...] = low
            low_s[...] = low
            store_sums(sum_ref, rows_sum(g))

    act, slope = gelu_pair(mm(n_s[...], up_ref[...]) + bias_ref[...])
    act = act.astype(BF)
    act_ref[...] = act
    here = mm(act, down_ref[...], NT)
    if back:
        d = (mm(low_s[...], down_ref[...]) * slope).astype(BF)
        d_ref[...] = d
        usum_ref[...] = jnp.broadcast_to(rows_sum(d.astype(F32))[None], usum_ref.shape)
        here2 = mm(d, up_ref[...], NT)
    else:
        slope_ref[...] = slope.astype(BF)

    @pl.when(tile == 0)
    def _():
        acc_s[...] = here
        if back:
            acc2_s[...] = here2

    @pl.when(tile > 0)
    def _():
        acc_s[...] += here
        if back:
            acc2_s[...] += here2

    @pl.when(tile == tiles - 1)
    def _():
        out_ref[...] = acc_s[...].astype(BF)
        if back:
            back_ref[...] = acc2_s[...].astype(BF)


def norm2_back_kernel(
    edge_ref, got_ref, part_ref, g_ref, mid_ref, gain_ref, w_ref, spread_ref, mg_ref, low_ref, do_ref, sum_ref
):
    dn = summed(edge_ref, got_ref, part_ref)
    back, gg = norm_back(mid_ref[...], gain_ref[...], dn)
    mg = g_ref[...] + back
    mg_ref[...] = mg
    low = mg.astype(BF)
    low_ref[...] = low
    do_ref[...] = mm(mm(low, w_ref[...]).astype(BF), spread_ref[...]).astype(BF)
    store_sums(sum_ref, rows_sum(gg), rows_sum(dn), rows_sum(mg))


def attend_back_kernel(first, edge_ref, qa_ref, o_ref, do_ref, k0_ref, v0_ref, k1_ref, v1_ref, *refs):
    if first:
        dq_ref, dk0_ref, dv0_ref, dk1_ref, dv1_ref = refs
        olds = (None,) * 4
    else:
        olds = refs[:4]
        dq_ref, dk0_ref, dv0_ref, dk1_ref, dv1_ref = refs[4:]
    qa = qa_ref[...]
    do = do_ref[...].astype(F32)
    lane = lane_iota(do.shape)
    delta = -jnp.sum(o_ref[...].astype(F32) * do, axis=1, keepdims=True)
    hi = delta.astype(BF).astype(F32)
    doa = jnp.where(lane == HEAD_DIM, hi, do)
    doa = jnp.where(lane == HEAD_DIM + 1, delta - hi, doa).astype(BF)
    dqt = None
    for k_ref, v_ref, dk_ref, dv_ref, dk_old, dv_old in (
        (k0_ref, v0_ref, dk0_ref, dv0_ref, olds[0], olds[1]),
        (k1_ref, v1_ref, dk1_ref, dv1_ref, olds[2], olds[3]),
    ):
        k = k_ref[0]
        pt = jnp.exp2(mm(k, qa, NT) * SCALE2)
        dst = (pt * mm(v_ref[0], doa, NT)).astype(BF)
        dv = mm(pt.astype(BF), doa)
        dk = mm(dst, qa)
        dv_ref[...] = dv if first else dv_old[...] + dv
        dk_ref[...] = dk if first else dk_old[...] + dk
        part = mm(k.T, dst)
        dqt = part if dqt is None else dqt + part
    dq_ref[...] = (dqt.T * SCALE).astype(BF)


def project_back_kernel(
    local, edge_ref, dq_ref, dk_ref, dv_ref, got_ref, gather_ref, w_ref, d_ref, part_ref, sum_ref
):
    gather = gather_ref[...]
    dq = mm(dq_ref[...], gather).astype(BF)
    dk = mm((dk_ref[...] * SCALE + got_ref[0].astype(F32)).astype(BF), gather).astype(BF)
    dv = mm((dv_ref[...] + got_ref[1].astype(F32)).astype(BF), gather).astype(BF)
    d = jnp.concatenate([jnp.zeros_like(dq), dq, dk, dv], axis=1)
    d_ref[...] = d
    part_ref[...] = mm(d, w_ref[...], NT).astype(BF)
    store_sums(sum_ref, rows_sum(d.astype(F32)))


def norm1_back_kernel(edge_ref, got_ref, part_ref, mg_ref, h_ref, gain_ref, g_ref, sum_ref):
    dn = summed(edge_ref, got_ref, part_ref)
    back, gg = norm_back(h_ref[...], gain_ref[...], dn)
    g_ref[...] = mg_ref[...] + back
    store_sums(sum_ref, rows_sum(gg), rows_sum(dn))


def feed_back_kernel(
    tiles, edge_ref, got_ref, part_ref, mg_ref, h_ref, gain_ref, down_ref, up_ref, slope_ref,
    g_ref, low_ref, d_ref, out_ref, sum_ref, usum_ref, low_s, acc_s,
):
    tile = pl.program_id(0)

    @pl.when(tile == 0)
    def _():
        dn = summed(edge_ref, got_ref, part_ref)
        back, gg = norm_back(h_ref[...], gain_ref[...], dn)
        g = mg_ref[...] + back
        g_ref[...] = g
        low = g.astype(BF)
        low_ref[...] = low
        low_s[...] = low
        store_sums(sum_ref, rows_sum(gg), rows_sum(dn), rows_sum(g))

    d = (mm(low_s[...], down_ref[...]) * slope_ref[...].astype(F32)).astype(BF)
    d_ref[...] = d
    usum_ref[...] = jnp.broadcast_to(rows_sum(d.astype(F32))[None], usum_ref.shape)
    here = mm(d, up_ref[...], NT)

    @pl.when(tile == 0)
    def _():
        acc_s[...] = here

    @pl.when(tile > 0)
    def _():
        acc_s[...] += here

    @pl.when(tile == tiles - 1)
    def _():
        out_ref[...] = acc_s[...].astype(BF)


def swap(n, step):
    return [(i, i ^ step) for i in range(n)]


def turn_kernel(edge_ref, *refs):
    part, got, pair, there, fresh = refs[:5]
    outs = refs[5:]
    if part is not None:
        outs[0][...] = part[...] + got[...]
    if pair is not None:
        total = pair[...] + there[...]
        outs[-1][...] = total if fresh is None else jnp.where(edge_ref[0] == 1, fresh[...], total)


class Flow:
    def __init__(self, tp):
        self.tp, self.token = tp, None
        self.inward = self.across = self.outward = None
        index = lax.axis_index("tp")
        self.edge = jnp.where((index == 0) | (index == 3), 1, 0).astype(jnp.int32)[None]

    def enter(self, value):
        if self.token is not None:
            value, self.token = lax.optimization_barrier((value, self.token))
        return value

    def leave(self, value):
        self.token = value

    def knob(self):
        return self.enter(self.edge)

    def tick(self, fresh=None):
        if self.tp != 4:
            whole = lax.psum(fresh, "tp")
            return {"part": whole, "got": whole, "done": True}
        inward, across, outward = self.inward, self.across, self.outward
        got = self.got if inward or outward else None
        if outward:
            outward.update(got=got, done=True)
        job = {"part": fresh, "done": False} if fresh is not None else None
        pair = send = None
        if inward or across:
            values = [inward and inward["part"], inward and got, across and across["part"], across and self.there,
                      fresh if across else None]
            shape = (inward or across)["part"].shape
            spec = pl.BlockSpec((shape[0] // 2, shape[1]), lambda i: (i, 0))
            given = [n for n, v in enumerate(values) if v is not None]
            made = (inward is not None) + (across is not None)

            def body(edge_ref, *refs):
                full = [None] * 5
                for n, ref in zip(given, refs):
                    full[n] = ref
                turn_kernel(edge_ref, *full, *refs[len(given) :])

            res = pl.pallas_call(
                body,
                grid=(2,),
                in_specs=[pl.BlockSpec(memory_space=pltpu.SMEM)] + [spec] * len(given),
                out_specs=[spec] * made,
                out_shape=[jax.ShapeDtypeStruct(shape, BF)] * made,
                compiler_params=pltpu.CompilerParams(vmem_limit_bytes=LIMIT * MIB),
                cost_estimate=pl.CostEstimate(flops=0, bytes_accessed=14 * shape[0] * shape[1], transcendentals=0),
                name="turn",
            )(self.knob(), *[values[n] for n in given])
            self.leave(res[0])
            if inward:
                pair = res[0]
            if across:
                send = res[-1]
                across["part"] = send
        self.across = inward
        if inward:
            inward["part"] = pair
            self.there = lax.ppermute(pair, "tp", [(1, 2), (2, 1)])
        self.inward, self.outward = job, across
        if job or across:
            perm = ([(0, 1), (3, 2)] if job else []) + ([(1, 0), (2, 3)] if across else [])
            self.got = lax.ppermute(send if across else fresh, "tp", perm)
        return job

    def take(self, job):
        while not job["done"]:
            self.tick()
        return job["got"], job["part"]


def group_sum(v, fsdp):
    v = v + lax.ppermute(v, "ctx", swap(2, 1))
    step = 1
    while step < fsdp:
        v = v + lax.ppermute(v, "fsdp", swap(fsdp, step))
        step *= 2
    return v


def per_device(
    sizes,
    inputs,
    lengths,
    cotangent,
    norm_gains,
    norm_shifts,
    qkv_weight,
    qv_bias,
    out_weight,
    out_bias,
    up_weight,
    up_bias,
    down_weight,
    down_bias,
):
    fsdp, tp = sizes
    clips, rows, width = inputs.shape
    assert clips == 1
    local = qkv_weight.shape[-1]
    units = up_weight.shape[-1]
    heads = local // HEAD_DIM
    wide = heads * LANES
    square = 4 * local
    lined = up_to(local, LANES)
    layers = norm_gains.shape[0]
    last = layers - 1
    me = lax.axis_index("ctx")
    full = up_to(rows, BACK)
    count = full // CHUNK
    each = range(count)
    unit = 256 if units % 256 == 0 else LANES
    tiles = units // unit
    length = lengths[0]
    flow = Flow(tp)

    spread = np.zeros((lined, wide), np.float32)
    for f in range(local):
        spread[f, f // HEAD_DIM * LANES + f % HEAD_DIM] = 1.0
    spread_line = jnp.asarray(spread, BF)
    spread_own = jnp.asarray(spread[:local], BF)
    gather_line = jnp.asarray(spread.T, BF)
    gather_own = jnp.asarray(spread[:local].T, BF)
    head_lane = np.arange(wide) % LANES
    q_extra = jnp.asarray((head_lane == HEAD_DIM)[None, :], F32)
    k_ones = jnp.asarray(((head_lane > HEAD_DIM) & (head_lane <= HEAD_DIM + 3))[None, :], F32)
    v_ones = jnp.asarray(((head_lane >= HEAD_DIM) & (head_lane <= HEAD_DIM + 1))[None, :], F32)
    row = jnp.arange(full)[:, None]
    live = (row < rows) & (row + me * rows < length)
    k_extra = (k_ones + jnp.where(live, 0.0, NEG) * q_extra).astype(BF)

    half = qkv_weight.shape[1] // 2

    def mine(w):
        return lax.dynamic_slice_in_dim(w, me * half, half, axis=0)

    def fetch(w):
        return lax.all_gather(w, ("fsdp", "ctx"), axis=0, tiled=True)

    attn_w, up_w, down_w = [], [], []
    for layer in range(layers):
        q3 = mine(qkv_weight[layer]).reshape(half, 3 * local)
        mats = [jnp.concatenate([mine(out_weight[layer]), q3], axis=1), mine(up_weight[layer]), mine(down_weight[layer])]
        if layer == 0:
            attn = fetch(mats[0])
            feeds = fetch(jnp.concatenate(mats[1:], axis=1))
            starts = (0, 0, units)
            held = (attn, feeds, feeds)
        else:
            everything = fetch(jnp.concatenate(mats, axis=1))
            starts = (0, square, square + units)
            held = (everything,) * 3
        attn_w.append(held[0])
        up_w.append((held[1], starts[1] // unit))
        down_w.append((held[2], starts[2] // unit))

    def give(*mats):
        theirs, ours = [], []
        for g in mats:
            n = g.shape[1] // 2
            theirs.append(lax.dynamic_slice_in_dim(g, (1 - me) * n, n, axis=1))
            ours.append(lax.dynamic_slice_in_dim(g, me * n, n, axis=1))
        got = lax.ppermute(jnp.concatenate(theirs, axis=1), "ctx", swap(2, 1))
        part = lax.psum_scatter(jnp.concatenate(ours, axis=1) + got, "fsdp", scatter_dimension=0, tiled=True)
        other = lax.ppermute(part, "ctx", swap(2, 1))
        low = jnp.where(me == 0, part, other)
        high = jnp.where(me == 0, other, part)
        outs, at = [], 0
        for g in mats:
            n = g.shape[1] // 2
            outs.append(jnp.concatenate([low[:, at : at + n], high[:, at : at + n]], axis=1).astype(F32))
            at += n
        return outs

    tall = ((0, full - rows), (0, 0))
    first_input = jnp.pad(inputs[0], tall)
    first_grad = jnp.where(live, jnp.pad(cotangent[0], tall).astype(F32), 0.0)
    edge_spec = pl.BlockSpec(memory_space=pltpu.SMEM)

    def rows_of(c, cols):
        return block((CHUNK, cols), (c, 0))

    def whole(a):
        return (a, block(a.shape, (0,) * a.ndim))

    def line(v):
        return (v[None, :], block((1, v.shape[0]), (0, 0)))

    def unit_line(v):
        return (v[None, :], pl.BlockSpec((1, unit), lambda t: (0, t)))

    def unit_cols(w):
        array, first = w
        return (array, pl.BlockSpec((array.shape[0], unit), lambda t: (0, first + t)))

    sum_spec = block((1, 8, width), (0, 0, 0))
    sum_out = (None, (1, 8, width), F32, sum_spec)
    square_sum_out = (None, (1, 8, square), F32, block((1, 8, square), (0, 0, 0)))
    unit_sum_out = (None, (1, 8, units), F32, pl.BlockSpec((1, 8, unit), lambda t: (0, 0, t)))
    part_out = (None, (CHUNK, width), BF, block((CHUNK, width), (0, 0)))
    f32_rows = pltpu.VMEM((CHUNK, width), F32)
    bf_rows = pltpu.VMEM((CHUNK, width), BF)

    keep = [dict() for _ in range(layers)]
    grads = {"now": first_grad}

    def edge():
        return (flow.knob(), edge_spec)

    def both_of(job):
        spec = block((CHUNK, width), (0, 0))
        got, part = flow.take(job)
        return [(got, spec), (part, spec)]

    def out(store, name, cols, dtype, c):
        return (store.get(name) if c else None, (full, cols), dtype, rows_of(c, cols))

    def tile_out(store, name, c):
        return (store.get(name) if c else None, (full, units), BF, pl.BlockSpec((CHUNK, unit), lambda t: (c, t)))

    def project(layer, c, job):
        k = keep[layer]
        if job is None:
            pair = [(jnp.zeros((8, LANES), BF), block((8, LANES), (0, 0)))] * 2
            base, add = first_input, jnp.zeros((width,), F32)
        else:
            pair = both_of(job)
            base, add = keep[layer - 1]["mid"], down_bias[layer - 1]
        qb, vb = qv_bias[layer, 0], qv_bias[layer, 1]
        bias = jnp.concatenate([jnp.zeros_like(qb), qb, jnp.zeros_like(qb), vb])
        ins = [edge(), *pair, (base, rows_of(c, width)), line(add), line(norm_gains[layer, 0]), line(norm_shifts[layer, 0]),
               (attn_w[layer], block((width, square), (0, 0))), line(bias), whole(spread_own), (k_extra, rows_of(c, wide)), whole(q_extra), whole(v_ones)]
        outs = [out(k, "hidden", width, F32, c), out(k, "normed", width, BF, c), out(k, "q", wide, BF, c),
                (k.get("kv0") if c else None, (2, full, wide), BF, block((2, CHUNK, wide), (0, c, 0)))]
        res = call(functools.partial(project_kernel, job is None, local), "project", (1,), ins, outs,
                   flops=2 * CHUNK * width * square, moved=2 * width * square)
        k["hidden"], k["normed"], k["q"], k["kv0"] = res
        flow.leave(res[2])

    def share(layer):
        k = keep[layer]
        k["kv1"] = lax.ppermute(k["kv0"], "ctx", swap(2, 1))

    def head_specs(c, rows=CHUNK):
        q = pl.BlockSpec((rows, LANES), lambda h: (c, h))
        keys = pl.BlockSpec((1, full, LANES), lambda h: (0, 0, h))
        values = pl.BlockSpec((1, full, LANES), lambda h: (1, 0, h))
        return q, keys, values

    def attend(layer, c):
        k = keep[layer]
        q, keys, values = head_specs(c)
        ins = [edge(), (k["q"], q), (k["kv0"], keys), (k["kv0"], values), (k["kv1"], keys), (k["kv1"], values),
               (gather_line, pl.BlockSpec((LANES, lined), lambda h: (h, 0))),
               (attn_w[layer], block((width, lined), (0, 0)))]
        outs = [(k.get("o") if c else None, (full, wide), BF, q), (k.get("qa") if c else None, (full, wide), BF, q),
                out(k, "attended", lined, BF, c), part_out]
        res = call(functools.partial(attend_kernel, heads), "attend", (heads,), ins, outs,
                   [pltpu.VMEM((CHUNK, lined), F32)], flops=8 * CHUNK * full * wide, moved=8 * full * wide)
        k["o"], k["qa"], k["attended"], part = res
        flow.leave(part)
        return flow.tick(part)

    def feed(layer, c, job):
        k = keep[layer]
        back = layer == last
        pair = both_of(job)
        ins = [edge(), *pair, (k["hidden"], rows_of(c, width)), line(out_bias[layer]), line(norm_gains[layer, 1]),
               line(norm_shifts[layer, 1]), unit_cols(up_w[layer]), unit_line(up_bias[layer]), unit_cols(down_w[layer])]
        outs = [out(k, "mid", width, F32, c), out(k, "normed2", width, BF, c), tile_out(k, "active", c)]
        scratch = [bf_rows, f32_rows]
        if back:
            ins.append((grads["now"], rows_of(c, width)))
            outs += [out(k, "low", width, BF, c), tile_out(k, "d_upper", c), out(k, "late", width, BF, c), part_out,
                     sum_out, unit_sum_out]
            scratch += [bf_rows, f32_rows]
        else:
            outs += [tile_out(k, "slope", c), part_out]
        res = call(functools.partial(feed_kernel, back, tiles), "feed", (tiles,), ins, outs, scratch,
                   flops=4 * CHUNK * width * units, moved=4 * width * units)
        k["mid"], k["normed2"], k["active"] = res[:3]
        if back:
            k["low"], k["d_upper"], k["late"], part_back, s, us = res[3:]
            k.setdefault("down_b", []).append(s[0, 0])
            k.setdefault("up_b", []).append(us[0, 0])
            flow.leave(part_back)
            return flow.tick(part_back)
        k["slope"], part = res[3:]
        flow.leave(part)
        return flow.tick(part)

    def norm2_back(layer, c, job):
        k = keep[layer]
        pair = both_of(job)
        ins = [edge(), *pair, (grads["now"], rows_of(c, width)), (k["mid"], rows_of(c, width)), line(norm_gains[layer, 1]),
               (attn_w[layer], block((width, lined), (0, 0))), whole(spread_line)]
        outs = [out(k, "mid_grad", width, F32, c), out(k, "low2", width, BF, c), out(k, "do", wide, BF, c), sum_out]
        k["mid_grad"], k["low2"], k["do"], s = call(norm2_back_kernel, "norm2_back", (1,), ins, outs,
                                                    flops=2 * CHUNK * width * lined, moved=20 * CHUNK * width)
        k.setdefault("gains2", []).append(s[0, 0])
        k.setdefault("shifts2", []).append(s[0, 1])
        k.setdefault("out_b", []).append(s[0, 2])
        flow.leave(k["do"])

    def attend_back(layer, c, sums):
        k = keep[layer]
        q, keys, values = head_specs(c, BACK)
        acc = pl.BlockSpec((full, LANES), lambda h: (0, h))
        first = sums is None
        ins = [edge(), (k["qa"], q), (k["o"], q), (k["do"], q), (k["kv0"], keys), (k["kv0"], values), (k["kv1"], keys),
               (k["kv1"], values)]
        live_in = len(ins)
        olds = [] if first else [(s, acc) for s in sums]
        old_dq = k.get("dq") if c else None
        everything = ins + olds + ([] if old_dq is None else [(old_dq, pl.BlockSpec(memory_space=pl.ANY))])
        aliases = {} if first else {live_in + n: 1 + n for n in range(4)}
        if old_dq is not None:
            aliases[len(everything) - 1] = 0

        def body(*refs):
            kept = live_in + len(olds)
            attend_back_kernel(first, *refs[:kept], *refs[len(everything) :])

        res = pl.pallas_call(
            body,
            grid=(heads,),
            in_specs=[s for _, s in everything],
            out_specs=[q] + [acc] * 4,
            out_shape=[jax.ShapeDtypeStruct((full, wide), BF)] + [jax.ShapeDtypeStruct((full, wide), F32)] * 4,
            input_output_aliases=aliases,
            compiler_params=pltpu.CompilerParams(vmem_limit_bytes=LIMIT * MIB),
            cost_estimate=pl.CostEstimate(flops=20 * BACK * full * wide, bytes_accessed=40 * full * wide, transcendentals=0),
            name="attend_back",
        )(*[a for a, _ in everything])
        k["dq"] = res[0]
        flow.leave(res[0])
        return res[1:]

    def share_back(sums):
        dk0, dv0, dk1, dv1 = sums
        theirs = jnp.stack([dk1 * SCALE, dv1]).astype(BF)
        return dk0, dv0, lax.ppermute(theirs, "ctx", swap(2, 1))

    def project_back(layer, c, shared):
        k = keep[layer]
        dk0, dv0, got = shared
        ins = [edge(), (k["dq"], rows_of(c, wide)), (dk0, rows_of(c, wide)), (dv0, rows_of(c, wide)),
               (got, block((2, CHUNK, wide), (0, c, 0))), whole(gather_own), (attn_w[layer], block((width, square), (0, 0)))]
        outs = [out(k, "d_mixed", square, BF, c), part_out, square_sum_out]
        k["d_mixed"], part, s = call(functools.partial(project_back_kernel, local), "project_back", (1,), ins, outs,
                                     flops=2 * CHUNK * width * square, moved=2 * width * square)
        k.setdefault("mixed_b", []).append(s[0, 0])
        flow.leave(part)
        return flow.tick(part)

    def norm1_back(layer, c, job):
        k = keep[layer]
        pair = both_of(job)
        ins = [edge(), *pair, (k["mid_grad"], rows_of(c, width)), (k["hidden"], rows_of(c, width)), line(norm_gains[layer, 0])]
        outs = [out(k, "grad", width, F32, c), sum_out]
        k["grad"], s = call(norm1_back_kernel, "norm1_back", (1,), ins, outs, moved=20 * CHUNK * width)
        k.setdefault("gains1", []).append(s[0, 0])
        k.setdefault("shifts1", []).append(s[0, 1])
        flow.leave(k["grad"])

    def feed_back(layer, c, job):
        k, b = keep[layer], keep[layer - 1]
        pair = both_of(job)
        ins = [edge(), *pair, (k["mid_grad"], rows_of(c, width)), (k["hidden"], rows_of(c, width)), line(norm_gains[layer, 0]),
               unit_cols(down_w[layer - 1]), unit_cols(up_w[layer - 1]),
               (b["slope"], pl.BlockSpec((CHUNK, unit), lambda t: (c, t)))]
        outs = [out(k, "grad", width, F32, c), out(b, "low", width, BF, c), tile_out(b, "d_upper", c), part_out, sum_out,
                unit_sum_out]
        res = call(functools.partial(feed_back_kernel, tiles), "feed_back", (tiles,), ins, outs, [bf_rows, f32_rows],
                   flops=4 * CHUNK * width * units, moved=4 * width * units)
        k["grad"], b["low"], b["d_upper"], part, s, us = res
        k.setdefault("gains1", []).append(s[0, 0])
        k.setdefault("shifts1", []).append(s[0, 1])
        b.setdefault("down_b", []).append(s[0, 2])
        b.setdefault("up_b", []).append(us[0, 0])
        flow.leave(part)
        return flow.tick(part)

    def weight_grad(left, right):
        return lax.dot_general(left, right, (((0,), (0,)), ((), ())), preferred_element_type=F32).astype(BF)

    owned = [dict() for _ in range(layers)]

    def grad_feed(layer):
        k = keep[layer]
        down = weight_grad(flow.enter(k["low"]), k["active"])
        flow.leave(down)
        up = weight_grad(flow.enter(k["normed2"]), k["d_upper"])
        flow.leave(up)
        owned[layer]["up"], owned[layer]["down"] = give(up, down)

    def grad_attn(layer):
        k = keep[layer]
        g1 = weight_grad(flow.enter(k["normed"]), k["d_mixed"])
        g2 = weight_grad(k["low2"], k["attended"])
        g = jnp.concatenate([g2[:, :local], g1[:, local:]], axis=1)
        flow.leave(g)
        (owned[layer]["attn"],) = give(g)

    jobs = [None] * count
    for layer in range(layers):
        for c in each:
            project(layer, c, jobs[c])
        share(layer)
        jobs = [attend(layer, c) for c in each]
        jobs = [feed(layer, c, jobs[c]) for c in each]
    k = keep[last]
    final = lax.psum(k["late"], "tp").astype(F32)
    outputs = (k["mid"] + final + down_bias[last]).astype(BF)
    vectors = [None] * layers
    for layer in reversed(range(layers)):
        k = keep[layer]
        sums = None
        for c in each:
            norm2_back(layer, c, jobs[c])
            if (c + 1) * CHUNK % BACK == 0:
                sums = attend_back(layer, c * CHUNK // BACK, sums)
        shared = share_back(sums)
        grad_feed(layer)
        jobs = [project_back(layer, c, shared) for c in each]
        grad_attn(layer)
        for c in each:
            if layer > 0:
                jobs[c] = feed_back(layer, c, jobs[c])
            else:
                norm1_back(layer, c, jobs[c])
        grads["now"] = k["grad"]
        total = {n: functools.reduce(jnp.add, k[n])
                 for n in ("gains1", "gains2", "shifts1", "shifts2", "mixed_b", "out_b", "up_b", "down_b")}
        mixed = total["mixed_b"]
        flat = jnp.concatenate(
            [total["gains1"], total["gains2"], total["shifts1"], total["shifts2"], mixed[local : 2 * local],
             mixed[3 * local :], total["out_b"], total["up_b"], total["down_b"]]
        )
        size = flat.shape[0]
        flat = jnp.pad(flat, (0, up_to(size, 1024) - size)).reshape(-1, LANES)
        flat = group_sum(flat, fsdp).reshape(-1)
        ends = np.cumsum([width] * 4 + [local] * 2 + [width, units, width])[:-1]
        vectors[layer] = jnp.split(flat[:size], ends)

    def stack(index):
        return jnp.stack([v[index] for v in vectors])

    def both(index):
        return jnp.stack([jnp.stack([v[index], v[index + 1]]) for v in vectors])

    def matrices(name):
        return jnp.stack([o[name] for o in owned])

    attn = matrices("attn")
    return (
        outputs[None, :rows],
        grads["now"][None, :rows],
        both(0),
        both(2),
        attn[:, :, local:].reshape(layers, -1, 3, local),
        both(4),
        attn[:, :, :local],
        stack(6),
        matrices("up"),
        stack(7),
        matrices("down"),
        stack(8),
    )


def solution(mesh):
    in_specs = (
        P("fsdp", "ctx", None),
        P("fsdp"),
        P("fsdp", "ctx", None),
        P(),
        P(),
        P(None, "fsdp", None, "tp"),
        P(None, None, "tp"),
        P(None, "fsdp", "tp"),
        P(),
        P(None, "fsdp", "tp"),
        P(None, "tp"),
        P(None, "fsdp", "tp"),
        P(),
    )
    out_specs = (
        P("fsdp", "ctx", None),
        P("fsdp", "ctx", None),
        P(),
        P(),
        P(None, "fsdp", None, "tp"),
        P(None, None, "tp"),
        P(None, "fsdp", "tp"),
        P(),
        P(None, "fsdp", "tp"),
        P(None, "tp"),
        P(None, "fsdp", "tp"),
        P(),
    )
    sizes = (mesh.shape["fsdp"], mesh.shape["tp"])
    return jax.shard_map(
        functools.partial(per_device, sizes), mesh=mesh, in_specs=in_specs, out_specs=out_specs, check_vma=False
    )
```

time: 1010 us -> 837 us (0.83)
  waiting for transfers between devices: 387 us -> 152 us
  Pallas kernels: 73.9 us -> 219 us
  matrix products: 136 us -> 25.6 us
  other arithmetic: 142 us -> 56.9 us
  local copies, waits for them, and re-layouts: 103 us -> 187 us
  starting transfers between devices: 137 us -> 165 us
    ppermute x76 -> x72, waiting for transfers between devices: 358 us -> 121 us  [the longest x36 115 us: tick(): self.got = lax.ppermute(send if across else fresh, 'tp', perm)]
    pallas_call x12 -> x84, Pallas kernels: 73.9 us -> 219 us  [the longest x48 166 us: call(): pl.pallas_call(body, grid=grid, in_specs=specs, out_specs=[o[3] for o in...]
    dot_general x76 -> x0, matrix products: 105 us -> none  [mm(): return lax.dot_general(a, b, dims, preferred_element_type=F32)]
    unnamed x630 -> x475, local copies, waits for them, and re-layouts: 79 us -> 156 us
    reduce_sum x38 -> x0, other arithmetic: 40.4 us -> none  [the longest x8 16.1 us: norm_back(): return (back, jnp.sum(dn * xhat, axis=0), jnp.sum(dn, axis=0))]
    ppermute x76 -> x72, starting transfers between devices: 126 us -> 156 us  [the longest x36 89.3 us: tick(): self.got = lax.ppermute(send if across else fresh, 'tp', perm)]
    add x64 -> x13, other arithmetic: 51.5 us -> 25.6 us  [the longest x4 16.6 us: give(): jnp.concatenate(ours, axis=1) + got]
    convert_element_type x25 -> x1, other arithmetic: 12.6 us -> 0.2 us  [per_device(): k_extra = (k_ones + jnp.where(live, 0.0, NEG) * q_extra).astype(BF)]
  transfers between devices with their start and end apart: 100 -> 90, of which waited for: 41 -> 30; matrix products, arithmetic and copies ran while one was open for 32% -> 17% of each run, Pallas kernels for 7% -> 24%
where the time goes in v2:
time: 837 us; the launch traced here: 823 us
  Pallas kernels  219 us (26%)
  local copies, waits for them, and re-layouts  187 us (22%)
  starting transfers between devices  165 us (20%)
  waiting for transfers between devices  152 us (18%)
  other arithmetic  56.9 us (7%)
  matrix products  25.6 us (3%)
  between operations  18.6 us (2%)
    pallas_call x48, Pallas kernels, call(): pl.pallas_call(body, grid=grid, in_specs=specs, out_specs=[o[3] for o in...  166 us
    unnamed x475, local copies, waits for them, and re-layouts  156 us
    ppermute x36, waiting for transfers between devices, tick(): self.got = lax.ppermute(send if across else fresh, 'tp', perm)  115 us
    ppermute x36, starting transfers between devices, tick(): self.got = lax.ppermute(send if across else fresh, 'tp', perm)  89.3 us
    pallas_call x4, Pallas kernels, attend_back(): pl.pallas_call(body, grid=(heads,), in_specs=[s for _, s in everything],...  36.3 us
    ppermute x4, starting transfers between devices, give(): got = lax.ppermute(jnp.concatenate(theirs, axis=1), 'ctx', swap(2, 1))  28 us
    dot_general x8, matrix products, weight_grad(): lax.dot_general(left, right, (((0,), (0,)), ((), ())), preferred_element_...  25.6 us
    all_gather x3, waiting for transfers between devices, fetch(): return lax.all_gather(w, ('fsdp', 'ctx'), axis=0, tiled=True)  24.4 us
  transfers between devices with their start and end apart: 90, of which 30 were waited for; matrix products, arithmetic and copies ran while one was open for 17% of the time, Pallas kernels for 24%

profile of v2, /device:TPU:1, one launch (start us, length us, event | category | flops | bytes accessed | tf_op | source)
XLA Modules:
  0.0 823.5 jit_solution(13890826954098424770)
XLA Ops:
  22.7 24.3 %all-gather.4.cloned.1.call-done.refs_7_.refs_6_ = bf16[1280,1280]{1,0:T(8,128)(2,1)} async-done(((bf16[160,1280]{1,0:T(8,128)(2,1)}), bf16[1280,1280]{1,0:T(8,128)(2,1)}) %all-gather.4.cloned.1.call-update) | async-done | bytes 3276816 | tf_op jit(solution)/shard_map/all_gather | solution.py:470
  57.4 5.0 attend.8
  65.5 5.0 attend.9
  71.9 4.0 collective-permute-done.1.refs_1_
  76.7 5.0 attend.10
  81.6 4.8 collective-permute-done.2.refs_1_
  86.6 4.8 collective-permute-start.4
  92.3 5.0 attend.11
  111.7 5.5 feed.8
  121.1 6.5 feed.9
  132.7 5.6 feed.10
  143.5 5.6 feed.11
  160.9 3.8 copy-done
  176.0 4.9 collective-permute-done.17.refs_1_
  182.2 11.1 %collective-permute-done.18.refs_1_ = bf16[192,1280]{1,0:T(8,128)(2,1)S(1)} collective-permute-done((bf16[192,1280]{1,0:T(8,128)(2,1)S(1)}, bf16[192,1280]{1,0:T(8,128)(2,1)S(1)}, u32[]{:S(2)}, u32[]{:S(2)}) %collective-permute-start.18) | collective-permute-done | bytes 491552 | tf_op jit(solution)/shard_map/ppermute | solution.py:395
  194.6 5.0 collective-permute-start.19
  202.6 4.9 attend.12
  208.9 5.0 attend.13
  215.2 4.0 collective-permute-done.20.refs_1_
  220.0 5.0 attend.14
  225.0 4.8 collective-permute-done.21.refs_1_
  229.9 4.7 collective-permute-start.23
  235.3 5.0 attend.15
  251.0 9.1 %feed.12 = (f32[768,1280]{1,0:T(8,128)S(1)}, bf16[768,1280]{1,0:T(8,128)(2,1)S(1)}, bf16[768,1280]{1,0:T(8,128)(2,1)S(1)}, bf16[768,1280]{1,0:T(8,128)(2,1)S(1)}...) custom-call(s32[1]{0:T(128)} %bitcast.refs_0_.edge_ref, ...), custom_call_target="tpu_custom_call" | custom-call | flops 1258291200 | bytes 6553600 | tf_op jit(solution)/shard_map/feed/pallas_call | solution.py:47
  263.8 9.2 %feed.13 = (f32[768,1280]{1,0:T(8,128)S(1)}, bf16[768,1280]{1,0:T(8,128)(2,1)S(1)}, bf16[768,1280]{1,0:T(8,128)(2,1)S(1)}, bf16[768,1280]{1,0:T(8,128)(2,1)S(1)}...) custom-call(s32[1]{0:T(128)} %bitcast.refs_0_.edge_ref, ...), custom_call_target="tpu_custom_call", output_to_operand_aliasing={{0}: (11, {}), {1}: (12, {}), {2}: (13, {}), {3}: (14, {}),... | custom-call | flops 1258291200 | bytes 6553600 | tf_op jit(solution)/shard_map/feed/pallas_call | solution.py:47
  276.7 9.2 %feed.14 = (f32[768,1280]{1,0:T(8,128)S(1)}, bf16[768,1280]{1,0:T(8,128)(2,1)S(1)}, bf16[768,1280]{1,0:T(8,128)(2,1)S(1)}, bf16[768,1280]{1,0:T(8,128)(2,1)S(1)}...) custom-call(s32[1]{0:T(128)} %bitcast.refs_0_.edge_ref, ...), custom_call_target="tpu_custom_call", output_to_operand_aliasing={{0}: (11, {}), {1}: (12, {}), {2}: (13, {}), {3}: (14, {}),... | custom-call | flops 1258291200 | bytes 6553600 | tf_op jit(solution)/shard_map/feed/pallas_call | solution.py:47
  289.3 9.2 %feed.15 = (f32[768,1280]{1,0:T(8,128)S(1)}, bf16[768,1280]{1,0:T(8,128)(2,1)S(1)}, bf16[768,1280]{1,0:T(8,128)(2,1)S(1)}, bf16[768,1280]{1,0:T(8,128)(2,1)S(1)}...) custom-call(s32[1]{0:T(128)} %bitcast.refs_0_.edge_ref, ...), custom_call_target="tpu_custom_call", output_to_operand_aliasing={{0}: (11, {}), {1}: (12, {}), {2}: (13, {}), {3}: (14, {}),... | custom-call | flops 1258291200 | bytes 6553600 | tf_op jit(solution)/shard_map/feed/pallas_call | solution.py:47
  311.9 8.7 %attend_back.4 = (bf16[768,512]{1,0:T(8,128)(2,1)S(1)}, f32[768,512]{1,0:T(8,128)S(1)}, f32[768,512]{1,0:T(8,128)S(1)}, f32[768,512]{1,0:T(8,128)S(1)}, f32[768,512]{1,0:T(8,128)S(1)}) custom-call(s32[1]{0:T(128)} %bitcast.refs_0_.edge_ref, bf16[768,512]{1,0:T(8,128)(2,1)S(1)} %copy-done.103, bf16[768,512]{1,0:T(8,128)(2,1)S(1)} %get-tuple-element.549.refs_2_, ...), custom_call_target="tpu_custom_call" | custom-call | flops 3019898880 | bytes 15728640 | tf_op jit(solution)/shard_map/attend_back/pallas_call | solution.py:656
  326.4 9.7 %collective-permute-done.37.refs_1_ = bf16[192,1280]{1,0:T(8,128)(2,1)S(1)} collective-permute-done((bf16[192,1280]{1,0:T(8,128)(2,1)S(1)}, bf16[192,1280]{1,0:T(8,128)(2,1)S(1)}, u32[]{:S(2)}, u32[]{:S(2)}) %collective-permute-start.37) | collective-permute-done | bytes 491552 | tf_op jit(solution)/shard_map/ppermute | solution.py:395
  338.5 9.5 %attend_back.5 = (bf16[768,512]{1,0:T(8,128)(2,1)S(1)}, f32[768,512]{1,0:T(8,128)S(1)}, f32[768,512]{1,0:T(8,128)S(1)}, f32[768,512]{1,0:T(8,128)S(1)}, f32[768,512]{1,0:T(8,128)S(1)}) custom-call(s32[1]{0:T(128)} %bitcast.refs_0_.edge_ref, ...), custom_call_target="tpu_custom_call", output_to_operand_aliasing={{1}: (8, {}), {2}: (9, {}), {3}: (10, {}), {4}: (11, {}), {... | custom-call | flops 3019898880 | bytes 15728640 | tf_op jit(solution)/shard_map/attend_back/pallas_call | solution.py:656
  348.5 7.2 collective-permute-start.38
  355.7 4.2 convolution_convert_fusion.3
  359.9 4.2 convolution_convert_fusion.2
  370.8 5.9 collective-permute-done.39.refs_1_
  380.2 7.0 collective-permute-done.40.refs_1_
  393.6 3.8 copy-done.1
  414.3 7.0 feed_back.4
  421.9 18.2 %collective-permute-done.44.refs_1_ = bf16[192,1280]{1,0:T(8,128)(2,1)S(1)} collective-permute-done((bf16[192,1280]{1,0:T(8,128)(2,1)S(1)}, bf16[192,1280]{1,0:T(8,128)(2,1)S(1)}, u32[]{:S(2)}, u32[]{:S(2)}) %collective-permute-start.44) | collective-permute-done | bytes 491552 | tf_op jit(solution)/shard_map/ppermute | solution.py:395
  441.1 4.2 fusion.23
  447.1 5.9 feed_back.5
  459.5 9.9 %collective-permute-start.76 = (bf16[1280,640]{0,1:T(8,128)(2,1)}, bf16[1280,640]{0,1:T(8,128)(2,1)}, u32[]{:S(2)}, u32[]{:S(2)}) collective-permute-start(bf16[1280,640]{0,1:T(8,128)(2,1)} %fusion.8), channel_id=1, source_target_pairs={{0,4},{4,0},{1,5},{5,1},{2,6},{6,2},{3,7},{7,3},{8,12},{12,8},{9,1... | collective-permute-start | bytes 4915208 | tf_op jit(solution)/shard_map/ppermute | solution.py:495
  470.7 5.9 feed_back.6
  479.6 12.9 %collective-permute-start.50 = (bf16[192,1280]{1,0:T(8,128)(2,1)S(1)}, bf16[192,1280]{1,0:T(8,128)(2,1)}, u32[]{:S(2)}, u32[]{:S(2)}) collective-permute-start(bf16[192,1280]{1,0:T(8,128)(2,1)S(1)} %get-tuple-element.628.refs_2_), channel_id=1, source_target_pairs={{0,1},{3,2},{1,0},{2,3},{4,5},{7,6},{5,4},{6,7},{8,9},{11,10},{9,8... | collective-permute-start | bytes 1474568 | tf_op jit(solution)/shard_map/ppermute | solution.py:395
  496.1 13.8 %collective-permute-start.80 = (bf16[1280,1280]{0,1:T(8,128)(2,1)}, bf16[1280,1280]{0,1:T(8,128)(2,1)}, u32[]{:S(2)}, u32[]{:S(2)}) collective-permute-start(bf16[1280,1280]{0,1:T(8,128)(2,1)} %pad_maximum_fusion.3), channel_id=1, source_target_pairs={{0,4},{4,0},{1,5},{5,1},{2,6},{6,2},{3,7},{7,3},{8,12},{12,8},{9,1... | collective-permute-start | bytes 9830408 | tf_op jit(solution)/shard_map/ppermute | solution.py:495
  513.0 5.9 feed_back.7
  532.9 5.2 collective-permute-done.52.refs_1_
  569.4 8.7 %attend_back.6 = (bf16[768,512]{1,0:T(8,128)(2,1)S(1)}, f32[768,512]{1,0:T(8,128)S(1)}, f32[768,512]{1,0:T(8,128)S(1)}, f32[768,512]{1,0:T(8,128)S(1)}, f32[768,512]{1,0:T(8,128)S(1)}) custom-call(s32[1]{0:T(128)} %bitcast.refs_0_.edge_ref, bf16[768,512]{1,0:T(8,128)(2,1)S(1)} %copy-done.108, bf16[768,512]{1,0:T(8,128)(2,1)S(1)} %copy-done.106, ...), custom_call_target="tpu_custom_call" | custom-call | flops 3019898880 | bytes 15728640 | tf_op jit(solution)/shard_map/attend_back/pallas_call | solution.py:656
  585.9 9.6 %collective-permute-done.56.refs_1_ = bf16[192,1280]{1,0:T(8,128)(2,1)S(1)} collective-permute-done((bf16[192,1280]{1,0:T(8,128)(2,1)S(1)}, bf16[192,1280]{1,0:T(8,128)(2,1)S(1)}, u32[]{:S(2)}, u32[]{:S(2)}) %collective-permute-start.56) | collective-permute-done | bytes 491552 | tf_op jit(solution)/shard_map/ppermute | solution.py:395
  596.9 9.5 %attend_back.7 = (bf16[768,512]{1,0:T(8,128)(2,1)S(1)}, f32[768,512]{1,0:T(8,128)S(1)}, f32[768,512]{1,0:T(8,128)S(1)}, f32[768,512]{1,0:T(8,128)S(1)}, f32[768,512]{1,0:T(8,128)S(1)}) custom-call(s32[1]{0:T(128)} %bitcast.refs_0_.edge_ref, ...), custom_call_target="tpu_custom_call", output_to_operand_aliasing={{1}: (8, {}), {2}: (9, {}), {3}: (10, {}), {4}: (11, {}), {... | custom-call | flops 3019898880 | bytes 15728640 | tf_op jit(solution)/shard_map/attend_back/pallas_call | solution.py:656
  611.4 4.4 maximum_add_fusion.1
  615.8 5.6 copy.183
  621.5 5.0 convolution_convert_fusion.1
  639.2 4.0 collective-permute-done.58.refs_1_
  649.7 4.0 collective-permute-done.59.refs_1_
  671.6 4.3 collective-permute-start.74
  686.5 4.0 fusion.4
  694.2 4.6 fusion.2
  701.8 4.4 maximum_add_fusion
  706.2 5.7 copy.181
  718.1 6.5 collective-permute-start.63
  760.1 4.6 collective-permute-done.67.refs_1_
  779.9 5.8 copy.172
  803.5 5.3 copy.176
  811.0 5.2 copy.175
  (806 shorter events, 378.8 us)
Async XLA Ops:
  7.2 39.8 %all-gather.4.cloned.1.call-start = ((), (), s32[]{:S(2)}) async-start(), calls=%async_computation.4 | async-start | bytes 3686400 | tf_op jit(solution)/shard_map/all_gather | solution.py:470
  11.5 94.7 %all-gather.6.cloned.1.call-start = ((), (), s32[]{:S(2)}) async-start(), calls=%async_computation.5 | async-start | bytes 7372800 | tf_op jit(solution)/shard_map/all_gather | solution.py:470
  15.6 145.3 %all-gather.8.cloned.1.call-start = ((), (), s32[]{:S(2)}) async-start(), calls=%async_computation.6 | async-start | bytes 11059200 | tf_op jit(solution)/shard_map/all_gather | solution.py:470
  18.5 675.7 %all-reduce.6.cloned.1.call-start = ((), (), s32[]{:S(2)}) async-start(), calls=%async_computation.7 | async-start | bytes 3932160 | tf_op jit(solution)/shard_map/psum | solution.py:745
  62.4 13.5 %collective-permute-start.1 = (bf16[192,1280]{1,0:T(8,128)(2,1)S(1)}, bf16[192,1280]{1,0:T(8,128)(2,1)S(1)}, u32[]{:S(2)}, u32[]{:S(2)}) collective-permute-start(bf16[192,1280]{1,0:T(8,128)(2,1)S(1)} %get-tuple-element.395.refs_0_), channel_id=1, source_target_pairs={{0,1},{3,2},{4,5},{7,6},{8,9},{11,10},{12,13},{15,14},{16,17},{19,... | collective-permute-start | bytes 1474568 | tf_op jit(solution)/shard_map/ppermute | solution.py:395
  70.5 15.9 %collective-permute-start.2 = (bf16[192,1280]{1,0:T(8,128)(2,1)S(1)}, bf16[192,1280]{1,0:T(8,128)(2,1)S(1)}, u32[]{:S(2)}, u32[]{:S(2)}) collective-permute-start(bf16[192,1280]{1,0:T(8,128)(2,1)S(1)} %get-tuple-element.400.refs_0_), channel_id=1, source_target_pairs={{0,1},{3,2},{4,5},{7,6},{8,9},{11,10},{12,13},{15,14},{16,17},{19,... | collective-permute-start | bytes 1474568 | tf_op jit(solution)/shard_map/ppermute | solution.py:395
  86.6 13.8 %collective-permute-start.4 = (bf16[192,1280]{1,0:T(8,128)(2,1)S(1)}, bf16[192,1280]{1,0:T(8,128)(2,1)S(1)}, u32[]{:S(2)}, u32[]{:S(2)}) collective-permute-start(bf16[192,1280]{1,0:T(8,128)(2,1)S(1)} %get-tuple-element.415.refs_2_), channel_id=1, source_target_pairs={{0,1},{3,2},{1,0},{2,3},{4,5},{7,6},{5,4},{6,7},{8,9},{11,10},{9,8... | collective-permute-start | bytes 1474568 | tf_op jit(solution)/shard_map/ppermute | solution.py:395
  101.4 15.9 %collective-permute-start.6 = (bf16[192,1280]{1,0:T(8,128)(2,1)}, bf16[192,1280]{1,0:T(8,128)(2,1)S(1)}, u32[]{:S(2)}, u32[]{:S(2)}) collective-permute-start(bf16[192,1280]{1,0:T(8,128)(2,1)} %get-tuple-element.421.refs_2_), channel_id=1, source_target_pairs={{0,1},{3,2},{1,0},{2,3},{4,5},{7,6},{5,4},{6,7},{8,9},{11,10},{9,8... | collective-permute-start | bytes 1474568 | tf_op jit(solution)/shard_map/ppermute | solution.py:395
  104.7 12.6 %collective-permute-start.7 = (bf16[192,1280]{1,0:T(8,128)(2,1)}, bf16[192,1280]{1,0:T(8,128)(2,1)}, u32[]{:S(2)}, u32[]{:S(2)}) collective-permute-start(bf16[192,1280]{1,0:T(8,128)(2,1)} %get-tuple-element.416.refs_2_), channel_id=1, source_target_pairs={{1,2},{2,1},{5,6},{6,5},{9,10},{10,9},{13,14},{14,13},{17,18},{18,... | collective-permute-start | bytes 1474568 | tf_op jit(solution)/shard_map/ppermute | solution.py:391
  128.8 10.6 %collective-permute-start.10 = (bf16[192,1280]{1,0:T(8,128)(2,1)S(1)}, bf16[192,1280]{1,0:T(8,128)(2,1)S(1)}, u32[]{:S(2)}, u32[]{:S(2)}) collective-permute-start(bf16[192,1280]{1,0:T(8,128)(2,1)S(1)} %get-tuple-element.439.refs_2_), channel_id=1, source_target_pairs={{0,1},{3,2},{1,0},{2,3},{4,5},{7,6},{5,4},{6,7},{8,9},{11,10},{9,8... | collective-permute-start | bytes 1474568 | tf_op jit(solution)/shard_map/ppermute | solution.py:395
  139.6 15.2 %collective-permute-start.12 = (bf16[192,1280]{1,0:T(8,128)(2,1)S(1)}, bf16[192,1280]{1,0:T(8,128)(2,1)S(1)}, u32[]{:S(2)}, u32[]{:S(2)}) collective-permute-start(bf16[192,1280]{1,0:T(8,128)(2,1)S(1)} %get-tuple-element.448.refs_2_), channel_id=1, source_target_pairs={{0,1},{3,2},{1,0},{2,3},{4,5},{7,6},{5,4},{6,7},{8,9},{11,10},{9,8... | collective-permute-start | bytes 1474568 | tf_op jit(solution)/shard_map/ppermute | solution.py:395
  142.8 12.0 %collective-permute-start.13 = (bf16[192,1280]{1,0:T(8,128)(2,1)S(1)}, bf16[192,1280]{1,0:T(8,128)(2,1)S(1)}, u32[]{:S(2)}, u32[]{:S(2)}) collective-permute-start(bf16[192,1280]{1,0:T(8,128)(2,1)S(1)} %get-tuple-element.440.refs_2_), channel_id=1, source_target_pairs={{1,2},{2,1},{5,6},{6,5},{9,10},{10,9},{13,14},{14,13},{17,18},{18,... | collective-permute-start | bytes 1474568 | tf_op jit(solution)/shard_map/ppermute | solution.py:391
  155.8 12.2 %collective-permute-start.14 = (bf16[192,1280]{1,0:T(8,128)(2,1)}, bf16[192,1280]{1,0:T(8,128)(2,1)S(1)}, u32[]{:S(2)}, u32[]{:S(2)}) collective-permute-start(bf16[192,1280]{1,0:T(8,128)(2,1)} %get-tuple-element.454.refs_2_), channel_id=1, source_target_pairs={{0,1},{3,2},{1,0},{2,3},{4,5},{7,6},{5,4},{6,7},{8,9},{11,10},{9,8... | collective-permute-start | bytes 1474568 | tf_op jit(solution)/shard_map/ppermute | solution.py:395
  170.2 10.7 %collective-permute-start.17 = (bf16[192,1280]{1,0:T(8,128)(2,1)S(1)}, bf16[192,1280]{1,0:T(8,128)(2,1)S(1)}, u32[]{:S(2)}, u32[]{:S(2)}) collective-permute-start(bf16[192,1280]{1,0:T(8,128)(2,1)S(1)} %get-tuple-element.463.refs_2_), channel_id=1, source_target_pairs={{1,0},{2,3},{5,4},{6,7},{9,8},{10,11},{13,12},{14,15},{17,16},{18,... | collective-permute-start | bytes 1474568 | tf_op jit(solution)/shard_map/ppermute | solution.py:395
  174.1 19.1 %collective-permute-start.18 = (bf16[192,1280]{1,0:T(8,128)(2,1)S(1)}, bf16[192,1280]{1,0:T(8,128)(2,1)S(1)}, u32[]{:S(2)}, u32[]{:S(2)}) collective-permute-start(bf16[192,1280]{1,0:T(8,128)(2,1)S(1)} %turn.40.refs_2_), channel_id=1, source_target_pairs={{1,0},{2,3},{5,4},{6,7},{9,8},{10,11},{13,12},{14,15},{17,16},{18,... | collective-permute-start | bytes 1474568 | tf_op jit(solution)/shard_map/ppermute | solution.py:395
  207.6 11.6 %collective-permute-start.20 = (bf16[192,1280]{1,0:T(8,128)(2,1)S(1)}, bf16[192,1280]{1,0:T(8,128)(2,1)S(1)}, u32[]{:S(2)}, u32[]{:S(2)}) collective-permute-start(bf16[192,1280]{1,0:T(8,128)(2,1)S(1)} %get-tuple-element.475.refs_0_), channel_id=1, source_target_pairs={{0,1},{3,2},{4,5},{7,6},{8,9},{11,10},{12,13},{15,14},{16,17},{19,... | collective-permute-start | bytes 1474568 | tf_op jit(solution)/shard_map/ppermute | solution.py:395
  213.9 15.9 %collective-permute-start.21 = (bf16[192,1280]{1,0:T(8,128)(2,1)S(1)}, bf16[192,1280]{1,0:T(8,128)(2,1)S(1)}, u32[]{:S(2)}, u32[]{:S(2)}) collective-permute-start(bf16[192,1280]{1,0:T(8,128)(2,1)S(1)} %get-tuple-element.480.refs_0_), channel_id=1, source_target_pairs={{0,1},{3,2},{4,5},{7,6},{8,9},{11,10},{12,13},{15,14},{16,17},{19,... | collective-permute-start | bytes 1474568 | tf_op jit(solution)/shard_map/ppermute | solution.py:395
  229.9 13.5 %collective-permute-start.23 = (bf16[192,1280]{1,0:T(8,128)(2,1)S(1)}, bf16[192,1280]{1,0:T(8,128)(2,1)S(1)}, u32[]{:S(2)}, u32[]{:S(2)}) collective-permute-start(bf16[192,1280]{1,0:T(8,128)(2,1)S(1)} %get-tuple-element.495.refs_2_), channel_id=1, source_target_pairs={{0,1},{3,2},{1,0},{2,3},{4,5},{7,6},{5,4},{6,7},{8,9},{11,10},{9,8... | collective-permute-start | bytes 1474568 | tf_op jit(solution)/shard_map/ppermute | solution.py:395
  243.6 17.1 %collective-permute-start.25 = (bf16[192,1280]{1,0:T(8,128)(2,1)S(1)}, bf16[192,1280]{1,0:T(8,128)(2,1)S(1)}, u32[]{:S(2)}, u32[]{:S(2)}) collective-permute-start(bf16[192,1280]{1,0:T(8,128)(2,1)S(1)} %get-tuple-element.501.refs_2_), channel_id=1, source_target_pairs={{0,1},{3,2},{1,0},{2,3},{4,5},{7,6},{5,4},{6,7},{8,9},{11,10},{9,8... | collective-permute-start | bytes 1474568 | tf_op jit(solution)/shard_map/ppermute | solution.py:395
  246.8 14.0 %collective-permute-start.26 = (bf16[192,1280]{1,0:T(8,128)(2,1)S(1)}, bf16[192,1280]{1,0:T(8,128)(2,1)S(1)}, u32[]{:S(2)}, u32[]{:S(2)}) collective-permute-start(bf16[192,1280]{1,0:T(8,128)(2,1)S(1)} %get-tuple-element.496.refs_2_), channel_id=1, source_target_pairs={{1,2},{2,1},{5,6},{6,5},{9,10},{10,9},{13,14},{14,13},{17,18},{18,... | collective-permute-start | bytes 1474568 | tf_op jit(solution)/shard_map/ppermute | solution.py:391
  261.0 12.6 %collective-permute-start.27 = (bf16[192,1280]{1,0:T(8,128)(2,1)S(1)}, bf16[192,1280]{1,0:T(8,128)(2,1)S(1)}, u32[]{:S(2)}, u32[]{:S(2)}) collective-permute-start(bf16[192,1280]{1,0:T(8,128)(2,1)S(1)} %get-tuple-element.512.refs_2_), channel_id=1, source_target_pairs={{0,1},{3,2},{1,0},{2,3},{4,5},{7,6},{5,4},{6,7},{8,9},{11,10},{9,8... | collective-permute-start | bytes 1474568 | tf_op jit(solution)/shard_map/ppermute | solution.py:395
  262.9 10.7 %collective-permute-start.28 = (bf16[192,1280]{1,0:T(8,128)(2,1)S(1)}, bf16[192,1280]{1,0:T(8,128)(2,1)S(1)}, u32[]{:S(2)}, u32[]{:S(2)}) collective-permute-start(bf16[192,1280]{1,0:T(8,128)(2,1)S(1)} %get-tuple-element.502.refs_2_), channel_id=1, source_target_pairs={{1,2},{2,1},{5,6},{6,5},{9,10},{10,9},{13,14},{14,13},{17,18},{18,... | collective-permute-start | bytes 1474568 | tf_op jit(solution)/shard_map/ppermute | solution.py:391
  273.8 12.7 %collective-permute-start.29 = (bf16[192,1280]{1,0:T(8,128)(2,1)S(1)}, bf16[192,1280]{1,0:T(8,128)(2,1)S(1)}, u32[]{:S(2)}, u32[]{:S(2)}) collective-permute-start(bf16[192,1280]{1,0:T(8,128)(2,1)S(1)} %get-tuple-element.523.refs_2_), channel_id=1, source_target_pairs={{0,1},{3,2},{1,0},{2,3},{4,5},{7,6},{5,4},{6,7},{8,9},{11,10},{9,8... | collective-permute-start | bytes 1474568 | tf_op jit(solution)/shard_map/ppermute | solution.py:395
  286.7 11.9 %collective-permute-start.31 = (bf16[192,1280]{1,0:T(8,128)(2,1)S(1)}, bf16[192,1280]{1,0:T(8,128)(2,1)S(1)}, u32[]{:S(2)}, u32[]{:S(2)}) collective-permute-start(bf16[192,1280]{1,0:T(8,128)(2,1)S(1)} %get-tuple-element.536.refs_2_), channel_id=1, source_target_pairs={{0,1},{3,2},{1,0},{2,3},{4,5},{7,6},{5,4},{6,7},{8,9},{11,10},{9,8... | collective-permute-start | bytes 1474568 | tf_op jit(solution)/shard_map/ppermute | solution.py:395
  307.9 12.6 %collective-permute-start.35 = (bf16[192,1280]{1,0:T(8,128)(2,1)S(1)}, bf16[192,1280]{1,0:T(8,128)(2,1)S(1)}, u32[]{:S(2)}, u32[]{:S(2)}) collective-permute-start(bf16[192,1280]{1,0:T(8,128)(2,1)S(1)} %get-tuple-element.542.refs_0_), channel_id=1, source_target_pairs={{1,2},{2,1},{5,6},{6,5},{9,10},{10,9},{13,14},{14,13},{17,18},{18,... | collective-permute-start | bytes 1474568 | tf_op jit(solution)/shard_map/ppermute | solution.py:391
  310.6 14.4 %collective-permute-start.36 = (bf16[192,1280]{1,0:T(8,128)(2,1)S(1)}, bf16[192,1280]{1,0:T(8,128)(2,1)S(1)}, u32[]{:S(2)}, u32[]{:S(2)}) collective-permute-start(bf16[192,1280]{1,0:T(8,128)(2,1)S(1)} %get-tuple-element.553.refs_2_), channel_id=1, source_target_pairs={{1,0},{2,3},{5,4},{6,7},{9,8},{10,11},{13,12},{14,15},{17,16},{18,... | collective-permute-start | bytes 1474568 | tf_op jit(solution)/shard_map/ppermute | solution.py:395
  323.5 12.6 %collective-permute-start.37 = (bf16[192,1280]{1,0:T(8,128)(2,1)S(1)}, bf16[192,1280]{1,0:T(8,128)(2,1)S(1)}, u32[]{:S(2)}, u32[]{:S(2)}) collective-permute-start(bf16[192,1280]{1,0:T(8,128)(2,1)S(1)} %turn.49.refs_2_), channel_id=1, source_target_pairs={{1,0},{2,3},{5,4},{6,7},{9,8},{10,11},{13,12},{14,15},{17,16},{18,... | collective-permute-start | bytes 1474568 | tf_op jit(solution)/shard_map/ppermute | solution.py:395
  348.5 15.6 %collective-permute-start.38 = (bf16[2,768,512]{2,1,0:T(8,128)(2,1)S(1)}, bf16[2,768,512]{2,1,0:T(8,128)(2,1)S(1)}, u32[]{:S(2)}, u32[]{:S(2)}) collective-permute-start(bf16[2,768,512]{2,1,0:T(8,128)(2,1)S(1)} %pad_maximum_fusion.4), channel_id=1, source_target_pairs={{0,4},{4,0},{1,5},{5,1},{2,6},{6,2},{3,7},{7,3},{8,12},{12,8},{9,1... | collective-permute-start | bytes 4718600 | tf_op jit(solution)/shard_map/ppermute | solution.py:674
  366.1 10.6 %collective-permute-start.39 = (bf16[192,1280]{1,0:T(8,128)(2,1)S(1)}, bf16[192,1280]{1,0:T(8,128)(2,1)S(1)}, u32[]{:S(2)}, u32[]{:S(2)}) collective-permute-start(bf16[192,1280]{1,0:T(8,128)(2,1)S(1)} %get-tuple-element.581.refs_0_), channel_id=1, source_target_pairs={{0,1},{3,2},{4,5},{7,6},{8,9},{11,10},{12,13},{15,14},{16,17},{19,... | collective-permute-start | bytes 1474568 | tf_op jit(solution)/shard_map/ppermute | solution.py:395
  369.5 17.8 %collective-permute-start.40 = (bf16[192,1280]{1,0:T(8,128)(2,1)S(1)}, bf16[192,1280]{1,0:T(8,128)(2,1)S(1)}, u32[]{:S(2)}, u32[]{:S(2)}) collective-permute-start(bf16[192,1280]{1,0:T(8,128)(2,1)S(1)} %get-tuple-element.584.refs_0_), channel_id=1, source_target_pairs={{0,1},{3,2},{4,5},{7,6},{8,9},{11,10},{12,13},{15,14},{16,17},{19,... | collective-permute-start | bytes 1474568 | tf_op jit(solution)/shard_map/ppermute | solution.py:395
  389.1 14.4 %collective-permute-start.42 = (bf16[192,1280]{1,0:T(8,128)(2,1)}, bf16[192,1280]{1,0:T(8,128)(2,1)}, u32[]{:S(2)}, u32[]{:S(2)}) collective-permute-start(bf16[192,1280]{1,0:T(8,128)(2,1)} %get-tuple-element.595.refs_2_), channel_id=1, source_target_pairs={{0,1},{3,2},{1,0},{2,3},{4,5},{7,6},{5,4},{6,7},{8,9},{11,10},{9,8... | collective-permute-start | bytes 1474568 | tf_op jit(solution)/shard_map/ppermute | solution.py:395
  391.6 11.9 %collective-permute-start.43 = (bf16[192,1280]{1,0:T(8,128)(2,1)}, bf16[192,1280]{1,0:T(8,128)(2,1)}, u32[]{:S(2)}, u32[]{:S(2)}) collective-permute-start(bf16[192,1280]{1,0:T(8,128)(2,1)} %get-tuple-element.590.refs_2_), channel_id=1, source_target_pairs={{1,2},{2,1},{5,6},{6,5},{9,10},{10,9},{13,14},{14,13},{17,18},{18,... | collective-permute-start | bytes 1474568 | tf_op jit(solution)/shard_map/ppermute | solution.py:391
  393.5 320.4 %reduce-scatter.15.cloned.1.call-start = ((), (), s32[]{:S(2)}) async-start(), calls=%async_computation.9 | async-start | bytes 2048000
  405.3 34.8 %collective-permute-start.44 = (bf16[192,1280]{1,0:T(8,128)(2,1)S(1)}, bf16[192,1280]{1,0:T(8,128)(2,1)S(1)}, u32[]{:S(2)}, u32[]{:S(2)}) collective-permute-start(bf16[192,1280]{1,0:T(8,128)(2,1)S(1)} %get-tuple-element.604.refs_2_), channel_id=1, source_target_pairs={{0,1},{3,2},{1,0},{2,3},{4,5},{7,6},{5,4},{6,7},{8,9},{11,10},{9,8... | collective-permute-start | bytes 1474568 | tf_op jit(solution)/shard_map/ppermute | solution.py:395
  406.7 33.4 %collective-permute-start.45 = (bf16[192,1280]{1,0:T(8,128)(2,1)S(1)}, bf16[192,1280]{1,0:T(8,128)(2,1)S(1)}, u32[]{:S(2)}, u32[]{:S(2)}) collective-permute-start(bf16[192,1280]{1,0:T(8,128)(2,1)S(1)} %get-tuple-element.596.refs_2_), channel_id=1, source_target_pairs={{1,2},{2,1},{5,6},{6,5},{9,10},{10,9},{13,14},{14,13},{17,18},{18,... | collective-permute-start | bytes 1474568 | tf_op jit(solution)/shard_map/ppermute | solution.py:391
  440.3 12.8 %collective-permute-start.46 = (bf16[192,1280]{1,0:T(8,128)(2,1)S(1)}, bf16[192,1280]{1,0:T(8,128)(2,1)S(1)}, u32[]{:S(2)}, u32[]{:S(2)}) collective-permute-start(bf16[192,1280]{1,0:T(8,128)(2,1)S(1)} %get-tuple-element.612.refs_2_), channel_id=1, source_target_pairs={{0,1},{3,2},{1,0},{2,3},{4,5},{7,6},{5,4},{6,7},{8,9},{11,10},{9,8... | collective-permute-start | bytes 1474568 | tf_op jit(solution)/shard_map/ppermute | solution.py:395
  440.4 12.7 %collective-permute-start.47 = (bf16[192,1280]{1,0:T(8,128)(2,1)S(1)}, bf16[192,1280]{1,0:T(8,128)(2,1)S(1)}, u32[]{:S(2)}, u32[]{:S(2)}) collective-permute-start(bf16[192,1280]{1,0:T(8,128)(2,1)S(1)} %get-tuple-element.605.refs_2_), channel_id=1, source_target_pairs={{1,2},{2,1},{5,6},{6,5},{9,10},{10,9},{13,14},{14,13},{17,18},{18,... | collective-permute-start | bytes 1474568 | tf_op jit(solution)/shard_map/ppermute | solution.py:391
  453.3 24.6 %collective-permute-start.48 = (bf16[192,1280]{1,0:T(8,128)(2,1)S(1)}, bf16[192,1280]{1,0:T(8,128)(2,1)S(1)}, u32[]{:S(2)}, u32[]{:S(2)}) collective-permute-start(bf16[192,1280]{1,0:T(8,128)(2,1)S(1)} %get-tuple-element.620.refs_2_), channel_id=1, source_target_pairs={{0,1},{3,2},{1,0},{2,3},{4,5},{7,6},{5,4},{6,7},{8,9},{11,10},{9,8... | collective-permute-start | bytes 1474568 | tf_op jit(solution)/shard_map/ppermute | solution.py:395
  456.6 21.3 %collective-permute-start.49 = (bf16[192,1280]{1,0:T(8,128)(2,1)S(1)}, bf16[192,1280]{1,0:T(8,128)(2,1)S(1)}, u32[]{:S(2)}, u32[]{:S(2)}) collective-permute-start(bf16[192,1280]{1,0:T(8,128)(2,1)S(1)} %get-tuple-element.613.refs_2_), channel_id=1, source_target_pairs={{1,2},{2,1},{5,6},{6,5},{9,10},{10,9},{13,14},{14,13},{17,18},{18,... | collective-permute-start | bytes 1474568 | tf_op jit(solution)/shard_map/ppermute | solution.py:391
  459.5 82.5 %collective-permute-start.76 = (bf16[1280,640]{0,1:T(8,128)(2,1)}, bf16[1280,640]{0,1:T(8,128)(2,1)}, u32[]{:S(2)}, u32[]{:S(2)}) collective-permute-start(bf16[1280,640]{0,1:T(8,128)(2,1)} %fusion.8), channel_id=1, source_target_pairs={{0,4},{4,0},{1,5},{5,1},{2,6},{6,2},{3,7},{7,3},{8,12},{12,8},{9,1... | collective-permute-start | bytes 4915208 | tf_op jit(solution)/shard_map/ppermute | solution.py:495
  479.6 42.5 %collective-permute-start.50 = (bf16[192,1280]{1,0:T(8,128)(2,1)S(1)}, bf16[192,1280]{1,0:T(8,128)(2,1)}, u32[]{:S(2)}, u32[]{:S(2)}) collective-permute-start(bf16[192,1280]{1,0:T(8,128)(2,1)S(1)} %get-tuple-element.628.refs_2_), channel_id=1, source_target_pairs={{0,1},{3,2},{1,0},{2,3},{4,5},{7,6},{5,4},{6,7},{8,9},{11,10},{9,8... | collective-permute-start | bytes 1474568 | tf_op jit(solution)/shard_map/ppermute | solution.py:395
  492.5 29.6 %collective-permute-start.51 = (bf16[192,1280]{1,0:T(8,128)(2,1)}, bf16[192,1280]{1,0:T(8,128)(2,1)}, u32[]{:S(2)}, u32[]{:S(2)}) collective-permute-start(bf16[192,1280]{1,0:T(8,128)(2,1)} %get-tuple-element.621.refs_2_), channel_id=1, source_target_pairs={{1,2},{2,1},{5,6},{6,5},{9,10},{10,9},{13,14},{14,13},{17,18},{18,... | collective-permute-start | bytes 1474568 | tf_op jit(solution)/shard_map/ppermute | solution.py:391
  496.1 115.3 %collective-permute-start.80 = (bf16[1280,1280]{0,1:T(8,128)(2,1)}, bf16[1280,1280]{0,1:T(8,128)(2,1)}, u32[]{:S(2)}, u32[]{:S(2)}) collective-permute-start(bf16[1280,1280]{0,1:T(8,128)(2,1)} %pad_maximum_fusion.3), channel_id=1, source_target_pairs={{0,4},{4,0},{1,5},{5,1},{2,6},{6,2},{3,7},{7,3},{8,12},{12,8},{9,1... | collective-permute-start | bytes 9830408 | tf_op jit(solution)/shard_map/ppermute | solution.py:495
  525.2 12.9 %collective-permute-start.52 = (bf16[192,1280]{1,0:T(8,128)(2,1)S(1)}, bf16[192,1280]{1,0:T(8,128)(2,1)S(1)}, u32[]{:S(2)}, u32[]{:S(2)}) collective-permute-start(bf16[192,1280]{1,0:T(8,128)(2,1)S(1)} %get-tuple-element.634.refs_2_), channel_id=1, source_target_pairs={{0,1},{3,2},{1,0},{2,3},{4,5},{7,6},{5,4},{6,7},{8,9},{11,10},{9,8... | collective-permute-start | bytes 1474568 | tf_op jit(solution)/shard_map/ppermute | solution.py:395
  525.4 12.6 %collective-permute-start.53 = (bf16[192,1280]{1,0:T(8,128)(2,1)S(1)}, bf16[192,1280]{1,0:T(8,128)(2,1)S(1)}, u32[]{:S(2)}, u32[]{:S(2)}) collective-permute-start(bf16[192,1280]{1,0:T(8,128)(2,1)S(1)} %get-tuple-element.629.refs_2_), channel_id=1, source_target_pairs={{1,2},{2,1},{5,6},{6,5},{9,10},{10,9},{13,14},{14,13},{17,18},{18,... | collective-permute-start | bytes 1474568 | tf_op jit(solution)/shard_map/ppermute | solution.py:391
  540.5 37.5 %collective-permute-start.54 = (bf16[192,1280]{1,0:T(8,128)(2,1)}, bf16[192,1280]{1,0:T(8,128)(2,1)}, u32[]{:S(2)}, u32[]{:S(2)}) collective-permute-start(bf16[192,1280]{1,0:T(8,128)(2,1)} %get-tuple-element.635.refs_0_), channel_id=1, source_target_pairs={{1,2},{2,1},{5,6},{6,5},{9,10},{10,9},{13,14},{14,13},{17,18},{18,... | collective-permute-start | bytes 1474568 | tf_op jit(solution)/shard_map/ppermute | solution.py:391
  549.3 176.6 %reduce-scatter.19.cloned.1.call-start = ((), (), s32[]{:S(2)}) async-start(), calls=%async_computation.11 | async-start | bytes 4096000 | tf_op jit(solution)/shard_map/reduce_scatter | solution.py:496
  566.9 16.1 %collective-permute-start.55 = (bf16[192,1280]{1,0:T(8,128)(2,1)S(1)}, bf16[192,1280]{1,0:T(8,128)(2,1)S(1)}, u32[]{:S(2)}, u32[]{:S(2)}) collective-permute-start(bf16[192,1280]{1,0:T(8,128)(2,1)S(1)} %copy-done.128), channel_id=1, source_target_pairs={{1,0},{2,3},{5,4},{6,7},{9,8},{10,11},{13,12},{14,15},{17,16},{18,... | collective-permute-start | bytes 1474568 | tf_op jit(solution)/shard_map/ppermute | solution.py:395
  579.4 16.1 %collective-permute-start.56 = (bf16[192,1280]{1,0:T(8,128)(2,1)S(1)}, bf16[192,1280]{1,0:T(8,128)(2,1)S(1)}, u32[]{:S(2)}, u32[]{:S(2)}) collective-permute-start(bf16[192,1280]{1,0:T(8,128)(2,1)S(1)} %turn.58.refs_2_), channel_id=1, source_target_pairs={{1,0},{2,3},{5,4},{6,7},{9,8},{10,11},{13,12},{14,15},{17,16},{18,... | collective-permute-start | bytes 1474568 | tf_op jit(solution)/shard_map/ppermute | solution.py:395
  609.6 20.1 %collective-permute-start.57 = (bf16[2,768,512]{2,1,0:T(8,128)(2,1)}, bf16[2,768,512]{2,1,0:T(8,128)(2,1)}, u32[]{:S(2)}, u32[]{:S(2)}) collective-permute-start(bf16[2,768,512]{2,1,0:T(8,128)(2,1)} %pad_maximum_fusion.5), channel_id=1, source_target_pairs={{0,4},{4,0},{1,5},{5,1},{2,6},{6,2},{3,7},{7,3},{8,12},{12,8},{9,1... | collective-permute-start | bytes 4718600 | tf_op jit(solution)/shard_map/ppermute | solution.py:674
  621.5 167.0 %reduce-scatter.13.cloned.1.call-start = ((), (), s32[]{:S(2)}) async-start(), calls=%async_computation.8 | async-start | bytes 2048000
  632.2 11.0 %collective-permute-start.58 = (bf16[192,1280]{1,0:T(8,128)(2,1)S(1)}, bf16[192,1280]{1,0:T(8,128)(2,1)S(1)}, u32[]{:S(2)}, u32[]{:S(2)}) collective-permute-start(bf16[192,1280]{1,0:T(8,128)(2,1)S(1)} %get-tuple-element.674.refs_0_), channel_id=1, source_target_pairs={{0,1},{3,2},{4,5},{7,6},{8,9},{11,10},{12,13},{15,14},{16,17},{19,... | collective-permute-start | bytes 1474568 | tf_op jit(solution)/shard_map/ppermute | solution.py:395
  637.9 15.8 %collective-permute-start.59 = (bf16[192,1280]{1,0:T(8,128)(2,1)S(1)}, bf16[192,1280]{1,0:T(8,128)(2,1)S(1)}, u32[]{:S(2)}, u32[]{:S(2)}) collective-permute-start(bf16[192,1280]{1,0:T(8,128)(2,1)S(1)} %get-tuple-element.677.refs_0_), channel_id=1, source_target_pairs={{0,1},{3,2},{4,5},{7,6},{8,9},{11,10},{12,13},{15,14},{16,17},{19,... | collective-permute-start | bytes 1474568 | tf_op jit(solution)/shard_map/ppermute | solution.py:395
  653.9 11.5 %collective-permute-start.61 = (bf16[192,1280]{1,0:T(8,128)(2,1)S(1)}, bf16[192,1280]{1,0:T(8,128)(2,1)S(1)}, u32[]{:S(2)}, u32[]{:S(2)}) collective-permute-start(bf16[192,1280]{1,0:T(8,128)(2,1)S(1)} %get-tuple-element.688.refs_2_), channel_id=1, source_target_pairs={{0,1},{3,2},{1,0},{2,3},{4,5},{7,6},{5,4},{6,7},{8,9},{11,10},{9,8... | collective-permute-start | bytes 1474568 | tf_op jit(solution)/shard_map/ppermute | solution.py:395
  671.6 14.9 %collective-permute-start.74 = (bf16[1280,640]{0,1:T(8,128)(2,1)}, bf16[1280,640]{0,1:T(8,128)(2,1)}, u32[]{:S(2)}, u32[]{:S(2)}) collective-permute-start(bf16[1280,640]{0,1:T(8,128)(2,1)} %fusion.5), channel_id=1, source_target_pairs={{0,4},{4,0},{1,5},{5,1},{2,6},{6,2},{3,7},{7,3},{8,12},{12,8},{9,1... | collective-permute-start | bytes 4915208 | tf_op jit(solution)/shard_map/ppermute | solution.py:495
  677.9 23.9 %collective-permute-start.78 = (bf16[1280,1280]{0,1:T(8,128)(2,1)}, bf16[1280,1280]{0,1:T(8,128)(2,1)}, u32[]{:S(2)}, u32[]{:S(2)}) collective-permute-start(bf16[1280,1280]{0,1:T(8,128)(2,1)} %pad_maximum_fusion.2), channel_id=1, source_target_pairs={{0,4},{4,0},{1,5},{5,1},{2,6},{6,2},{3,7},{7,3},{8,12},{12,8},{9,1... | collective-permute-start | bytes 9830408 | tf_op jit(solution)/shard_map/ppermute | solution.py:495
  683.8 14.9 %collective-permute-start.72 = (f32[80,128]{1,0:T(8,128)S(1)}, f32[80,128]{1,0:T(8,128)S(1)}, u32[]{:S(2)}, u32[]{:S(2)}) collective-permute-start(f32[80,128]{1,0:T(8,128)S(1)} %fusion.13), channel_id=1, source_target_pairs={{0,8},{8,0},{16,24},{24,16},{1,9},{9,1},{17,25},{25,17},{2,10},{10... | collective-permute-start | bytes 122888 | tf_op jit(solution)/shard_map/ppermute | solution.py:408
  694.1 97.5 %reduce-scatter.17.cloned.1.call-start = ((), (), s32[]{:S(2)}) async-start(), calls=%async_computation.10 | async-start | bytes 4096000 | tf_op jit(solution)/shard_map/reduce_scatter | solution.py:496
  717.4 18.6 %collective-permute-start.64 = (bf16[192,1280]{1,0:T(8,128)(2,1)S(1)}, bf16[192,1280]{1,0:T(8,128)(2,1)S(1)}, u32[]{:S(2)}, u32[]{:S(2)}) collective-permute-start(bf16[192,1280]{1,0:T(8,128)(2,1)S(1)} %get-tuple-element.689.refs_2_), channel_id=1, source_target_pairs={{1,2},{2,1},{5,6},{6,5},{9,10},{10,9},{13,14},{14,13},{17,18},{18,... | collective-permute-start | bytes 1474568 | tf_op jit(solution)/shard_map/ppermute | solution.py:391
  718.1 17.9 %collective-permute-start.63 = (bf16[192,1280]{1,0:T(8,128)(2,1)S(1)}, bf16[192,1280]{1,0:T(8,128)(2,1)S(1)}, u32[]{:S(2)}, u32[]{:S(2)}) collective-permute-start(bf16[192,1280]{1,0:T(8,128)(2,1)S(1)} %get-tuple-element.696.refs_2_), channel_id=1, source_target_pairs={{0,1},{3,2},{1,0},{2,3},{4,5},{7,6},{5,4},{6,7},{8,9},{11,10},{9,8... | collective-permute-start | bytes 1474568 | tf_op jit(solution)/shard_map/ppermute | solution.py:395
  725.8 29.1 %collective-permute-start.81 = (bf16[320,1280]{1,0:T(8,128)(2,1)}, bf16[320,1280]{1,0:T(8,128)(2,1)}, u32[]{:S(2)}, u32[]{:S(2)}) collective-permute-start(bf16[320,1280]{1,0:T(8,128)(2,1)} %reduce-scatter.19.cloned.1.call-done), channel_id=1, source_target_pairs={{0,4},{4,0},{1,5},{5,1},{2,6},{6,2},{3,7},{7,3},{8,12},{12,8},{9,1... | collective-permute-start | bytes 2457608 | tf_op jit(solution)/shard_map/ppermute | solution.py:497
  736.1 15.4 %collective-permute-start.66 = (bf16[192,1280]{1,0:T(8,128)(2,1)S(1)}, bf16[192,1280]{1,0:T(8,128)(2,1)S(1)}, u32[]{:S(2)}, u32[]{:S(2)}) collective-permute-start(bf16[192,1280]{1,0:T(8,128)(2,1)S(1)} %get-tuple-element.702.refs_2_), channel_id=1, source_target_pairs={{1,0},{2,3},{5,4},{6,7},{9,8},{10,11},{13,12},{14,15},{17,16},{18,... | collective-permute-start | bytes 1474568 | tf_op jit(solution)/shard_map/ppermute | solution.py:395
  737.4 12.2 %collective-permute-start.65 = (bf16[192,1280]{1,0:T(8,128)(2,1)S(1)}, bf16[192,1280]{1,0:T(8,128)(2,1)S(1)}, u32[]{:S(2)}, u32[]{:S(2)}) collective-permute-start(bf16[192,1280]{1,0:T(8,128)(2,1)S(1)} %get-tuple-element.697.refs_0_), channel_id=1, source_target_pairs={{1,2},{2,1},{5,6},{6,5},{9,10},{10,9},{13,14},{14,13},{17,18},{18,... | collective-permute-start | bytes 1474568 | tf_op jit(solution)/shard_map/ppermute | solution.py:391
  749.7 15.0 %collective-permute-start.67 = (bf16[192,1280]{1,0:T(8,128)(2,1)S(1)}, bf16[192,1280]{1,0:T(8,128)(2,1)S(1)}, u32[]{:S(2)}, u32[]{:S(2)}) collective-permute-start(bf16[192,1280]{1,0:T(8,128)(2,1)S(1)} %turn.63.refs_2_), channel_id=1, source_target_pairs={{1,0},{2,3},{5,4},{6,7},{9,8},{10,11},{13,12},{14,15},{17,16},{18,... | collective-permute-start | bytes 1474568 | tf_op jit(solution)/shard_map/ppermute | solution.py:395
  (249 other events, 1740.7 us)
Sparse Core Ops, SparseCore 0:
  11.6 35.3 all-gather.3
  49.4 46.6 all-gather.5
  98.6 60.4 all-gather.7
  393.7 111.3 all-reduce.5
  549.4 34.6 reduce-scatter.14
  621.6 44.9 reduce-scatter.18
  694.2 31.1 reduce-scatter.12
  728.5 45.0 reduce-scatter.16

commit v3 on v2

--- a/solution.py
+++ b/solution.py
@@ -5,6 +5,7 @@
 import numpy as np
 from jax import lax
 from jax.experimental import pallas as pl
+from jax.experimental.layout import Layout, with_layout_constraint
 from jax.experimental.pallas import tpu as pltpu
 from jax.sharding import PartitionSpec as P
 
@@ -22,6 +23,7 @@
 NN = (((1,), (0,)), ((), ()))
 MIB = 1024 * 1024
 LIMIT = 20
+COST = 0.1
 
 
 def mm(a, b, dims=NN):
@@ -53,7 +55,7 @@
         scratch_shapes=list(scratch),
         input_output_aliases={live + k: n for k, (n, _) in enumerate(olds)},
         compiler_params=pltpu.CompilerParams(vmem_limit_bytes=limit * MIB),
-        cost_estimate=pl.CostEstimate(flops=int(flops), bytes_accessed=int(moved), transcendentals=0),
+        cost_estimate=pl.CostEstimate(flops=int(flops * COST), bytes_accessed=int(moved * COST), transcendentals=0),
         name=name,
     )(*[a for a, _ in ins], *[o for _, o in olds])
 
@@ -70,8 +72,8 @@
     return centred * r, r
 
 
-def norm_back(v, gain, dn):
-    xhat, r = norm_stats(v)
+def norm_back(x_ref, r_ref, gain, dn):
+    xhat, r = x_ref[...].astype(F32), r_ref[:, :1]
     dx = dn * gain
     back = r * (dx - jnp.mean(dx, axis=-1, keepdims=True) - xhat * jnp.mean(dx * xhat, axis=-1, keepdims=True))
     return back, dn * xhat
@@ -91,21 +93,34 @@
     return jnp.sum(v, axis=0, keepdims=True)
 
 
-def store_sums(ref, *values):
-    ref[...] = jnp.zeros_like(ref)
+def keep_norm(xhat, r, x_ref, r_ref):
+    x_ref[...] = xhat.astype(BF)
+    r_ref[...] = jnp.broadcast_to(r, r_ref.shape)
+
+
+def add_sums(ref, at, *values):
     for n, v in enumerate(values):
-        ref[0, n : n + 1, :] = v
+        ref[at + n : at + n + 1, : v.shape[1]] += v
+
+
+NORM1_ROW, NORM2_ROW, OUT_ROW, DOWN_ROW, MIXED_ROW, UP_ROW = 0, 2, 4, 5, 6, 7
+
+
+def add_unit_sums(ref, tile, d):
+    n = d.shape[1]
+    ref[UP_ROW : UP_ROW + 1, pl.ds(pl.multiple_of(tile * n, n), n)] += rows_sum(d.astype(F32))
 
 
 def project_kernel(
     first, local, edge_ref, got_ref, part_ref, base_ref, add_ref, gain_ref, shift_ref, w_ref, bias_ref, spread_ref,
-    ke_ref, qe_ref, ve_ref, h_ref, n_ref, q_ref, kv_ref,
+    ke_ref, qe_ref, ve_ref, h_ref, x_ref, r_ref, n_ref, q_ref, kv_ref,
 ):
     h = base_ref[...].astype(F32)
     if not first:
         h = h + summed(edge_ref, got_ref, part_ref) + add_ref[...]
     h_ref[...] = h
-    xhat, _ = norm_stats(h)
+    xhat, r = norm_stats(h)
+    keep_norm(xhat, r, x_ref, r_ref)
     n = (xhat * gain_ref[...] + shift_ref[...]).astype(BF)
     n_ref[...] = n
     m = (mm(n, w_ref[...]) + bias_ref[...]).astype(BF)
@@ -162,26 +177,27 @@
     back, tiles, edge_ref, got_ref, part_ref, h_ref, add_ref, gain_ref, shift_ref, up_ref, bias_ref, down_ref, *refs
 ):
     if back:
-        (g_ref, mid_ref, n_ref, act_ref, low_ref, d_ref, out_ref, back_ref, sum_ref, usum_ref,
+        (g_ref, old_ref, mid_ref, x_ref, r_ref, n_ref, act_ref, low_ref, d_ref, out_ref, back_ref, sum_ref,
          n_s, acc_s, low_s, acc2_s) = refs
     else:
-        mid_ref, n_ref, act_ref, slope_ref, out_ref, n_s, acc_s = refs
+        mid_ref, x_ref, r_ref, n_ref, act_ref, slope_ref, out_ref, n_s, acc_s = refs
     tile = pl.program_id(0)
 
     @pl.when(tile == 0)
     def _():
         mid = h_ref[...] + summed(edge_ref, got_ref, part_ref) + add_ref[...]
         mid_ref[...] = mid
-        xhat, _ = norm_stats(mid)
+        xhat, r = norm_stats(mid)
+        keep_norm(xhat, r, x_ref, r_ref)
         n = (xhat * gain_ref[...] + shift_ref[...]).astype(BF)
         n_ref[...] = n
         n_s[...] = n
         if back:
-            g = g_ref[...]
-            low = g.astype(BF)
+            low = g_ref[...]
             low_ref[...] = low
             low_s[...] = low
-            store_sums(sum_ref, rows_sum(g))
+            sum_ref[...] = old_ref[...]
+            add_sums(sum_ref, DOWN_ROW, rows_sum(low.astype(F32)))
 
     act, slope = gelu_pair(mm(n_s[...], up_ref[...]) + bias_ref[...])
     act = act.astype(BF)
@@ -190,7 +206,7 @@
     if back:
         d = (mm(low_s[...], down_ref[...]) * slope).astype(BF)
         d_ref[...] = d
-        usum_ref[...] = jnp.broadcast_to(rows_sum(d.astype(F32))[None], usum_ref.shape)
+        add_unit_sums(sum_ref, tile, d)
         here2 = mm(d, up_ref[...], NT)
     else:
         slope_ref[...] = slope.astype(BF)
@@ -215,25 +231,23 @@
 
 
 def norm2_back_kernel(
-    edge_ref, got_ref, part_ref, g_ref, mid_ref, gain_ref, w_ref, spread_ref, mg_ref, low_ref, do_ref, sum_ref
+    edge_ref, got_ref, part_ref, g_ref, x_ref, r_ref, gain_ref, w_ref, spread_ref, old_ref, mg_ref, low_ref, do_ref, sum_ref
 ):
     dn = summed(edge_ref, got_ref, part_ref)
-    back, gg = norm_back(mid_ref[...], gain_ref[...], dn)
-    mg = g_ref[...] + back
+    back, gg = norm_back(x_ref, r_ref, gain_ref[...], dn)
+    mg = g_ref[...].astype(F32) + back
     mg_ref[...] = mg
     low = mg.astype(BF)
     low_ref[...] = low
     do_ref[...] = mm(mm(low, w_ref[...]).astype(BF), spread_ref[...]).astype(BF)
-    store_sums(sum_ref, rows_sum(gg), rows_sum(dn), rows_sum(mg))
-
-
-def attend_back_kernel(first, edge_ref, qa_ref, o_ref, do_ref, k0_ref, v0_ref, k1_ref, v1_ref, *refs):
-    if first:
-        dq_ref, dk0_ref, dv0_ref, dk1_ref, dv1_ref = refs
-        olds = (None,) * 4
-    else:
-        olds = refs[:4]
-        dq_ref, dk0_ref, dv0_ref, dk1_ref, dv1_ref = refs[4:]
+    sum_ref[...] = old_ref[...]
+    add_sums(sum_ref, NORM2_ROW, rows_sum(gg), rows_sum(dn), rows_sum(mg))
+
+
+def attend_back_kernel(first, done, edge_ref, qa_ref, o_ref, do_ref, k0_ref, v0_ref, k1_ref, v1_ref, *refs):
+    olds = (None,) * 4 if first else refs[:4]
+    dq_ref, dk0_ref, dv0_ref, *rest = refs[len(refs) - (4 if done else 5) :]
+    dk1_ref, dv1_ref = (None, None) if done else rest
     qa = qa_ref[...]
     do = do_ref[...].astype(F32)
     lane = lane_iota(do.shape)
@@ -251,15 +265,21 @@
         dst = (pt * mm(v_ref[0], doa, NT)).astype(BF)
         dv = mm(pt.astype(BF), doa)
         dk = mm(dst, qa)
-        dv_ref[...] = dv if first else dv_old[...] + dv
-        dk_ref[...] = dk if first else dk_old[...] + dk
+        if not first:
+            dv, dk = dv_old[...] + dv, dk_old[...] + dk
+        if dk_ref is None:
+            rest[0][0] = (dk * SCALE).astype(BF)
+            rest[0][1] = dv.astype(BF)
+        else:
+            dk_ref[...] = dk
+            dv_ref[...] = dv
         part = mm(k.T, dst)
         dqt = part if dqt is None else dqt + part
     dq_ref[...] = (dqt.T * SCALE).astype(BF)
 
 
 def project_back_kernel(
-    local, edge_ref, dq_ref, dk_ref, dv_ref, got_ref, gather_ref, w_ref, d_ref, part_ref, sum_ref
+    local, edge_ref, dq_ref, dk_ref, dv_ref, got_ref, gather_ref, w_ref, old_ref, d_ref, part_ref, sum_ref
 ):
     gather = gather_ref[...]
     dq = mm(dq_ref[...], gather).astype(BF)
@@ -268,36 +288,75 @@
     d = jnp.concatenate([jnp.zeros_like(dq), dq, dk, dv], axis=1)
     d_ref[...] = d
     part_ref[...] = mm(d, w_ref[...], NT).astype(BF)
-    store_sums(sum_ref, rows_sum(d.astype(F32)))
-
-
-def norm1_back_kernel(edge_ref, got_ref, part_ref, mg_ref, h_ref, gain_ref, g_ref, sum_ref):
+    sum_ref[...] = old_ref[...]
+    add_sums(sum_ref, MIXED_ROW, rows_sum(d.astype(F32)))
+
+
+def norm1_back_kernel(edge_ref, got_ref, part_ref, mg_ref, x_ref, r_ref, gain_ref, old_ref, g_ref, sum_ref):
     dn = summed(edge_ref, got_ref, part_ref)
-    back, gg = norm_back(h_ref[...], gain_ref[...], dn)
-    g_ref[...] = mg_ref[...] + back
-    store_sums(sum_ref, rows_sum(gg), rows_sum(dn))
+    back, gg = norm_back(x_ref, r_ref, gain_ref[...], dn)
+    g_ref[...] = (mg_ref[...] + back).reshape(g_ref.shape)
+    sum_ref[...] = old_ref[...]
+    add_sums(sum_ref, NORM1_ROW, rows_sum(gg), rows_sum(dn))
+
+
+def output_kernel(edge_ref, got_ref, part_ref, mid_ref, add_ref, out_ref):
+    out_ref[...] = (mid_ref[...] + summed(edge_ref, got_ref, part_ref) + add_ref[...]).astype(BF)
+
+
+def vectors_kernel(layers, local, sum_ref, gain_ref, shift_ref, qv_ref, out_ref, up_ref, down_ref):
+    for n in range(layers):
+        def row(at, start, size):
+            return sum_ref[8 * n + at : 8 * n + at + 1, :][:, start : start + size]
+
+        width = gain_ref.shape[2]
+        for at, first in ((0, NORM1_ROW), (1, NORM2_ROW)):
+            gain_ref[n, at : at + 1, :] = row(first, 0, width)
+            shift_ref[n, at : at + 1, :] = row(first + 1, 0, width)
+        qv_ref[n, 0:1, :] = row(MIXED_ROW, local, local)
+        qv_ref[n, 1:2, :] = row(MIXED_ROW, 3 * local, local)
+        out_ref[n : n + 1, :] = row(OUT_ROW, 0, width)
+        up_ref[n : n + 1, :] = row(UP_ROW, 0, up_ref.shape[1])
+        down_ref[n : n + 1, :] = row(DOWN_ROW, 0, width)
+
+
+def finish_kernel(cuts, me_ref, own_ref, other_ref, *out_refs):
+    half = own_ref.shape[2]
+    first = me_ref[0] == 0
+    for m in range(own_ref.shape[1]):
+        for at, (a, b) in ((0, (own_ref, other_ref)), (half, (other_ref, own_ref))):
+            v = jnp.where(first, a[0, m].astype(F32), b[0, m].astype(F32))
+            if cuts is None:
+                out_refs[m][0, at : at + half, :] = v
+            else:
+                out_refs[0][0, at : at + half, :] = v[:, :cuts]
+                for t in range(3):
+                    out_refs[1][0, t, at : at + half, :] = v[:, (t + 1) * cuts : (t + 2) * cuts]
 
 
 def feed_back_kernel(
-    tiles, edge_ref, got_ref, part_ref, mg_ref, h_ref, gain_ref, down_ref, up_ref, slope_ref,
-    g_ref, low_ref, d_ref, out_ref, sum_ref, usum_ref, low_s, acc_s,
+    tiles, edge_ref, got_ref, part_ref, mg_ref, x_ref, r_ref, gain_ref, down_ref, up_ref, slope_ref, old_ref, lold_ref,
+    g_ref, low_ref, d_ref, out_ref, sum_ref, lsum_ref, low_s, acc_s,
 ):
     tile = pl.program_id(0)
 
     @pl.when(tile == 0)
     def _():
         dn = summed(edge_ref, got_ref, part_ref)
-        back, gg = norm_back(h_ref[...], gain_ref[...], dn)
+        back, gg = norm_back(x_ref, r_ref, gain_ref[...], dn)
         g = mg_ref[...] + back
         g_ref[...] = g
         low = g.astype(BF)
         low_ref[...] = low
         low_s[...] = low
-        store_sums(sum_ref, rows_sum(gg), rows_sum(dn), rows_sum(g))
+        sum_ref[...] = old_ref[...]
+        lsum_ref[...] = lold_ref[...]
+        add_sums(sum_ref, NORM1_ROW, rows_sum(gg), rows_sum(dn))
+        add_sums(lsum_ref, DOWN_ROW, rows_sum(g))
 
     d = (mm(low_s[...], down_ref[...]) * slope_ref[...].astype(F32)).astype(BF)
     d_ref[...] = d
-    usum_ref[...] = jnp.broadcast_to(rows_sum(d.astype(F32))[None], usum_ref.shape)
+    add_unit_sums(lsum_ref, tile, d)
     here = mm(d, up_ref[...], NT)
 
     @pl.when(tile == 0)
@@ -376,7 +435,7 @@
                 out_specs=[spec] * made,
                 out_shape=[jax.ShapeDtypeStruct(shape, BF)] * made,
                 compiler_params=pltpu.CompilerParams(vmem_limit_bytes=LIMIT * MIB),
-                cost_estimate=pl.CostEstimate(flops=0, bytes_accessed=14 * shape[0] * shape[1], transcendentals=0),
+                cost_estimate=pl.CostEstimate(flops=0, bytes_accessed=int(14 * shape[0] * shape[1] * COST), transcendentals=0),
                 name="turn",
             )(self.knob(), *[values[n] for n in given])
             self.leave(res[0])
@@ -486,34 +545,42 @@
         up_w.append((held[1], starts[1] // unit))
         down_w.append((held[2], starts[2] // unit))
 
-    def give(*mats):
-        theirs, ours = [], []
-        for g in mats:
-            n = g.shape[1] // 2
-            theirs.append(lax.dynamic_slice_in_dim(g, (1 - me) * n, n, axis=1))
-            ours.append(lax.dynamic_slice_in_dim(g, me * n, n, axis=1))
-        got = lax.ppermute(jnp.concatenate(theirs, axis=1), "ctx", swap(2, 1))
-        part = lax.psum_scatter(jnp.concatenate(ours, axis=1) + got, "fsdp", scatter_dimension=0, tiled=True)
-        other = lax.ppermute(part, "ctx", swap(2, 1))
-        low = jnp.where(me == 0, part, other)
-        high = jnp.where(me == 0, other, part)
-        outs, at = [], 0
-        for g in mats:
-            n = g.shape[1] // 2
-            outs.append(jnp.concatenate([low[:, at : at + n], high[:, at : at + n]], axis=1).astype(F32))
-            at += n
-        return outs
+    edge_spec = pl.BlockSpec(memory_space=pltpu.SMEM)
+
+    def whole(a):
+        return (a, block(a.shape, (0,) * a.ndim))
+
+    me_flag = me.astype(jnp.int32)[None]
+    ready = {}
+
+    def give(layer, names, g, first_half=False):
+        g = g.reshape(fsdp, 2, half, g.shape[1])
+        if first_half:
+            got = lax.ppermute(lax.dynamic_index_in_dim(g, 1 - me, 1, False), "ctx", swap(2, 1))
+            mine_half = lax.dynamic_index_in_dim(g, me, 1, False) + got
+            part = lax.psum_scatter(mine_half.reshape(fsdp * half, -1), "fsdp", scatter_dimension=0, tiled=True)
+        else:
+            part = lax.psum_scatter(g.reshape(fsdp * 2 * half, -1), ("fsdp", "ctx"), scatter_dimension=0, tiled=True)
+
+        def finish():
+            mine_half = flow.enter(part)[None, None]
+            other = lax.ppermute(part, "ctx", swap(2, 1))[None, None]
+            attn = len(names) == 2
+            shapes = [(layers, 2 * half, local), (layers, 3, 2 * half, local)] if attn else [(layers, 2 * half, units)]
+            outs = [(ready.get(n), shape, F32, block((1, *shape[1:]), (layer,) + (0,) * (len(shape) - 1)))
+                    for n, shape in zip(names, shapes)]
+            res = call(functools.partial(finish_kernel, local if attn else None), "finish", (1,),
+                       [(me_flag, edge_spec), whole(mine_half), whole(other)], outs, moved=12 * part.size)
+            ready.update(zip(names, res))
+            flow.leave(res[0])
+
+        return finish
 
     tall = ((0, full - rows), (0, 0))
     first_input = jnp.pad(inputs[0], tall)
-    first_grad = jnp.where(live, jnp.pad(cotangent[0], tall).astype(F32), 0.0)
-    edge_spec = pl.BlockSpec(memory_space=pltpu.SMEM)
-
+    first_grad = jnp.where(live, jnp.pad(cotangent[0], tall), jnp.zeros((), BF))
     def rows_of(c, cols):
         return block((CHUNK, cols), (c, 0))
-
-    def whole(a):
-        return (a, block(a.shape, (0,) * a.ndim))
 
     def line(v):
         return (v[None, :], block((1, v.shape[0]), (0, 0)))
@@ -525,16 +592,27 @@
         array, first = w
         return (array, pl.BlockSpec((array.shape[0], unit), lambda t: (0, first + t)))
 
-    sum_spec = block((1, 8, width), (0, 0, 0))
-    sum_out = (None, (1, 8, width), F32, sum_spec)
-    square_sum_out = (None, (1, 8, square), F32, block((1, 8, square), (0, 0, 0)))
-    unit_sum_out = (None, (1, 8, units), F32, pl.BlockSpec((1, 8, unit), lambda t: (0, 0, t)))
+    broad = max(width, square, units)
+    sum_out = (None, (8, broad), F32, block((8, broad), (0, 0)))
+    r_out = (None, (CHUNK, LANES), F32, block((CHUNK, LANES), (0, 0)))
+    x_out = (None, (CHUNK, width), BF, block((CHUNK, width), (0, 0)))
+    rows_out = (None, (CHUNK, width), F32, block((CHUNK, width), (0, 0)))
+    wide_out = (None, (CHUNK, wide), BF, block((CHUNK, wide), (0, 0)))
     part_out = (None, (CHUNK, width), BF, block((CHUNK, width), (0, 0)))
     f32_rows = pltpu.VMEM((CHUNK, width), F32)
     bf_rows = pltpu.VMEM((CHUNK, width), BF)
 
-    keep = [dict() for _ in range(layers)]
-    grads = {"now": first_grad}
+    keep = [{n: [None] * count for n in ("hidden", "mid", "mid_grad", "slope", "q", "x1", "r1", "x2", "r2")}
+            for _ in range(layers)]
+    for k in keep:
+        k["sums"] = jnp.zeros((8, broad), F32)
+    grads = [None] * count
+
+    def chunk(a):
+        return (a, block(a.shape, (0, 0)))
+
+    def given_grad(layer, c):
+        return (first_grad, rows_of(c, width)) if layer == last else chunk(grads[c])
 
     def edge():
         return (flow.knob(), edge_spec)
@@ -554,20 +632,20 @@
         k = keep[layer]
         if job is None:
             pair = [(jnp.zeros((8, LANES), BF), block((8, LANES), (0, 0)))] * 2
-            base, add = first_input, jnp.zeros((width,), F32)
+            base, add = (first_input, rows_of(c, width)), jnp.zeros((width,), F32)
         else:
             pair = both_of(job)
-            base, add = keep[layer - 1]["mid"], down_bias[layer - 1]
+            base, add = chunk(keep[layer - 1]["mid"][c]), down_bias[layer - 1]
         qb, vb = qv_bias[layer, 0], qv_bias[layer, 1]
         bias = jnp.concatenate([jnp.zeros_like(qb), qb, jnp.zeros_like(qb), vb])
-        ins = [edge(), *pair, (base, rows_of(c, width)), line(add), line(norm_gains[layer, 0]), line(norm_shifts[layer, 0]),
+        ins = [edge(), *pair, base, line(add), line(norm_gains[layer, 0]), line(norm_shifts[layer, 0]),
                (attn_w[layer], block((width, square), (0, 0))), line(bias), whole(spread_own), (k_extra, rows_of(c, wide)), whole(q_extra), whole(v_ones)]
-        outs = [out(k, "hidden", width, F32, c), out(k, "normed", width, BF, c), out(k, "q", wide, BF, c),
+        outs = [rows_out, x_out, r_out, out(k, "normed", width, BF, c), wide_out,
                 (k.get("kv0") if c else None, (2, full, wide), BF, block((2, CHUNK, wide), (0, c, 0)))]
         res = call(functools.partial(project_kernel, job is None, local), "project", (1,), ins, outs,
                    flops=2 * CHUNK * width * square, moved=2 * width * square)
-        k["hidden"], k["normed"], k["q"], k["kv0"] = res
-        flow.leave(res[2])
+        k["hidden"][c], k["x1"][c], k["r1"][c], k["normed"], k["q"][c], k["kv0"] = res
+        flow.leave(res[4])
 
     def share(layer):
         k = keep[layer]
@@ -582,7 +660,7 @@
     def attend(layer, c):
         k = keep[layer]
         q, keys, values = head_specs(c)
-        ins = [edge(), (k["q"], q), (k["kv0"], keys), (k["kv0"], values), (k["kv1"], keys), (k["kv1"], values),
+        ins = [edge(), (k["q"][c], pl.BlockSpec((CHUNK, LANES), lambda h: (0, h))), (k["kv0"], keys), (k["kv0"], values), (k["kv1"], keys), (k["kv1"], values),
                (gather_line, pl.BlockSpec((LANES, lined), lambda h: (h, 0))),
                (attn_w[layer], block((width, lined), (0, 0)))]
         outs = [(k.get("o") if c else None, (full, wide), BF, q), (k.get("qa") if c else None, (full, wide), BF, q),
@@ -597,207 +675,202 @@
         k = keep[layer]
         back = layer == last
         pair = both_of(job)
-        ins = [edge(), *pair, (k["hidden"], rows_of(c, width)), line(out_bias[layer]), line(norm_gains[layer, 1]),
+        ins = [edge(), *pair, chunk(k["hidden"][c]), line(out_bias[layer]), line(norm_gains[layer, 1]),
                line(norm_shifts[layer, 1]), unit_cols(up_w[layer]), unit_line(up_bias[layer]), unit_cols(down_w[layer])]
-        outs = [out(k, "mid", width, F32, c), out(k, "normed2", width, BF, c), tile_out(k, "active", c)]
+        outs = [rows_out, x_out, r_out, out(k, "normed2", width, BF, c), tile_out(k, "active", c)]
         scratch = [bf_rows, f32_rows]
         if back:
-            ins.append((grads["now"], rows_of(c, width)))
-            outs += [out(k, "low", width, BF, c), tile_out(k, "d_upper", c), out(k, "late", width, BF, c), part_out,
-                     sum_out, unit_sum_out]
+            ins += [given_grad(layer, c), whole(k["sums"])]
+            outs += [out(k, "low", width, BF, c), tile_out(k, "d_upper", c), part_out, part_out, sum_out]
             scratch += [bf_rows, f32_rows]
         else:
-            outs += [tile_out(k, "slope", c), part_out]
+            outs += [(None, (CHUNK, units), BF, pl.BlockSpec((CHUNK, unit), lambda t: (0, t))), part_out]
         res = call(functools.partial(feed_kernel, back, tiles), "feed", (tiles,), ins, outs, scratch,
                    flops=4 * CHUNK * width * units, moved=4 * width * units)
-        k["mid"], k["normed2"], k["active"] = res[:3]
+        k["mid"][c], k["x2"][c], k["r2"][c], k["normed2"], k["active"] = res[:5]
         if back:
-            k["low"], k["d_upper"], k["late"], part_back, s, us = res[3:]
-            k.setdefault("down_b", []).append(s[0, 0])
-            k.setdefault("up_b", []).append(us[0, 0])
+            k["low"], k["d_upper"], late[c], part_back, k["sums"] = res[5:]
             flow.leave(part_back)
             return flow.tick(part_back)
-        k["slope"], part = res[3:]
+        k["slope"][c], part = res[5:]
         flow.leave(part)
         return flow.tick(part)
 
     def norm2_back(layer, c, job):
         k = keep[layer]
         pair = both_of(job)
-        ins = [edge(), *pair, (grads["now"], rows_of(c, width)), (k["mid"], rows_of(c, width)), line(norm_gains[layer, 1]),
-               (attn_w[layer], block((width, lined), (0, 0))), whole(spread_line)]
-        outs = [out(k, "mid_grad", width, F32, c), out(k, "low2", width, BF, c), out(k, "do", wide, BF, c), sum_out]
-        k["mid_grad"], k["low2"], k["do"], s = call(norm2_back_kernel, "norm2_back", (1,), ins, outs,
+        ins = [edge(), *pair, given_grad(layer, c), chunk(k["x2"][c]), chunk(k["r2"][c]), line(norm_gains[layer, 1]),
+               (attn_w[layer], block((width, lined), (0, 0))), whole(spread_line), whole(k["sums"])]
+        outs = [rows_out, out(k, "low2", width, BF, c), out(k, "do", wide, BF, c), sum_out]
+        k["mid_grad"][c], k["low2"], k["do"], k["sums"] = call(norm2_back_kernel, "norm2_back", (1,), ins, outs,
                                                     flops=2 * CHUNK * width * lined, moved=20 * CHUNK * width)
-        k.setdefault("gains2", []).append(s[0, 0])
-        k.setdefault("shifts2", []).append(s[0, 1])
-        k.setdefault("out_b", []).append(s[0, 2])
         flow.leave(k["do"])
 
     def attend_back(layer, c, sums):
         k = keep[layer]
         q, keys, values = head_specs(c, BACK)
         acc = pl.BlockSpec((full, LANES), lambda h: (0, h))
-        first = sums is None
+        first, done = sums is None, (c + 1) * BACK == full
         ins = [edge(), (k["qa"], q), (k["o"], q), (k["do"], q), (k["kv0"], keys), (k["kv0"], values), (k["kv1"], keys),
                (k["kv1"], values)]
-        live_in = len(ins)
-        olds = [] if first else [(s, acc) for s in sums]
-        old_dq = k.get("dq") if c else None
+        olds = [] if first else [(v, acc) for v in sums]
+        old_dq = k.get("dq")
         everything = ins + olds + ([] if old_dq is None else [(old_dq, pl.BlockSpec(memory_space=pl.ANY))])
-        aliases = {} if first else {live_in + n: 1 + n for n in range(4)}
+        aliases = {} if first else {len(ins) + n: 1 + n for n in range(2 if done else 4)}
         if old_dq is not None:
             aliases[len(everything) - 1] = 0
+        kept = len(ins) + len(olds)
+        sum_shape = jax.ShapeDtypeStruct((full, wide), F32)
 
         def body(*refs):
-            kept = live_in + len(olds)
-            attend_back_kernel(first, *refs[:kept], *refs[len(everything) :])
+            attend_back_kernel(first, done, *refs[:kept], *refs[len(everything) :])
 
         res = pl.pallas_call(
             body,
             grid=(heads,),
-            in_specs=[s for _, s in everything],
-            out_specs=[q] + [acc] * 4,
-            out_shape=[jax.ShapeDtypeStruct((full, wide), BF)] + [jax.ShapeDtypeStruct((full, wide), F32)] * 4,
+            in_specs=[v for _, v in everything],
+            out_specs=[q, acc, acc] + ([pl.BlockSpec((2, full, LANES), lambda h: (0, 0, h))] if done else [acc, acc]),
+            out_shape=[jax.ShapeDtypeStruct((full, wide), BF), sum_shape, sum_shape]
+            + ([jax.ShapeDtypeStruct((2, full, wide), BF)] if done else [sum_shape, sum_shape]),
             input_output_aliases=aliases,
             compiler_params=pltpu.CompilerParams(vmem_limit_bytes=LIMIT * MIB),
-            cost_estimate=pl.CostEstimate(flops=20 * BACK * full * wide, bytes_accessed=40 * full * wide, transcendentals=0),
+            cost_estimate=pl.CostEstimate(flops=int(20 * BACK * full * wide * COST), bytes_accessed=int(40 * full * wide * COST), transcendentals=0),
             name="attend_back",
-        )(*[a for a, _ in everything])
+        )(*[v for v, _ in everything])
         k["dq"] = res[0]
         flow.leave(res[0])
         return res[1:]
 
     def share_back(sums):
-        dk0, dv0, dk1, dv1 = sums
-        theirs = jnp.stack([dk1 * SCALE, dv1]).astype(BF)
+        dk0, dv0, theirs = sums
         return dk0, dv0, lax.ppermute(theirs, "ctx", swap(2, 1))
 
     def project_back(layer, c, shared):
         k = keep[layer]
         dk0, dv0, got = shared
         ins = [edge(), (k["dq"], rows_of(c, wide)), (dk0, rows_of(c, wide)), (dv0, rows_of(c, wide)),
-               (got, block((2, CHUNK, wide), (0, c, 0))), whole(gather_own), (attn_w[layer], block((width, square), (0, 0)))]
-        outs = [out(k, "d_mixed", square, BF, c), part_out, square_sum_out]
-        k["d_mixed"], part, s = call(functools.partial(project_back_kernel, local), "project_back", (1,), ins, outs,
+               (got, block((2, CHUNK, wide), (0, c, 0))), whole(gather_own), (attn_w[layer], block((width, square), (0, 0))),
+               whole(k["sums"])]
+        outs = [out(k, "d_mixed", square, BF, c), part_out, sum_out]
+        k["d_mixed"], part, k["sums"] = call(functools.partial(project_back_kernel, local), "project_back", (1,), ins, outs,
                                      flops=2 * CHUNK * width * square, moved=2 * width * square)
-        k.setdefault("mixed_b", []).append(s[0, 0])
         flow.leave(part)
         return flow.tick(part)
 
     def norm1_back(layer, c, job):
         k = keep[layer]
         pair = both_of(job)
-        ins = [edge(), *pair, (k["mid_grad"], rows_of(c, width)), (k["hidden"], rows_of(c, width)), line(norm_gains[layer, 0])]
-        outs = [out(k, "grad", width, F32, c), sum_out]
-        k["grad"], s = call(norm1_back_kernel, "norm1_back", (1,), ins, outs, moved=20 * CHUNK * width)
-        k.setdefault("gains1", []).append(s[0, 0])
-        k.setdefault("shifts1", []).append(s[0, 1])
-        flow.leave(k["grad"])
+        ins = [edge(), *pair, chunk(k["mid_grad"][c]), chunk(k["x1"][c]), chunk(k["r1"][c]),
+               line(norm_gains[layer, 0]), whole(k["sums"])]
+        outs = [(k.get("grad"), (rows, 1, width), F32, block((CHUNK, 1, width), (c, 0, 0))), sum_out]
+        k["grad"], k["sums"] = call(norm1_back_kernel, "norm1_back", (1,), ins, outs, moved=20 * CHUNK * width)
+        flow.leave(k["sums"])
+
+    def finish_output(layer, c, job):
+        k = keep[layer]
+        pair = both_of(job)
+        ins = [edge(), *pair, chunk(k["mid"][c]), line(down_bias[layer])]
+        (k["outputs"],) = call(output_kernel, "output", (1,), ins, [out(k, "outputs", width, BF, c)], moved=10 * CHUNK * width)
+        flow.leave(k["outputs"])
 
     def feed_back(layer, c, job):
         k, b = keep[layer], keep[layer - 1]
         pair = both_of(job)
-        ins = [edge(), *pair, (k["mid_grad"], rows_of(c, width)), (k["hidden"], rows_of(c, width)), line(norm_gains[layer, 0]),
+        ins = [edge(), *pair, chunk(k["mid_grad"][c]), chunk(k["x1"][c]), chunk(k["r1"][c]), line(norm_gains[layer, 0]),
                unit_cols(down_w[layer - 1]), unit_cols(up_w[layer - 1]),
-               (b["slope"], pl.BlockSpec((CHUNK, unit), lambda t: (c, t)))]
-        outs = [out(k, "grad", width, F32, c), out(b, "low", width, BF, c), tile_out(b, "d_upper", c), part_out, sum_out,
-                unit_sum_out]
+               (b["slope"][c], pl.BlockSpec((CHUNK, unit), lambda t: (0, t))), whole(k["sums"]), whole(b["sums"])]
+        outs = [rows_out, out(b, "low", width, BF, c), tile_out(b, "d_upper", c), part_out, sum_out, sum_out]
         res = call(functools.partial(feed_back_kernel, tiles), "feed_back", (tiles,), ins, outs, [bf_rows, f32_rows],
                    flops=4 * CHUNK * width * units, moved=4 * width * units)
-        k["grad"], b["low"], b["d_upper"], part, s, us = res
-        k.setdefault("gains1", []).append(s[0, 0])
-        k.setdefault("shifts1", []).append(s[0, 1])
-        b.setdefault("down_b", []).append(s[0, 2])
-        b.setdefault("up_b", []).append(us[0, 0])
+        grads[c], b["low"], b["d_upper"], part, k["sums"], b["sums"] = res
         flow.leave(part)
         return flow.tick(part)
 
     def weight_grad(left, right):
-        return lax.dot_general(left, right, (((0,), (0,)), ((), ())), preferred_element_type=F32).astype(BF)
-
-    owned = [dict() for _ in range(layers)]
-
-    def grad_feed(layer):
-        k = keep[layer]
-        down = weight_grad(flow.enter(k["low"]), k["active"])
-        flow.leave(down)
-        up = weight_grad(flow.enter(k["normed2"]), k["d_upper"])
-        flow.leave(up)
-        owned[layer]["up"], owned[layer]["down"] = give(up, down)
+        g = lax.dot_general(left, right, (((0,), (0,)), ((), ())), preferred_element_type=F32).astype(BF)
+        return with_layout_constraint(g, Layout((0, 1)))
+
+    def grad_down(layer):
+        k = keep[layer]
+        g = weight_grad(flow.enter(k["low"]), k["active"])
+        flow.leave(g)
+        return give(layer, ("down",), g)
+
+    def grad_up(layer):
+        k = keep[layer]
+        g = weight_grad(flow.enter(k["normed2"]), k["d_upper"])
+        flow.leave(g)
+        return give(layer, ("up",), g)
 
     def grad_attn(layer):
         k = keep[layer]
-        g1 = weight_grad(flow.enter(k["normed"]), k["d_mixed"])
-        g2 = weight_grad(k["low2"], k["attended"])
+        g2 = weight_grad(flow.enter(k["low2"]), k["attended"])
+        g1 = weight_grad(k["normed"], k["d_mixed"])
         g = jnp.concatenate([g2[:, :local], g1[:, local:]], axis=1)
         flow.leave(g)
-        (owned[layer]["attn"],) = give(g)
-
-    jobs = [None] * count
+        return give(layer, ("out", "qkv"), g, layer == 0)
+
+    jobs, late = [None] * count, [None] * count
     for layer in range(layers):
         for c in each:
             project(layer, c, jobs[c])
         share(layer)
         jobs = [attend(layer, c) for c in each]
         jobs = [feed(layer, c, jobs[c]) for c in each]
-    k = keep[last]
-    final = lax.psum(k["late"], "tp").astype(F32)
-    outputs = (k["mid"] + final + down_bias[last]).astype(BF)
-    vectors = [None] * layers
+    late_jobs, endings = [None] * count, []
     for layer in reversed(range(layers)):
         k = keep[layer]
         sums = None
         for c in each:
             norm2_back(layer, c, jobs[c])
-            if (c + 1) * CHUNK % BACK == 0:
+            if c == 0:
+                endings.append(grad_down(layer))
+            if c == 1:
+                endings.append(grad_up(layer))
+            final = (c + 1) * CHUNK % BACK == 0
+            if c < count - 1:
+                late_jobs[c] = flow.tick(late[c]) if layer == last else flow.tick()
+            if final:
                 sums = attend_back(layer, c * CHUNK // BACK, sums)
+        if layer == last:
+            late_jobs[-1] = flow.tick(late[-1])
         shared = share_back(sums)
-        grad_feed(layer)
-        jobs = [project_back(layer, c, shared) for c in each]
-        grad_attn(layer)
+        for c in each:
+            jobs[c] = project_back(layer, c, shared)
+            if layer == last:
+                finish_output(layer, c, late_jobs[c])
+            elif endings and c < len(endings) - 2:
+                endings[c]()
+        endings.append(grad_attn(layer))
         for c in each:
             if layer > 0:
                 jobs[c] = feed_back(layer, c, jobs[c])
             else:
                 norm1_back(layer, c, jobs[c])
-        grads["now"] = k["grad"]
-        total = {n: functools.reduce(jnp.add, k[n])
-                 for n in ("gains1", "gains2", "shifts1", "shifts2", "mixed_b", "out_b", "up_b", "down_b")}
-        mixed = total["mixed_b"]
-        flat = jnp.concatenate(
-            [total["gains1"], total["gains2"], total["shifts1"], total["shifts2"], mixed[local : 2 * local],
-             mixed[3 * local :], total["out_b"], total["up_b"], total["down_b"]]
-        )
-        size = flat.shape[0]
-        flat = jnp.pad(flat, (0, up_to(size, 1024) - size)).reshape(-1, LANES)
-        flat = group_sum(flat, fsdp).reshape(-1)
-        ends = np.cumsum([width] * 4 + [local] * 2 + [width, units, width])[:-1]
-        vectors[layer] = jnp.split(flat[:size], ends)
-
-    def stack(index):
-        return jnp.stack([v[index] for v in vectors])
-
-    def both(index):
-        return jnp.stack([jnp.stack([v[index], v[index + 1]]) for v in vectors])
-
-    def matrices(name):
-        return jnp.stack([o[name] for o in owned])
-
-    attn = matrices("attn")
+    group = group_sum(jnp.concatenate([flow.enter(keep[0]["sums"])] + [k["sums"] for k in keep[1:]]), fsdp)
+    for ending in endings[-3:]:
+        ending()
+
+    def all_of(*shape):
+        return (None, shape, F32, block(shape, (0,) * len(shape)))
+
+    gains, shifts, qv, out_b, up_b, down_b = call(
+        functools.partial(vectors_kernel, layers, local), "vectors", (1,), [whole(group)],
+        [all_of(layers, 2, width)] * 2 + [all_of(layers, 2, local), all_of(layers, width), all_of(layers, units), all_of(layers, width)],
+    )
     return (
-        outputs[None, :rows],
-        grads["now"][None, :rows],
-        both(0),
-        both(2),
-        attn[:, :, local:].reshape(layers, -1, 3, local),
-        both(4),
-        attn[:, :, :local],
-        stack(6),
-        matrices("up"),
-        stack(7),
-        matrices("down"),
-        stack(8),
+        keep[last]["outputs"][None, :rows],
+        keep[0]["grad"].reshape(1, rows, width),
+        gains,
+        shifts,
+        ready["qkv"].transpose(0, 2, 1, 3),
+        qv,
+        ready["out"],
+        out_b,
+        ready["up"],
+        up_b,
+        ready["down"],
+        down_b,
     )
 
 

time: 837 us -> 753 us (0.90)
  local copies, waits for them, and re-layouts: 187 us -> 133 us
  other arithmetic: 56.9 us -> 10.6 us
  Pallas kernels: 219 us -> 235 us
    unnamed x475 -> x606, local copies, waits for them, and re-layouts: 156 us -> 113 us
    ppermute x8 -> x7, starting transfers between devices: 31.3 us -> 4.76 us  [the longest x6 3.26 us: finish(): other = lax.ppermute(part, 'ctx', swap(2, 1))[None, None]]
    add x13 -> x1, other arithmetic: 25.6 us -> 2.84 us  [give(): mine_half = lax.dynamic_index_in_dim(g, me, 1, False) + got]
    pallas_call x48 -> x59, Pallas kernels: 166 us -> 180 us  [call(): pl.pallas_call(body, grid=grid, in_specs=specs, out_specs=[o[3] for o in...]
    another operation x21 -> x0, other arithmetic: 11 us -> none  [the longest x3 4.66 us: matrices(): return jnp.stack([o[name] for o in owned])]
    ppermute x36 -> x38, starting transfers between devices: 89.3 us -> 99.3 us  [tick(): self.got = lax.ppermute(send if across else fresh, 'tp', perm)]
    ppermute x2, starting transfers between devices: 8.93 us -> 17.4 us  [share_back(): return (dk0, dv0, lax.ppermute(theirs, 'ctx', swap(2, 1)))]
    ppermute x28 -> x32, starting transfers between devices: 24.1 us -> 27.5 us  [tick(): self.there = lax.ppermute(pair, 'tp', [(1, 2), (2, 1)])]
  transfers between devices with their start and end apart: 90 -> 93, of which waited for: 30 -> 30; matrix products, arithmetic and copies ran while one was open for 17% -> 6% of each run, Pallas kernels for 24% -> 30%
where the time goes in v3:
time: 753 us; the launch traced here: 742 us
  Pallas kernels  235 us (31%)
  waiting for transfers between devices  160 us (21%)
  starting transfers between devices  159 us (21%)
  local copies, waits for them, and re-layouts  133 us (18%)
  matrix products  25.2 us (3%)
  between operations  18.8 us (2%)
  other arithmetic  10.6 us (1%)
    pallas_call x59, Pallas kernels, call(): pl.pallas_call(body, grid=grid, in_specs=specs, out_specs=[o[3] for o in...  180 us
    ppermute x38, waiting for transfers between devices, tick(): self.got = lax.ppermute(send if across else fresh, 'tp', perm)  117 us
    unnamed x606, local copies, waits for them, and re-layouts  113 us
    ppermute x38, starting transfers between devices, tick(): self.got = lax.ppermute(send if across else fresh, 'tp', perm)  99.3 us
    pallas_call x4, Pallas kernels, attend_back(): pl.pallas_call(body, grid=(heads,), in_specs=[v for _, v in everything],...  36.1 us
    ppermute x32, starting transfers between devices, tick(): self.there = lax.ppermute(pair, 'tp', [(1, 2), (2, 1)])  27.5 us
    dot_general x8, matrix products, weight_grad(): lax.dot_general(left, right, (((0,), (0,)), ((), ())), preferred_element_...  25.2 us
    all_gather x3, waiting for transfers between devices, fetch(): return lax.all_gather(w, ('fsdp', 'ctx'), axis=0, tiled=True)  23.4 us
  transfers between devices with their start and end apart: 93, of which 30 were waited for; matrix products, arithmetic and copies ran while one was open for 6% of the time, Pallas kernels for 30%

profile of v3, /device:TPU:1, one launch (start us, length us, event | category | flops | bytes accessed | tf_op | source)
XLA Modules:
  0.0 741.9 jit_solution(838744759670082091)
XLA Ops:
  23.6 23.4 %all-gather.4.cloned.1.call-done.refs_7_.refs_6_ = bf16[1280,1280]{1,0:T(8,128)(2,1)} async-done(((bf16[160,1280]{1,0:T(8,128)(2,1)}), bf16[1280,1280]{1,0:T(8,128)(2,1)}) %all-gather.4.cloned.1.call-update) | async-done | bytes 3276816 | tf_op jit(solution)/shard_map/all_gather | solution.py:529
  61.6 3.2 collective-permute-done.refs_4_.refs_5_.refs_6_.refs_7_
  64.7 5.0 attend.8
  72.9 5.0 attend.9
  79.2 4.0 collective-permute-done.1.refs_1_
  84.2 5.0 attend.10
  89.1 4.6 collective-permute-done.2.refs_1_
  93.9 4.9 collective-permute-start.4
  99.5 5.0 attend.11
  108.8 3.2 collective-permute-start.6
  119.2 5.6 feed.8
  129.6 6.6 feed.9
  140.8 5.6 feed.10
  151.2 5.6 feed.11
  165.8 3.8 copy-done
  184.4 4.2 collective-permute-done.17.refs_1_
  190.8 10.8 %collective-permute-done.18.refs_1_ = bf16[192,1280]{1,0:T(8,128)(2,1)S(1)} collective-permute-done((bf16[192,1280]{1,0:T(8,128)(2,1)S(1)}, bf16[192,1280]{1,0:T(8,128)(2,1)S(1)}, u32[]{:S(2)}, u32[]{:S(2)}) %collective-permute-start.18) | collective-permute-done | bytes 491552 | tf_op jit(solution)/shard_map/ppermute | solution.py:454
  203.0 5.5 collective-permute-start.19
  211.5 5.0 attend.12
  217.8 5.0 attend.13
  224.1 4.0 collective-permute-done.20.refs_1_
  228.9 5.0 attend.14
  233.9 4.8 collective-permute-done.21.refs_1_
  238.8 4.7 collective-permute-start.23
  244.2 5.0 attend.15
  249.2 3.2 collective-permute-done.23.refs_1_
  257.5 9.2 %feed.12 = (f32[192,1280]{1,0:T(8,128)S(1)}, bf16[192,1280]{1,0:T(8,128)(2,1)S(1)}, f32[192,128]{1,0:T(8,128)S(1)}, bf16[768,1280]{1,0:T(8,128)(2,1)S(1)}, bf16[...) custom-call(s32[1]{0:T(128)} %bitcast.refs_0_.edge_ref, ...), custom_call_target="tpu_custom_call" | custom-call | flops 125829120 | bytes 655360 | tf_op jit(solution)/shard_map/feed/pallas_call | solution.py:49
  269.5 9.2 %feed.13 = (f32[192,1280]{1,0:T(8,128)S(1)}, bf16[192,1280]{1,0:T(8,128)(2,1)S(1)}, f32[192,128]{1,0:T(8,128)S(1)}, bf16[768,1280]{1,0:T(8,128)(2,1)S(1)}, bf16[...) custom-call(s32[1]{0:T(128)} %bitcast.refs_0_.edge_ref, ...), custom_call_target="tpu_custom_call", output_to_operand_aliasing={{3}: (12, {}), {4}: (13, {}), {5}: (14, {}), {6}: (15, {})} | custom-call | flops 125829120 | bytes 655360 | tf_op jit(solution)/shard_map/feed/pallas_call | solution.py:49
  282.0 9.2 %feed.14 = (f32[192,1280]{1,0:T(8,128)S(1)}, bf16[192,1280]{1,0:T(8,128)(2,1)S(1)}, f32[192,128]{1,0:T(8,128)S(1)}, bf16[768,1280]{1,0:T(8,128)(2,1)S(1)}, bf16[...) custom-call(s32[1]{0:T(128)} %bitcast.refs_0_.edge_ref, ...), custom_call_target="tpu_custom_call", output_to_operand_aliasing={{3}: (12, {}), {4}: (13, {}), {5}: (14, {}), {6}: (15, {})} | custom-call | flops 125829120 | bytes 655360 | tf_op jit(solution)/shard_map/feed/pallas_call | solution.py:49
  294.1 9.2 %feed.15 = (f32[192,1280]{1,0:T(8,128)S(1)}, bf16[192,1280]{1,0:T(8,128)(2,1)S(1)}, f32[192,128]{1,0:T(8,128)S(1)}, bf16[768,1280]{1,0:T(8,128)(2,1)S(1)}, bf16[...) custom-call(s32[1]{0:T(128)} %bitcast.refs_0_.edge_ref, ...), custom_call_target="tpu_custom_call", output_to_operand_aliasing={{3}: (12, {}), {4}: (13, {}), {5}: (14, {}), {6}: (15, {})} | custom-call | flops 125829120 | bytes 655360 | tf_op jit(solution)/shard_map/feed/pallas_call | solution.py:49
  312.4 4.2 convolution_convert_fusion.3
  319.6 6.4 collective-permute-done.33.refs_1_
  331.7 4.1 copy-done.1
  346.2 3.9 collective-permute-start.35
  350.1 4.2 convolution_convert_fusion.2
  363.1 8.7 %attend_back.4 = (bf16[768,512]{1,0:T(8,128)(2,1)S(1)}, f32[768,512]{1,0:T(8,128)S(1)}, f32[768,512]{1,0:T(8,128)S(1)}, f32[768,512]{1,0:T(8,128)S(1)}, f32[768,512]{1,0:T(8,128)S(1)}) custom-call(s32[1]{0:T(128)} %bitcast.refs_0_.edge_ref, bf16[768,512]{1,0:T(8,128)(2,1)S(1)} %copy-done.41, bf16[768,512]{1,0:T(8,128)(2,1)S(1)} %copy-done.39, ...), custom_call_target="tpu_custom_call" | custom-call | flops 301989888 | bytes 1572864 | tf_op jit(solution)/shard_map/attend_back/pallas_call | solution.py:728
  371.8 3.8 copy-done.2
  381.2 9.4 %attend_back.5 = (bf16[768,512]{1,0:T(8,128)(2,1)S(1)}, f32[768,512]{1,0:T(8,128)S(1)}, f32[768,512]{1,0:T(8,128)S(1)}, bf16[2,768,512]{2,1,0:T(8,128)(2,1)S(1)}) custom-call(s32[1]{0:T(128)} %bitcast.refs_0_.edge_ref, bf16[768,512]{1,0:T(8,128)(2,1)S(1)} %copy-done.41, ...), custom_call_target="tpu_custom_call", output_to_operand_aliasing={{1}: (8, {}), {2}: (9, {}), {0}: (12, {})} | custom-call | flops 301989888 | bytes 1572864 | tf_op jit(solution)/shard_map/attend_back/pallas_call | solution.py:728
  390.6 8.4 %collective-permute-start.41 = (bf16[2,768,512]{2,1,0:T(8,128)(2,1)S(1)}, bf16[2,768,512]{2,1,0:T(8,128)(2,1)S(1)}, u32[]{:S(2)}, u32[]{:S(2)}) collective-permute-start(bf16[2,768,512]{2,1,0:T(8,128)(2,1)S(1)} %get-tuple-element.646), channel_id=1, source_target_pairs={{0,4},{4,0},{1,5},{5,1},{2,6},{6,2},{3,7},{7,3},{8,12},{12,8},{9,1... | collective-permute-start | bytes 4718600 | tf_op jit(solution)/shard_map/ppermute | solution.py:746
  401.8 10.8 %collective-permute-done.39.refs_1_ = bf16[192,1280]{1,0:T(8,128)(2,1)S(1)} collective-permute-done((bf16[192,1280]{1,0:T(8,128)(2,1)S(1)}, bf16[192,1280]{1,0:T(8,128)(2,1)S(1)}, u32[]{:S(2)}, u32[]{:S(2)}) %collective-permute-start.39) | collective-permute-done | bytes 491552 | tf_op jit(solution)/shard_map/ppermute | solution.py:454
  412.8 3.3 collective-permute-start.42
  418.2 8.7 %collective-permute-done.42.refs_1_ = bf16[192,1280]{1,0:T(8,128)(2,1)S(1)} collective-permute-done((bf16[192,1280]{1,0:T(8,128)(2,1)S(1)}, bf16[192,1280]{1,0:T(8,128)(2,1)S(1)}, u32[]{:S(2)}, u32[]{:S(2)}) %collective-permute-start.42) | collective-permute-done | bytes 491552 | tf_op jit(solution)/shard_map/ppermute | solution.py:454
  432.5 7.6 %collective-permute-done.44.refs_1_ = bf16[192,1280]{1,0:T(8,128)(2,1)S(1)} collective-permute-done((bf16[192,1280]{1,0:T(8,128)(2,1)S(1)}, bf16[192,1280]{1,0:T(8,128)(2,1)S(1)}, u32[]{:S(2)}, u32[]{:S(2)}) %collective-permute-start.44) | collective-permute-done | bytes 491552 | tf_op jit(solution)/shard_map/ppermute | solution.py:454
  445.7 6.7 collective-permute-done.46.refs_1_
  453.8 5.0 collective-permute-start.48
  469.5 3.5 pad_maximum_fusion
  483.2 5.8 feed_back.4
  492.5 5.8 feed_back.5
  498.6 3.5 collective-permute-start.54
  503.0 5.9 feed_back.6
  509.8 3.4 collective-permute-start.56
  513.9 5.8 feed_back.7
  526.7 4.2 convolution_convert_fusion.1
  531.0 3.3 collective-permute-start.58
  535.0 5.7 collective-permute-done.58.refs_1_
  554.9 4.2 convolution_convert_fusion
  567.2 8.7 %attend_back.6 = (bf16[768,512]{1,0:T(8,128)(2,1)S(1)}, f32[768,512]{1,0:T(8,128)S(1)}, f32[768,512]{1,0:T(8,128)S(1)}, f32[768,512]{1,0:T(8,128)S(1)}, f32[768,512]{1,0:T(8,128)S(1)}) custom-call(s32[1]{0:T(128)} %bitcast.refs_0_.edge_ref, bf16[768,512]{1,0:T(8,128)(2,1)S(1)} %copy-done.45, bf16[768,512]{1,0:T(8,128)(2,1)S(1)} %copy-done.43, ...), custom_call_target="tpu_custom_call" | custom-call | flops 301989888 | bytes 1572864 | tf_op jit(solution)/shard_map/attend_back/pallas_call | solution.py:728
  582.7 9.4 %attend_back.7 = (bf16[768,512]{1,0:T(8,128)(2,1)S(1)}, f32[768,512]{1,0:T(8,128)S(1)}, f32[768,512]{1,0:T(8,128)S(1)}, bf16[2,768,512]{2,1,0:T(8,128)(2,1)S(1)}) custom-call(s32[1]{0:T(128)} %bitcast.refs_0_.edge_ref, bf16[768,512]{1,0:T(8,128)(2,1)S(1)} %copy-done.46, ...), custom_call_target="tpu_custom_call", output_to_operand_aliasing={{1}: (8, {}), {2}: (9, {}), {0}: (12, {})} | custom-call | flops 301989888 | bytes 1572864 | tf_op jit(solution)/shard_map/attend_back/pallas_call | solution.py:728
  592.1 9.0 %collective-permute-start.63 = (bf16[2,768,512]{2,1,0:T(8,128)(2,1)S(1)}, bf16[2,768,512]{2,1,0:T(8,128)(2,1)S(1)}, u32[]{:S(2)}, u32[]{:S(2)}) collective-permute-start(bf16[2,768,512]{2,1,0:T(8,128)(2,1)S(1)} %get-tuple-element.787), channel_id=1, source_target_pairs={{0,4},{4,0},{1,5},{5,1},{2,6},{6,2},{3,7},{7,3},{8,12},{12,8},{9,1... | collective-permute-start | bytes 4718600 | tf_op jit(solution)/shard_map/ppermute | solution.py:746
  607.7 10.0 %collective-permute-start.65 = (bf16[192,1280]{1,0:T(8,128)(2,1)}, bf16[192,1280]{1,0:T(8,128)(2,1)}, u32[]{:S(2)}, u32[]{:S(2)}) collective-permute-start(bf16[192,1280]{1,0:T(8,128)(2,1)} %get-tuple-element.789.refs_0_), channel_id=1, source_target_pairs={{0,1},{3,2},{4,5},{7,6},{8,9},{11,10},{12,13},{15,14},{16,17},{19,... | collective-permute-start | bytes 1474568 | tf_op jit(solution)/shard_map/ppermute | solution.py:454
  671.0 3.3 collective-permute-done.80
  681.9 8.2 %collective-permute-done.72.refs_1_ = bf16[192,1280]{1,0:T(8,128)(2,1)S(1)} collective-permute-done((bf16[192,1280]{1,0:T(8,128)(2,1)}, bf16[192,1280]{1,0:T(8,128)(2,1)S(1)}, u32[]{:S(2)}, u32[]{:S(2)}) %collective-permute-start.72) | collective-permute-done | bytes 491552 | tf_op jit(solution)/shard_map/ppermute | solution.py:454
  695.9 11.2 %collective-permute-done.75.refs_1_ = bf16[192,1280]{1,0:T(8,128)(2,1)S(1)} collective-permute-done((bf16[192,1280]{1,0:T(8,128)(2,1)S(1)}, bf16[192,1280]{1,0:T(8,128)(2,1)S(1)}, u32[]{:S(2)}, u32[]{:S(2)}) %collective-permute-start.75) | collective-permute-done | bytes 491552 | tf_op jit(solution)/shard_map/ppermute | solution.py:454
  708.9 8.2 %collective-permute-done.76.refs_1_ = bf16[192,1280]{1,0:T(8,128)(2,1)S(1)} collective-permute-done((bf16[192,1280]{1,0:T(8,128)(2,1)S(1)}, bf16[192,1280]{1,0:T(8,128)(2,1)S(1)}, u32[]{:S(2)}, u32[]{:S(2)}) %collective-permute-start.76) | collective-permute-done | bytes 491552 | tf_op jit(solution)/shard_map/ppermute | solution.py:454
  (891 shorter events, 324.8 us)
Async XLA Ops:
  7.2 39.8 %all-gather.4.cloned.1.call-start = ((), (), s32[]{:S(2)}) async-start(), calls=%async_computation.6 | async-start | bytes 3686400 | tf_op jit(solution)/shard_map/all_gather | solution.py:529
  11.5 102.6 %all-gather.6.cloned.1.call-start = ((), (), s32[]{:S(2)}) async-start(), calls=%async_computation.7 | async-start | bytes 7372800 | tf_op jit(solution)/shard_map/all_gather | solution.py:529
  15.6 150.1 %all-gather.8.cloned.1.call-start = ((), (), s32[]{:S(2)}) async-start(), calls=%async_computation.8 | async-start | bytes 11059200 | tf_op jit(solution)/shard_map/all_gather | solution.py:529
  19.9 597.9 %reduce-scatter.11.cloned.1.call-start = ((), (), s32[]{:S(2)}) async-start(), calls=%async_computation.11 | async-start | bytes 3686400 | tf_op jit(solution)/shard_map/reduce_scatter | solution.py:563
  69.7 13.5 %collective-permute-start.1 = (bf16[192,1280]{1,0:T(8,128)(2,1)S(1)}, bf16[192,1280]{1,0:T(8,128)(2,1)S(1)}, u32[]{:S(2)}, u32[]{:S(2)}) collective-permute-start(bf16[192,1280]{1,0:T(8,128)(2,1)S(1)} %get-tuple-element.450.refs_0_), channel_id=1, source_target_pairs={{0,1},{3,2},{4,5},{7,6},{8,9},{11,10},{12,13},{15,14},{16,17},{19,... | collective-permute-start | bytes 1474568 | tf_op jit(solution)/shard_map/ppermute | solution.py:454
  77.9 15.9 %collective-permute-start.2 = (bf16[192,1280]{1,0:T(8,128)(2,1)S(1)}, bf16[192,1280]{1,0:T(8,128)(2,1)S(1)}, u32[]{:S(2)}, u32[]{:S(2)}) collective-permute-start(bf16[192,1280]{1,0:T(8,128)(2,1)S(1)} %get-tuple-element.455.refs_0_), channel_id=1, source_target_pairs={{0,1},{3,2},{4,5},{7,6},{8,9},{11,10},{12,13},{15,14},{16,17},{19,... | collective-permute-start | bytes 1474568 | tf_op jit(solution)/shard_map/ppermute | solution.py:454
  83.3 10.5 %collective-permute-start.3 = (bf16[192,1280]{1,0:T(8,128)(2,1)S(1)}, bf16[192,1280]{1,0:T(8,128)(2,1)S(1)}, u32[]{:S(2)}, u32[]{:S(2)}) collective-permute-start(bf16[192,1280]{1,0:T(8,128)(2,1)S(1)} %turn.35.refs_2_), channel_id=1, source_target_pairs={{1,2},{2,1},{5,6},{6,5},{9,10},{10,9},{13,14},{14,13},{17,18},{18,... | collective-permute-start | bytes 1474568 | tf_op jit(solution)/shard_map/ppermute | solution.py:450
  93.9 13.9 %collective-permute-start.4 = (bf16[192,1280]{1,0:T(8,128)(2,1)S(1)}, bf16[192,1280]{1,0:T(8,128)(2,1)S(1)}, u32[]{:S(2)}, u32[]{:S(2)}) collective-permute-start(bf16[192,1280]{1,0:T(8,128)(2,1)S(1)} %get-tuple-element.470.refs_2_), channel_id=1, source_target_pairs={{0,1},{3,2},{1,0},{2,3},{4,5},{7,6},{5,4},{6,7},{8,9},{11,10},{9,8... | collective-permute-start | bytes 1474568 | tf_op jit(solution)/shard_map/ppermute | solution.py:454
  108.8 16.0 %collective-permute-start.6 = (bf16[192,1280]{1,0:T(8,128)(2,1)}, bf16[192,1280]{1,0:T(8,128)(2,1)S(1)}, u32[]{:S(2)}, u32[]{:S(2)}) collective-permute-start(bf16[192,1280]{1,0:T(8,128)(2,1)} %get-tuple-element.476.refs_2_), channel_id=1, source_target_pairs={{0,1},{3,2},{1,0},{2,3},{4,5},{7,6},{5,4},{6,7},{8,9},{11,10},{9,8... | collective-permute-start | bytes 1474568 | tf_op jit(solution)/shard_map/ppermute | solution.py:454
  112.0 12.8 %collective-permute-start.7 = (bf16[192,1280]{1,0:T(8,128)(2,1)}, bf16[192,1280]{1,0:T(8,128)(2,1)}, u32[]{:S(2)}, u32[]{:S(2)}) collective-permute-start(bf16[192,1280]{1,0:T(8,128)(2,1)} %get-tuple-element.471.refs_2_), channel_id=1, source_target_pairs={{1,2},{2,1},{5,6},{6,5},{9,10},{10,9},{13,14},{14,13},{17,18},{18,... | collective-permute-start | bytes 1474568 | tf_op jit(solution)/shard_map/ppermute | solution.py:450
  127.0 9.9 %collective-permute-start.8 = (bf16[192,1280]{1,0:T(8,128)(2,1)S(1)}, bf16[192,1280]{1,0:T(8,128)(2,1)S(1)}, u32[]{:S(2)}, u32[]{:S(2)}) collective-permute-start(bf16[192,1280]{1,0:T(8,128)(2,1)S(1)} %get-tuple-element.484.refs_2_), channel_id=1, source_target_pairs={{0,1},{3,2},{1,0},{2,3},{4,5},{7,6},{5,4},{6,7},{8,9},{11,10},{9,8... | collective-permute-start | bytes 1474568 | tf_op jit(solution)/shard_map/ppermute | solution.py:454
  147.6 12.5 %collective-permute-start.12 = (bf16[192,1280]{1,0:T(8,128)(2,1)S(1)}, bf16[192,1280]{1,0:T(8,128)(2,1)S(1)}, u32[]{:S(2)}, u32[]{:S(2)}) collective-permute-start(bf16[192,1280]{1,0:T(8,128)(2,1)S(1)} %get-tuple-element.500.refs_2_), channel_id=1, source_target_pairs={{0,1},{3,2},{1,0},{2,3},{4,5},{7,6},{5,4},{6,7},{8,9},{11,10},{9,8... | collective-permute-start | bytes 1474568 | tf_op jit(solution)/shard_map/ppermute | solution.py:454
  162.1 13.5 %collective-permute-start.14 = (bf16[192,1280]{1,0:T(8,128)(2,1)}, bf16[192,1280]{1,0:T(8,128)(2,1)}, u32[]{:S(2)}, u32[]{:S(2)}) collective-permute-start(bf16[192,1280]{1,0:T(8,128)(2,1)} %get-tuple-element.506.refs_2_), channel_id=1, source_target_pairs={{0,1},{3,2},{1,0},{2,3},{4,5},{7,6},{5,4},{6,7},{8,9},{11,10},{9,8... | collective-permute-start | bytes 1474568 | tf_op jit(solution)/shard_map/ppermute | solution.py:454
  163.7 11.9 %collective-permute-start.15 = (bf16[192,1280]{1,0:T(8,128)(2,1)}, bf16[192,1280]{1,0:T(8,128)(2,1)}, u32[]{:S(2)}, u32[]{:S(2)}) collective-permute-start(bf16[192,1280]{1,0:T(8,128)(2,1)} %get-tuple-element.501.refs_2_), channel_id=1, source_target_pairs={{1,2},{2,1},{5,6},{6,5},{9,10},{10,9},{13,14},{14,13},{17,18},{18,... | collective-permute-start | bytes 1474568 | tf_op jit(solution)/shard_map/ppermute | solution.py:450
  177.9 10.7 %collective-permute-start.17 = (bf16[192,1280]{1,0:T(8,128)(2,1)S(1)}, bf16[192,1280]{1,0:T(8,128)(2,1)S(1)}, u32[]{:S(2)}, u32[]{:S(2)}) collective-permute-start(bf16[192,1280]{1,0:T(8,128)(2,1)S(1)} %get-tuple-element.515.refs_2_), channel_id=1, source_target_pairs={{1,0},{2,3},{5,4},{6,7},{9,8},{10,11},{13,12},{14,15},{17,16},{18,... | collective-permute-start | bytes 1474568 | tf_op jit(solution)/shard_map/ppermute | solution.py:454
  183.0 18.6 %collective-permute-start.18 = (bf16[192,1280]{1,0:T(8,128)(2,1)S(1)}, bf16[192,1280]{1,0:T(8,128)(2,1)S(1)}, u32[]{:S(2)}, u32[]{:S(2)}) collective-permute-start(bf16[192,1280]{1,0:T(8,128)(2,1)S(1)} %turn.43.refs_2_), channel_id=1, source_target_pairs={{1,0},{2,3},{5,4},{6,7},{9,8},{10,11},{13,12},{14,15},{17,16},{18,... | collective-permute-start | bytes 1474568 | tf_op jit(solution)/shard_map/ppermute | solution.py:454
  216.5 11.7 %collective-permute-start.20 = (bf16[192,1280]{1,0:T(8,128)(2,1)S(1)}, bf16[192,1280]{1,0:T(8,128)(2,1)S(1)}, u32[]{:S(2)}, u32[]{:S(2)}) collective-permute-start(bf16[192,1280]{1,0:T(8,128)(2,1)S(1)} %get-tuple-element.527.refs_0_), channel_id=1, source_target_pairs={{0,1},{3,2},{4,5},{7,6},{8,9},{11,10},{12,13},{15,14},{16,17},{19,... | collective-permute-start | bytes 1474568 | tf_op jit(solution)/shard_map/ppermute | solution.py:454
  222.8 15.9 %collective-permute-start.21 = (bf16[192,1280]{1,0:T(8,128)(2,1)S(1)}, bf16[192,1280]{1,0:T(8,128)(2,1)S(1)}, u32[]{:S(2)}, u32[]{:S(2)}) collective-permute-start(bf16[192,1280]{1,0:T(8,128)(2,1)S(1)} %get-tuple-element.532.refs_0_), channel_id=1, source_target_pairs={{0,1},{3,2},{4,5},{7,6},{8,9},{11,10},{12,13},{15,14},{16,17},{19,... | collective-permute-start | bytes 1474568 | tf_op jit(solution)/shard_map/ppermute | solution.py:454
  228.2 10.5 %collective-permute-start.22 = (bf16[192,1280]{1,0:T(8,128)(2,1)S(1)}, bf16[192,1280]{1,0:T(8,128)(2,1)S(1)}, u32[]{:S(2)}, u32[]{:S(2)}) collective-permute-start(bf16[192,1280]{1,0:T(8,128)(2,1)S(1)} %turn.44.refs_2_), channel_id=1, source_target_pairs={{1,2},{2,1},{5,6},{6,5},{9,10},{10,9},{13,14},{14,13},{17,18},{18,... | collective-permute-start | bytes 1474568 | tf_op jit(solution)/shard_map/ppermute | solution.py:450
  238.8 13.6 %collective-permute-start.23 = (bf16[192,1280]{1,0:T(8,128)(2,1)S(1)}, bf16[192,1280]{1,0:T(8,128)(2,1)S(1)}, u32[]{:S(2)}, u32[]{:S(2)}) collective-permute-start(bf16[192,1280]{1,0:T(8,128)(2,1)S(1)} %get-tuple-element.547.refs_2_), channel_id=1, source_target_pairs={{0,1},{3,2},{1,0},{2,3},{4,5},{7,6},{5,4},{6,7},{8,9},{11,10},{9,8... | collective-permute-start | bytes 1474568 | tf_op jit(solution)/shard_map/ppermute | solution.py:454
  252.6 14.2 %collective-permute-start.25 = (bf16[192,1280]{1,0:T(8,128)(2,1)S(1)}, bf16[192,1280]{1,0:T(8,128)(2,1)S(1)}, u32[]{:S(2)}, u32[]{:S(2)}) collective-permute-start(bf16[192,1280]{1,0:T(8,128)(2,1)S(1)} %get-tuple-element.553.refs_2_), channel_id=1, source_target_pairs={{0,1},{3,2},{1,0},{2,3},{4,5},{7,6},{5,4},{6,7},{8,9},{11,10},{9,8... | collective-permute-start | bytes 1474568 | tf_op jit(solution)/shard_map/ppermute | solution.py:454
  255.7 11.1 %collective-permute-start.26 = (bf16[192,1280]{1,0:T(8,128)(2,1)S(1)}, bf16[192,1280]{1,0:T(8,128)(2,1)S(1)}, u32[]{:S(2)}, u32[]{:S(2)}) collective-permute-start(bf16[192,1280]{1,0:T(8,128)(2,1)S(1)} %get-tuple-element.548.refs_2_), channel_id=1, source_target_pairs={{1,2},{2,1},{5,6},{6,5},{9,10},{10,9},{13,14},{14,13},{17,18},{18,... | collective-permute-start | bytes 1474568 | tf_op jit(solution)/shard_map/ppermute | solution.py:450
  267.0 11.8 %collective-permute-start.27 = (bf16[192,1280]{1,0:T(8,128)(2,1)S(1)}, bf16[192,1280]{1,0:T(8,128)(2,1)S(1)}, u32[]{:S(2)}, u32[]{:S(2)}) collective-permute-start(bf16[192,1280]{1,0:T(8,128)(2,1)S(1)} %get-tuple-element.564.refs_2_), channel_id=1, source_target_pairs={{0,1},{3,2},{1,0},{2,3},{4,5},{7,6},{5,4},{6,7},{8,9},{11,10},{9,8... | collective-permute-start | bytes 1474568 | tf_op jit(solution)/shard_map/ppermute | solution.py:454
  268.8 10.0 %collective-permute-start.28 = (bf16[192,1280]{1,0:T(8,128)(2,1)S(1)}, bf16[192,1280]{1,0:T(8,128)(2,1)S(1)}, u32[]{:S(2)}, u32[]{:S(2)}) collective-permute-start(bf16[192,1280]{1,0:T(8,128)(2,1)S(1)} %get-tuple-element.554.refs_2_), channel_id=1, source_target_pairs={{1,2},{2,1},{5,6},{6,5},{9,10},{10,9},{13,14},{14,13},{17,18},{18,... | collective-permute-start | bytes 1474568 | tf_op jit(solution)/shard_map/ppermute | solution.py:450
  279.0 12.3 %collective-permute-start.29 = (bf16[192,1280]{1,0:T(8,128)(2,1)S(1)}, bf16[192,1280]{1,0:T(8,128)(2,1)S(1)}, u32[]{:S(2)}, u32[]{:S(2)}) collective-permute-start(bf16[192,1280]{1,0:T(8,128)(2,1)S(1)} %get-tuple-element.575.refs_2_), channel_id=1, source_target_pairs={{0,1},{3,2},{1,0},{2,3},{4,5},{7,6},{5,4},{6,7},{8,9},{11,10},{9,8... | collective-permute-start | bytes 1474568 | tf_op jit(solution)/shard_map/ppermute | solution.py:454
  281.3 10.0 %collective-permute-start.30 = (bf16[192,1280]{1,0:T(8,128)(2,1)S(1)}, bf16[192,1280]{1,0:T(8,128)(2,1)S(1)}, u32[]{:S(2)}, u32[]{:S(2)}) collective-permute-start(bf16[192,1280]{1,0:T(8,128)(2,1)S(1)} %get-tuple-element.565.refs_2_), channel_id=1, source_target_pairs={{1,2},{2,1},{5,6},{6,5},{9,10},{10,9},{13,14},{14,13},{17,18},{18,... | collective-permute-start | bytes 1474568 | tf_op jit(solution)/shard_map/ppermute | solution.py:450
  291.5 14.7 %collective-permute-start.31 = (bf16[192,1280]{1,0:T(8,128)(2,1)S(1)}, bf16[192,1280]{1,0:T(8,128)(2,1)S(1)}, u32[]{:S(2)}, u32[]{:S(2)}) collective-permute-start(bf16[192,1280]{1,0:T(8,128)(2,1)S(1)} %get-tuple-element.588.refs_2_), channel_id=1, source_target_pairs={{0,1},{3,2},{1,0},{2,3},{4,5},{7,6},{5,4},{6,7},{8,9},{11,10},{9,8... | collective-permute-start | bytes 1474568 | tf_op jit(solution)/shard_map/ppermute | solution.py:454
  293.2 12.9 %collective-permute-start.32 = (bf16[192,1280]{1,0:T(8,128)(2,1)S(1)}, bf16[192,1280]{1,0:T(8,128)(2,1)S(1)}, u32[]{:S(2)}, u32[]{:S(2)}) collective-permute-start(bf16[192,1280]{1,0:T(8,128)(2,1)S(1)} %get-tuple-element.576.refs_2_), channel_id=1, source_target_pairs={{1,2},{2,1},{5,6},{6,5},{9,10},{10,9},{13,14},{14,13},{17,18},{18,... | collective-permute-start | bytes 1474568 | tf_op jit(solution)/shard_map/ppermute | solution.py:450
  316.6 320.5 %reduce-scatter.9.cloned.1.call-start = ((), (), s32[]{:S(2)}) async-start(), calls=%async_computation.10 | async-start | bytes 3686400 | tf_op jit(solution)/shard_map/reduce_scatter | solution.py:563
  330.3 26.4 %collective-permute-start.36 = (bf16[192,1280]{1,0:T(8,128)(2,1)}, bf16[192,1280]{1,0:T(8,128)(2,1)}, u32[]{:S(2)}, u32[]{:S(2)}) collective-permute-start(bf16[192,1280]{1,0:T(8,128)(2,1)} %get-tuple-element.600.refs_2_), channel_id=1, source_target_pairs={{1,2},{2,1},{5,6},{6,5},{9,10},{10,9},{13,14},{14,13},{17,18},{18,... | collective-permute-start | bytes 1474568 | tf_op jit(solution)/shard_map/ppermute | solution.py:450
  346.2 10.4 %collective-permute-start.35 = (bf16[192,1280]{1,0:T(8,128)(2,1)}, bf16[192,1280]{1,0:T(8,128)(2,1)}, u32[]{:S(2)}, u32[]{:S(2)}) collective-permute-start(bf16[192,1280]{1,0:T(8,128)(2,1)} %get-tuple-element.610.refs_2_), channel_id=1, source_target_pairs={{0,1},{3,2},{1,0},{2,3},{4,5},{7,6},{5,4},{6,7},{8,9},{11,10},{9,8... | collective-permute-start | bytes 1474568 | tf_op jit(solution)/shard_map/ppermute | solution.py:454
  354.3 283.2 %reduce-scatter.7.cloned.1.call-start = ((), (), s32[]{:S(2)}) async-start(), calls=%async_computation.9 | async-start | bytes 3686400 | tf_op jit(solution)/shard_map/reduce_scatter | solution.py:563
  360.6 17.8 %collective-permute-start.37 = (bf16[192,1280]{1,0:T(8,128)(2,1)S(1)}, bf16[192,1280]{1,0:T(8,128)(2,1)S(1)}, u32[]{:S(2)}, u32[]{:S(2)}) collective-permute-start(bf16[192,1280]{1,0:T(8,128)(2,1)S(1)} %get-tuple-element.624.refs_2_), channel_id=1, source_target_pairs={{0,1},{3,2},{1,0},{2,3},{4,5},{7,6},{5,4},{6,7},{8,9},{11,10},{9,8... | collective-permute-start | bytes 1474568 | tf_op jit(solution)/shard_map/ppermute | solution.py:454
  362.1 16.2 %collective-permute-start.38 = (bf16[192,1280]{1,0:T(8,128)(2,1)S(1)}, bf16[192,1280]{1,0:T(8,128)(2,1)S(1)}, u32[]{:S(2)}, u32[]{:S(2)}) collective-permute-start(bf16[192,1280]{1,0:T(8,128)(2,1)S(1)} %get-tuple-element.612.refs_2_), channel_id=1, source_target_pairs={{1,2},{2,1},{5,6},{6,5},{9,10},{10,9},{13,14},{14,13},{17,18},{18,... | collective-permute-start | bytes 1474568 | tf_op jit(solution)/shard_map/ppermute | solution.py:450
  390.6 26.2 %collective-permute-start.41 = (bf16[2,768,512]{2,1,0:T(8,128)(2,1)S(1)}, bf16[2,768,512]{2,1,0:T(8,128)(2,1)S(1)}, u32[]{:S(2)}, u32[]{:S(2)}) collective-permute-start(bf16[2,768,512]{2,1,0:T(8,128)(2,1)S(1)} %get-tuple-element.646), channel_id=1, source_target_pairs={{0,4},{4,0},{1,5},{5,1},{2,6},{6,2},{3,7},{7,3},{8,12},{12,8},{9,1... | collective-permute-start | bytes 4718600 | tf_op jit(solution)/shard_map/ppermute | solution.py:746
  399.0 13.6 %collective-permute-start.39 = (bf16[192,1280]{1,0:T(8,128)(2,1)S(1)}, bf16[192,1280]{1,0:T(8,128)(2,1)S(1)}, u32[]{:S(2)}, u32[]{:S(2)}) collective-permute-start(bf16[192,1280]{1,0:T(8,128)(2,1)S(1)} %get-tuple-element.640.refs_2_), channel_id=1, source_target_pairs={{0,1},{3,2},{1,0},{2,3},{4,5},{7,6},{5,4},{6,7},{8,9},{11,10},{9,8... | collective-permute-start | bytes 1474568 | tf_op jit(solution)/shard_map/ppermute | solution.py:454
  401.1 11.5 %collective-permute-start.40 = (bf16[192,1280]{1,0:T(8,128)(2,1)S(1)}, bf16[192,1280]{1,0:T(8,128)(2,1)S(1)}, u32[]{:S(2)}, u32[]{:S(2)}) collective-permute-start(bf16[192,1280]{1,0:T(8,128)(2,1)S(1)} %get-tuple-element.626.refs_2_), channel_id=1, source_target_pairs={{1,2},{2,1},{5,6},{6,5},{9,10},{10,9},{13,14},{14,13},{17,18},{18,... | collective-permute-start | bytes 1474568 | tf_op jit(solution)/shard_map/ppermute | solution.py:450
  412.8 14.2 %collective-permute-start.42 = (bf16[192,1280]{1,0:T(8,128)(2,1)S(1)}, bf16[192,1280]{1,0:T(8,128)(2,1)S(1)}, u32[]{:S(2)}, u32[]{:S(2)}) collective-permute-start(bf16[192,1280]{1,0:T(8,128)(2,1)S(1)} %get-tuple-element.650.refs_2_), channel_id=1, source_target_pairs={{0,1},{3,2},{1,0},{2,3},{4,5},{7,6},{5,4},{6,7},{8,9},{11,10},{9,8... | collective-permute-start | bytes 1474568 | tf_op jit(solution)/shard_map/ppermute | solution.py:454
  416.1 10.8 %collective-permute-start.43 = (bf16[192,1280]{1,0:T(8,128)(2,1)S(1)}, bf16[192,1280]{1,0:T(8,128)(2,1)S(1)}, u32[]{:S(2)}, u32[]{:S(2)}) collective-permute-start(bf16[192,1280]{1,0:T(8,128)(2,1)S(1)} %get-tuple-element.642.refs_2_), channel_id=1, source_target_pairs={{1,2},{2,1},{5,6},{6,5},{9,10},{10,9},{13,14},{14,13},{17,18},{18,... | collective-permute-start | bytes 1474568 | tf_op jit(solution)/shard_map/ppermute | solution.py:450
  427.1 13.0 %collective-permute-start.44 = (bf16[192,1280]{1,0:T(8,128)(2,1)S(1)}, bf16[192,1280]{1,0:T(8,128)(2,1)S(1)}, u32[]{:S(2)}, u32[]{:S(2)}) collective-permute-start(bf16[192,1280]{1,0:T(8,128)(2,1)S(1)} %get-tuple-element.659.refs_2_), channel_id=1, source_target_pairs={{0,1},{3,2},{1,0},{2,3},{4,5},{7,6},{5,4},{6,7},{8,9},{11,10},{9,8... | collective-permute-start | bytes 1474568 | tf_op jit(solution)/shard_map/ppermute | solution.py:454
  440.3 12.1 %collective-permute-start.46 = (bf16[192,1280]{1,0:T(8,128)(2,1)S(1)}, bf16[192,1280]{1,0:T(8,128)(2,1)S(1)}, u32[]{:S(2)}, u32[]{:S(2)}) collective-permute-start(bf16[192,1280]{1,0:T(8,128)(2,1)S(1)} %get-tuple-element.668.refs_2_), channel_id=1, source_target_pairs={{0,1},{3,2},{1,0},{2,3},{4,5},{7,6},{5,4},{6,7},{8,9},{11,10},{9,8... | collective-permute-start | bytes 1474568 | tf_op jit(solution)/shard_map/ppermute | solution.py:454
  452.5 14.0 %collective-permute-start.49 = (bf16[192,1280]{1,0:T(8,128)(2,1)S(1)}, bf16[192,1280]{1,0:T(8,128)(2,1)S(1)}, u32[]{:S(2)}, u32[]{:S(2)}) collective-permute-start(bf16[192,1280]{1,0:T(8,128)(2,1)S(1)} %get-tuple-element.669.refs_2_), channel_id=1, source_target_pairs={{1,2},{2,1},{5,6},{6,5},{9,10},{10,9},{13,14},{14,13},{17,18},{18,... | collective-permute-start | bytes 1474568 | tf_op jit(solution)/shard_map/ppermute | solution.py:450
  453.8 12.8 %collective-permute-start.48 = (bf16[192,1280]{1,0:T(8,128)(2,1)S(1)}, bf16[192,1280]{1,0:T(8,128)(2,1)S(1)}, u32[]{:S(2)}, u32[]{:S(2)}) collective-permute-start(bf16[192,1280]{1,0:T(8,128)(2,1)S(1)} %get-tuple-element.677.refs_2_), channel_id=1, source_target_pairs={{0,1},{3,2},{1,0},{2,3},{4,5},{7,6},{5,4},{6,7},{8,9},{11,10},{9,8... | collective-permute-start | bytes 1474568 | tf_op jit(solution)/shard_map/ppermute | solution.py:454
  472.9 250.7 %reduce-scatter.17.cloned.1.call-start = ((), (), s32[]{:S(2)}) async-start(), calls=%async_computation.14 | async-start | bytes 3686400 | tf_op jit(solution)/shard_map/reduce_scatter | solution.py:563
  473.0 16.1 %collective-permute-start.50 = (bf16[192,1280]{1,0:T(8,128)(2,1)}, bf16[192,1280]{1,0:T(8,128)(2,1)S(1)}, u32[]{:S(2)}, u32[]{:S(2)}) collective-permute-start(bf16[192,1280]{1,0:T(8,128)(2,1)} %copy-done.186), channel_id=1, source_target_pairs={{0,1},{3,2},{1,0},{2,3},{4,5},{7,6},{5,4},{6,7},{8,9},{11,10},{9,8... | collective-permute-start | bytes 1474568 | tf_op jit(solution)/shard_map/ppermute | solution.py:454
  474.2 14.8 %collective-permute-start.51 = (bf16[192,1280]{1,0:T(8,128)(2,1)}, bf16[192,1280]{1,0:T(8,128)(2,1)S(1)}, u32[]{:S(2)}, u32[]{:S(2)}) collective-permute-start(bf16[192,1280]{1,0:T(8,128)(2,1)} %copy-done.190), channel_id=1, source_target_pairs={{1,2},{2,1},{5,6},{6,5},{9,10},{10,9},{13,14},{14,13},{17,18},{18,... | collective-permute-start | bytes 1474568 | tf_op jit(solution)/shard_map/ppermute | solution.py:450
  498.6 10.3 %collective-permute-start.54 = (bf16[192,1280]{1,0:T(8,128)(2,1)S(1)}, bf16[192,1280]{1,0:T(8,128)(2,1)S(1)}, u32[]{:S(2)}, u32[]{:S(2)}) collective-permute-start(bf16[192,1280]{1,0:T(8,128)(2,1)S(1)} %get-tuple-element.721.refs_2_), channel_id=1, source_target_pairs={{0,1},{3,2},{1,0},{2,3},{4,5},{7,6},{5,4},{6,7},{8,9},{11,10},{9,8... | collective-permute-start | bytes 1474568 | tf_op jit(solution)/shard_map/ppermute | solution.py:454
  509.8 11.5 %collective-permute-start.56 = (bf16[192,1280]{1,0:T(8,128)(2,1)S(1)}, bf16[192,1280]{1,0:T(8,128)(2,1)S(1)}, u32[]{:S(2)}, u32[]{:S(2)}) collective-permute-start(bf16[192,1280]{1,0:T(8,128)(2,1)S(1)} %get-tuple-element.735.refs_2_), channel_id=1, source_target_pairs={{0,1},{3,2},{1,0},{2,3},{4,5},{7,6},{5,4},{6,7},{8,9},{11,10},{9,8... | collective-permute-start | bytes 1474568 | tf_op jit(solution)/shard_map/ppermute | solution.py:454
  530.9 193.4 %reduce-scatter.15.cloned.1.call-start = ((), (), s32[]{:S(2)}) async-start(), calls=%async_computation.13 | async-start | bytes 3686400 | tf_op jit(solution)/shard_map/reduce_scatter | solution.py:563
  543.8 15.4 %collective-permute-start.60 = (bf16[192,1280]{1,0:T(8,128)(2,1)}, bf16[192,1280]{1,0:T(8,128)(2,1)}, u32[]{:S(2)}, u32[]{:S(2)}) collective-permute-start(bf16[192,1280]{1,0:T(8,128)(2,1)} %get-tuple-element.747.refs_0_), channel_id=1, source_target_pairs={{1,2},{2,1},{5,6},{6,5},{9,10},{10,9},{13,14},{14,13},{17,18},{18,... | collective-permute-start | bytes 1474568 | tf_op jit(solution)/shard_map/ppermute | solution.py:450
  553.6 22.3 %collective-permute-start.61 = (bf16[192,1280]{1,0:T(8,128)(2,1)}, bf16[192,1280]{1,0:T(8,128)(2,1)}, u32[]{:S(2)}, u32[]{:S(2)}) collective-permute-start(bf16[192,1280]{1,0:T(8,128)(2,1)} %get-tuple-element.763.refs_2_), channel_id=1, source_target_pairs={{1,0},{2,3},{5,4},{6,7},{9,8},{10,11},{13,12},{14,15},{17,16},{18,... | collective-permute-start | bytes 1474568 | tf_op jit(solution)/shard_map/ppermute | solution.py:454
  560.6 19.7 %collective-permute-start.62 = (bf16[192,1280]{1,0:T(8,128)(2,1)S(1)}, bf16[192,1280]{1,0:T(8,128)(2,1)S(1)}, u32[]{:S(2)}, u32[]{:S(2)}) collective-permute-start(bf16[192,1280]{1,0:T(8,128)(2,1)S(1)} %turn.64.refs_2_), channel_id=1, source_target_pairs={{1,0},{2,3},{5,4},{6,7},{9,8},{10,11},{13,12},{14,15},{17,16},{18,... | collective-permute-start | bytes 1474568 | tf_op jit(solution)/shard_map/ppermute | solution.py:454
  592.1 12.0 %collective-permute-start.63 = (bf16[2,768,512]{2,1,0:T(8,128)(2,1)S(1)}, bf16[2,768,512]{2,1,0:T(8,128)(2,1)S(1)}, u32[]{:S(2)}, u32[]{:S(2)}) collective-permute-start(bf16[2,768,512]{2,1,0:T(8,128)(2,1)S(1)} %get-tuple-element.787), channel_id=1, source_target_pairs={{0,4},{4,0},{1,5},{5,1},{2,6},{6,2},{3,7},{7,3},{8,12},{12,8},{9,1... | collective-permute-start | bytes 4718600 | tf_op jit(solution)/shard_map/ppermute | solution.py:746
  607.7 25.9 %collective-permute-start.65 = (bf16[192,1280]{1,0:T(8,128)(2,1)}, bf16[192,1280]{1,0:T(8,128)(2,1)}, u32[]{:S(2)}, u32[]{:S(2)}) collective-permute-start(bf16[192,1280]{1,0:T(8,128)(2,1)} %get-tuple-element.789.refs_0_), channel_id=1, source_target_pairs={{0,1},{3,2},{4,5},{7,6},{8,9},{11,10},{12,13},{15,14},{16,17},{19,... | collective-permute-start | bytes 1474568 | tf_op jit(solution)/shard_map/ppermute | solution.py:454
  618.4 108.7 %reduce-scatter.13.cloned.1.call-start = ((), (), s32[]{:S(2)}) async-start(), calls=%async_computation.12 | async-start | bytes 2048000 | tf_op jit(solution)/shard_map/reduce_scatter | solution.py:561
  631.5 16.8 %collective-permute-start.67 = (bf16[192,1280]{1,0:T(8,128)(2,1)}, bf16[192,1280]{1,0:T(8,128)(2,1)}, u32[]{:S(2)}, u32[]{:S(2)}) collective-permute-start(bf16[192,1280]{1,0:T(8,128)(2,1)} %get-tuple-element.794.refs_0_), channel_id=1, source_target_pairs={{0,1},{3,2},{4,5},{7,6},{8,9},{11,10},{12,13},{15,14},{16,17},{19,... | collective-permute-start | bytes 1474568 | tf_op jit(solution)/shard_map/ppermute | solution.py:454
  635.7 12.7 %collective-permute-start.68 = (bf16[192,1280]{1,0:T(8,128)(2,1)}, bf16[192,1280]{1,0:T(8,128)(2,1)}, u32[]{:S(2)}, u32[]{:S(2)}) collective-permute-start(bf16[192,1280]{1,0:T(8,128)(2,1)} %turn.65.refs_2_), channel_id=1, source_target_pairs={{1,2},{2,1},{5,6},{6,5},{9,10},{10,9},{13,14},{14,13},{17,18},{18,... | collective-permute-start | bytes 1474568 | tf_op jit(solution)/shard_map/ppermute | solution.py:450
  637.5 14.9 %collective-permute-start.69 = (bf16[160,1280]{1,0:T(8,128)(2,1)}, bf16[160,1280]{1,0:T(8,128)(2,1)}, u32[]{:S(2)}, u32[]{:S(2)}) collective-permute-start(bf16[160,1280]{1,0:T(8,128)(2,1)} %reduce-scatter.7.cloned.1.call-done), channel_id=1, source_target_pairs={{0,4},{4,0},{1,5},{5,1},{2,6},{6,2},{3,7},{7,3},{8,12},{12,8},{9,1... | collective-permute-start | bytes 1228808 | tf_op jit(solution)/shard_map/ppermute | solution.py:567
  650.2 13.2 %collective-permute-start.71 = (bf16[192,1280]{1,0:T(8,128)(2,1)S(1)}, bf16[192,1280]{1,0:T(8,128)(2,1)S(1)}, u32[]{:S(2)}, u32[]{:S(2)}) collective-permute-start(bf16[192,1280]{1,0:T(8,128)(2,1)S(1)} %get-tuple-element.802.refs_2_), channel_id=1, source_target_pairs={{1,2},{2,1},{5,6},{6,5},{9,10},{10,9},{13,14},{14,13},{17,18},{18,... | collective-permute-start | bytes 1474568 | tf_op jit(solution)/shard_map/ppermute | solution.py:450
  651.1 12.2 %collective-permute-start.70 = (bf16[192,1280]{1,0:T(8,128)(2,1)S(1)}, bf16[192,1280]{1,0:T(8,128)(2,1)S(1)}, u32[]{:S(2)}, u32[]{:S(2)}) collective-permute-start(bf16[192,1280]{1,0:T(8,128)(2,1)S(1)} %get-tuple-element.810.refs_2_), channel_id=1, source_target_pairs={{0,1},{3,2},{1,0},{2,3},{4,5},{7,6},{5,4},{6,7},{8,9},{11,10},{9,8... | collective-permute-start | bytes 1474568 | tf_op jit(solution)/shard_map/ppermute | solution.py:454
  677.2 12.8 %collective-permute-start.72 = (bf16[192,1280]{1,0:T(8,128)(2,1)}, bf16[192,1280]{1,0:T(8,128)(2,1)S(1)}, u32[]{:S(2)}, u32[]{:S(2)}) collective-permute-start(bf16[192,1280]{1,0:T(8,128)(2,1)} %copy-done.204), channel_id=1, source_target_pairs={{0,1},{3,2},{1,0},{2,3},{4,5},{7,6},{5,4},{6,7},{8,9},{11,10},{9,8... | collective-permute-start | bytes 1474568 | tf_op jit(solution)/shard_map/ppermute | solution.py:454
  678.6 11.5 %collective-permute-start.73 = (bf16[192,1280]{1,0:T(8,128)(2,1)S(1)}, bf16[192,1280]{1,0:T(8,128)(2,1)S(1)}, u32[]{:S(2)}, u32[]{:S(2)}) collective-permute-start(bf16[192,1280]{1,0:T(8,128)(2,1)S(1)} %get-tuple-element.811.refs_2_), channel_id=1, source_target_pairs={{1,2},{2,1},{5,6},{6,5},{9,10},{10,9},{13,14},{14,13},{17,18},{18,... | collective-permute-start | bytes 1474568 | tf_op jit(solution)/shard_map/ppermute | solution.py:450
  690.9 16.2 %collective-permute-start.75 = (bf16[192,1280]{1,0:T(8,128)(2,1)S(1)}, bf16[192,1280]{1,0:T(8,128)(2,1)S(1)}, u32[]{:S(2)}, u32[]{:S(2)}) collective-permute-start(bf16[192,1280]{1,0:T(8,128)(2,1)S(1)} %get-tuple-element.833.refs_2_), channel_id=1, source_target_pairs={{1,0},{2,3},{5,4},{6,7},{9,8},{10,11},{13,12},{14,15},{17,16},{18,... | collective-permute-start | bytes 1474568 | tf_op jit(solution)/shard_map/ppermute | solution.py:454
  694.1 23.0 %collective-permute-start.76 = (bf16[192,1280]{1,0:T(8,128)(2,1)S(1)}, bf16[192,1280]{1,0:T(8,128)(2,1)S(1)}, u32[]{:S(2)}, u32[]{:S(2)}) collective-permute-start(bf16[192,1280]{1,0:T(8,128)(2,1)S(1)} %turn.69.refs_2_), channel_id=1, source_target_pairs={{1,0},{2,3},{5,4},{6,7},{9,8},{10,11},{13,12},{14,15},{17,16},{18,... | collective-permute-start | bytes 1474568 | tf_op jit(solution)/shard_map/ppermute | solution.py:454
  (332 other events, 2020.1 us)
Sparse Core Ops, SparseCore 0:
  11.6 35.3 all-gather.3
  48.9 46.6 all-gather.5
  98.0 60.5 all-gather.7
  316.7 50.2 reduce-scatter.10
  370.8 46.8 reduce-scatter.8
  473.1 49.5 reduce-scatter.6
  531.0 54.5 reduce-scatter.16
  618.5 44.1 reduce-scatter.14
  677.3 29.3 reduce-scatter.12

commit v4 on v3

--- a/solution.py
+++ b/solution.py
@@ -829,17 +829,22 @@
                 endings.append(grad_up(layer))
             final = (c + 1) * CHUNK % BACK == 0
             if c < count - 1:
-                late_jobs[c] = flow.tick(late[c]) if layer == last else flow.tick()
+                if layer == last:
+                    late_jobs[c] = flow.tick(late[c])
+                elif layer == last - 1 and c == 0:
+                    late_jobs[-1] = flow.tick(late[-1])
+                else:
+                    flow.tick()
             if final:
                 sums = attend_back(layer, c * CHUNK // BACK, sums)
-        if layer == last:
-            late_jobs[-1] = flow.tick(late[-1])
         shared = share_back(sums)
         for c in each:
             jobs[c] = project_back(layer, c, shared)
-            if layer == last:
+            if layer == last and c < count - 1:
                 finish_output(layer, c, late_jobs[c])
-            elif endings and c < len(endings) - 2:
+            if layer == last - 1 and c == 0:
+                finish_output(last, count - 1, late_jobs[-1])
+            if layer < last and endings and c < len(endings) - 2:
                 endings[c]()
         endings.append(grad_attn(layer))
         for c in each:

time: 753 us -> 749 us (level)
    unnamed x606 -> x614, local copies, waits for them, and re-layouts: 113 us -> 112 us
  transfers between devices with their start and end apart: 93 -> 93, of which waited for: 30 -> 33; matrix products, arithmetic and copies ran while one was open for 6% -> 6% of each run, Pallas kernels for 30% -> 31%
where the time goes in v4:
time: 749 us; the launch traced here: 738 us
  Pallas kernels  239 us (32%)
  starting transfers between devices  158 us (21%)
  waiting for transfers between devices  155 us (21%)
  local copies, waits for them, and re-layouts  132 us (18%)
  matrix products  25.1 us (3%)
  between operations  18.7 us (2%)
  other arithmetic  10.6 us (1%)
    pallas_call x59, Pallas kernels, call(): pl.pallas_call(body, grid=grid, in_specs=specs, out_specs=[o[3] for o in...  183 us
    ppermute x38, waiting for transfers between devices, tick(): self.got = lax.ppermute(send if across else fresh, 'tp', perm)  115 us
    unnamed x614, local copies, waits for them, and re-layouts  112 us
    ppermute x38, starting transfers between devices, tick(): self.got = lax.ppermute(send if across else fresh, 'tp', perm)  97.6 us
    pallas_call x4, Pallas kernels, attend_back(): pl.pallas_call(body, grid=(heads,), in_specs=[v for _, v in everything],...  36.1 us
    ppermute x32, starting transfers between devices, tick(): self.there = lax.ppermute(pair, 'tp', [(1, 2), (2, 1)])  27.4 us
    dot_general x8, matrix products, weight_grad(): lax.dot_general(left, right, (((0,), (0,)), ((), ())), preferred_element_...  25.1 us
    all_gather x3, waiting for transfers between devices, fetch(): return lax.all_gather(w, ('fsdp', 'ctx'), axis=0, tiled=True)  23.4 us
  transfers between devices with their start and end apart: 93, of which 33 were waited for; matrix products, arithmetic and copies ran while one was open for 6% of the time, Pallas kernels for 31%

profile of v4, /device:TPU:1, one launch (start us, length us, event | category | flops | bytes accessed | tf_op | source)
XLA Modules:
  0.0 737.9 jit_solution(18019222296459271797)
XLA Ops:
  23.6 23.4 %all-gather.4.cloned.1.call-done.refs_7_.refs_6_ = bf16[1280,1280]{1,0:T(8,128)(2,1)} async-done(((bf16[160,1280]{1,0:T(8,128)(2,1)}), bf16[1280,1280]{1,0:T(8,128)(2,1)}) %all-gather.4.cloned.1.call-update) | async-done | bytes 3276816 | tf_op jit(solution)/shard_map/all_gather | solution.py:529
  61.5 3.2 collective-permute-done.refs_4_.refs_5_.refs_6_.refs_7_
  64.7 5.0 attend.8
  72.9 5.0 attend.9
  79.2 4.0 collective-permute-done.1.refs_1_
  84.1 5.0 attend.10
  89.1 4.6 collective-permute-done.2.refs_1_
  93.9 4.9 collective-permute-start.4
  99.5 5.0 attend.11
  108.8 3.2 collective-permute-start.6
  119.1 5.6 feed.8
  131.2 6.7 feed.9
  142.8 5.6 feed.10
  153.6 5.6 feed.11
  167.8 3.8 copy-done
  185.9 5.3 collective-permute-done.17.refs_1_
  193.3 11.0 %collective-permute-done.18.refs_1_ = bf16[192,1280]{1,0:T(8,128)(2,1)S(1)} collective-permute-done((bf16[192,1280]{1,0:T(8,128)(2,1)S(1)}, bf16[192,1280]{1,0:T(8,128)(2,1)S(1)}, u32[]{:S(2)}, u32[]{:S(2)}) %collective-permute-start.18) | collective-permute-done | bytes 491552 | tf_op jit(solution)/shard_map/ppermute | solution.py:454
  205.7 4.4 collective-permute-start.19
  213.1 5.0 attend.12
  219.5 5.0 attend.13
  225.8 4.0 collective-permute-done.20.refs_1_
  230.6 5.0 attend.14
  235.6 4.8 collective-permute-done.21.refs_1_
  240.5 4.7 collective-permute-start.23
  245.9 5.0 attend.15
  250.9 3.2 collective-permute-done.23.refs_1_
  254.3 3.1 collective-permute-start.25
  259.2 9.2 %feed.12 = (f32[192,1280]{1,0:T(8,128)S(1)}, bf16[192,1280]{1,0:T(8,128)(2,1)S(1)}, f32[192,128]{1,0:T(8,128)S(1)}, bf16[768,1280]{1,0:T(8,128)(2,1)S(1)}, bf16[...) custom-call(s32[1]{0:T(128)} %bitcast.refs_0_.edge_ref, ...), custom_call_target="tpu_custom_call" | custom-call | flops 125829120 | bytes 655360 | tf_op jit(solution)/shard_map/feed/pallas_call | solution.py:49
  271.6 9.2 %feed.13 = (f32[192,1280]{1,0:T(8,128)S(1)}, bf16[192,1280]{1,0:T(8,128)(2,1)S(1)}, f32[192,128]{1,0:T(8,128)S(1)}, bf16[768,1280]{1,0:T(8,128)(2,1)S(1)}, bf16[...) custom-call(s32[1]{0:T(128)} %bitcast.refs_0_.edge_ref, ...), custom_call_target="tpu_custom_call", output_to_operand_aliasing={{3}: (12, {}), {4}: (13, {}), {5}: (14, {}), {6}: (15, {})} | custom-call | flops 125829120 | bytes 655360 | tf_op jit(solution)/shard_map/feed/pallas_call | solution.py:49
  283.7 9.2 %feed.14 = (f32[192,1280]{1,0:T(8,128)S(1)}, bf16[192,1280]{1,0:T(8,128)(2,1)S(1)}, f32[192,128]{1,0:T(8,128)S(1)}, bf16[768,1280]{1,0:T(8,128)(2,1)S(1)}, bf16[...) custom-call(s32[1]{0:T(128)} %bitcast.refs_0_.edge_ref, ...), custom_call_target="tpu_custom_call", output_to_operand_aliasing={{3}: (12, {}), {4}: (13, {}), {5}: (14, {}), {6}: (15, {})} | custom-call | flops 125829120 | bytes 655360 | tf_op jit(solution)/shard_map/feed/pallas_call | solution.py:49
  296.3 9.2 %feed.15 = (f32[192,1280]{1,0:T(8,128)S(1)}, bf16[192,1280]{1,0:T(8,128)(2,1)S(1)}, f32[192,128]{1,0:T(8,128)S(1)}, bf16[768,1280]{1,0:T(8,128)(2,1)S(1)}, bf16[...) custom-call(s32[1]{0:T(128)} %bitcast.refs_0_.edge_ref, ...), custom_call_target="tpu_custom_call", output_to_operand_aliasing={{3}: (12, {}), {4}: (13, {}), {5}: (14, {}), {6}: (15, {})} | custom-call | flops 125829120 | bytes 655360 | tf_op jit(solution)/shard_map/feed/pallas_call | solution.py:49
  314.6 4.2 convolution_convert_fusion.3
  321.3 6.4 collective-permute-done.33.refs_1_
  333.4 4.2 copy-done.2
  348.0 4.2 collective-permute-start.35
  352.3 4.2 convolution_convert_fusion.2
  365.2 8.7 %attend_back.4 = (bf16[768,512]{1,0:T(8,128)(2,1)S(1)}, f32[768,512]{1,0:T(8,128)S(1)}, f32[768,512]{1,0:T(8,128)S(1)}, f32[768,512]{1,0:T(8,128)S(1)}, f32[768,512]{1,0:T(8,128)S(1)}) custom-call(s32[1]{0:T(128)} %bitcast.refs_0_.edge_ref, bf16[768,512]{1,0:T(8,128)(2,1)S(1)} %copy-done.45, bf16[768,512]{1,0:T(8,128)(2,1)S(1)} %copy-done.43, ...), custom_call_target="tpu_custom_call" | custom-call | flops 301989888 | bytes 1572864 | tf_op jit(solution)/shard_map/attend_back/pallas_call | solution.py:728
  374.0 3.8 copy-done.3
  383.4 9.4 %attend_back.5 = (bf16[768,512]{1,0:T(8,128)(2,1)S(1)}, f32[768,512]{1,0:T(8,128)S(1)}, f32[768,512]{1,0:T(8,128)S(1)}, bf16[2,768,512]{2,1,0:T(8,128)(2,1)S(1)}) custom-call(s32[1]{0:T(128)} %bitcast.refs_0_.edge_ref, bf16[768,512]{1,0:T(8,128)(2,1)S(1)} %copy-done.45, ...), custom_call_target="tpu_custom_call", output_to_operand_aliasing={{1}: (8, {}), {2}: (9, {}), {0}: (12, {})} | custom-call | flops 301989888 | bytes 1572864 | tf_op jit(solution)/shard_map/attend_back/pallas_call | solution.py:728
  392.8 8.4 %collective-permute-start.39 = (bf16[2,768,512]{2,1,0:T(8,128)(2,1)S(1)}, bf16[2,768,512]{2,1,0:T(8,128)(2,1)S(1)}, u32[]{:S(2)}, u32[]{:S(2)}) collective-permute-start(bf16[2,768,512]{2,1,0:T(8,128)(2,1)S(1)} %get-tuple-element.644), channel_id=1, source_target_pairs={{0,4},{4,0},{1,5},{5,1},{2,6},{6,2},{3,7},{7,3},{8,12},{12,8},{9,1... | collective-permute-start | bytes 4718600 | tf_op jit(solution)/shard_map/ppermute | solution.py:746
  405.6 8.9 %collective-permute-done.40.refs_1_ = bf16[192,1280]{1,0:T(8,128)(2,1)S(1)} collective-permute-done((bf16[192,1280]{1,0:T(8,128)(2,1)S(1)}, bf16[192,1280]{1,0:T(8,128)(2,1)S(1)}, u32[]{:S(2)}, u32[]{:S(2)}) %collective-permute-start.40) | collective-permute-done | bytes 491552 | tf_op jit(solution)/shard_map/ppermute | solution.py:454
  414.7 3.3 collective-permute-start.42
  420.3 8.5 %collective-permute-done.42.refs_1_ = bf16[192,1280]{1,0:T(8,128)(2,1)S(1)} collective-permute-done((bf16[192,1280]{1,0:T(8,128)(2,1)S(1)}, bf16[192,1280]{1,0:T(8,128)(2,1)S(1)}, u32[]{:S(2)}, u32[]{:S(2)}) %collective-permute-start.42) | collective-permute-done | bytes 491552 | tf_op jit(solution)/shard_map/ppermute | solution.py:454
  434.4 7.6 %collective-permute-done.44.refs_1_ = bf16[192,1280]{1,0:T(8,128)(2,1)S(1)} collective-permute-done((bf16[192,1280]{1,0:T(8,128)(2,1)S(1)}, bf16[192,1280]{1,0:T(8,128)(2,1)S(1)}, u32[]{:S(2)}, u32[]{:S(2)}) %collective-permute-start.44) | collective-permute-done | bytes 491552 | tf_op jit(solution)/shard_map/ppermute | solution.py:454
  443.5 5.2 collective-permute-start.46
  458.8 3.5 pad_maximum_fusion
  472.6 5.8 feed_back.4
  481.8 5.8 feed_back.5
  488.4 3.4 collective-permute-start.52
  492.7 5.9 feed_back.6
  502.6 5.8 feed_back.7
  515.1 4.2 convolution_convert_fusion.1
  522.9 5.7 collective-permute-done.56.refs_1_
  542.6 5.0 collective-permute-start.58
  547.5 4.2 convolution_convert_fusion
  564.0 8.7 %attend_back.6 = (bf16[768,512]{1,0:T(8,128)(2,1)S(1)}, f32[768,512]{1,0:T(8,128)S(1)}, f32[768,512]{1,0:T(8,128)S(1)}, f32[768,512]{1,0:T(8,128)S(1)}, f32[768,512]{1,0:T(8,128)S(1)}) custom-call(s32[1]{0:T(128)} %bitcast.refs_0_.edge_ref, bf16[768,512]{1,0:T(8,128)(2,1)S(1)} %copy-done.50, bf16[768,512]{1,0:T(8,128)(2,1)S(1)} %copy-done.47, ...), custom_call_target="tpu_custom_call" | custom-call | flops 301989888 | bytes 1572864 | tf_op jit(solution)/shard_map/attend_back/pallas_call | solution.py:728
  579.6 9.4 %attend_back.7 = (bf16[768,512]{1,0:T(8,128)(2,1)S(1)}, f32[768,512]{1,0:T(8,128)S(1)}, f32[768,512]{1,0:T(8,128)S(1)}, bf16[2,768,512]{2,1,0:T(8,128)(2,1)S(1)}) custom-call(s32[1]{0:T(128)} %bitcast.refs_0_.edge_ref, bf16[768,512]{1,0:T(8,128)(2,1)S(1)} %copy-done.51, ...), custom_call_target="tpu_custom_call", output_to_operand_aliasing={{1}: (8, {}), {2}: (9, {}), {0}: (12, {})} | custom-call | flops 301989888 | bytes 1572864 | tf_op jit(solution)/shard_map/attend_back/pallas_call | solution.py:728
  589.1 8.7 %collective-permute-start.62 = (bf16[2,768,512]{2,1,0:T(8,128)(2,1)S(1)}, bf16[2,768,512]{2,1,0:T(8,128)(2,1)S(1)}, u32[]{:S(2)}, u32[]{:S(2)}) collective-permute-start(bf16[2,768,512]{2,1,0:T(8,128)(2,1)S(1)} %get-tuple-element.784), channel_id=1, source_target_pairs={{0,4},{4,0},{1,5},{5,1},{2,6},{6,2},{3,7},{7,3},{8,12},{12,8},{9,1... | collective-permute-start | bytes 4718600 | tf_op jit(solution)/shard_map/ppermute | solution.py:746
  604.3 6.7 collective-permute-start.65
  619.5 3.7 finish.6.refs_3_
  666.7 3.3 collective-permute-done.80
  677.8 8.0 %collective-permute-done.72.refs_1_ = bf16[192,1280]{1,0:T(8,128)(2,1)S(1)} collective-permute-done((bf16[192,1280]{1,0:T(8,128)(2,1)}, bf16[192,1280]{1,0:T(8,128)(2,1)S(1)}, u32[]{:S(2)}, u32[]{:S(2)}) %collective-permute-start.72) | collective-permute-done | bytes 491552 | tf_op jit(solution)/shard_map/ppermute | solution.py:454
  691.6 11.0 %collective-permute-done.75.refs_1_ = bf16[192,1280]{1,0:T(8,128)(2,1)S(1)} collective-permute-done((bf16[192,1280]{1,0:T(8,128)(2,1)S(1)}, bf16[192,1280]{1,0:T(8,128)(2,1)S(1)}, u32[]{:S(2)}, u32[]{:S(2)}) %collective-permute-start.75) | collective-permute-done | bytes 491552 | tf_op jit(solution)/shard_map/ppermute | solution.py:454
  704.4 8.5 %collective-permute-done.76.refs_1_ = bf16[192,1280]{1,0:T(8,128)(2,1)S(1)} collective-permute-done((bf16[192,1280]{1,0:T(8,128)(2,1)S(1)}, bf16[192,1280]{1,0:T(8,128)(2,1)S(1)}, u32[]{:S(2)}, u32[]{:S(2)}) %collective-permute-start.76) | collective-permute-done | bytes 491552 | tf_op jit(solution)/shard_map/ppermute | solution.py:454
  (898 shorter events, 327.4 us)
Async XLA Ops:
  7.2 39.8 %all-gather.4.cloned.1.call-start = ((), (), s32[]{:S(2)}) async-start(), calls=%async_computation.6 | async-start | bytes 3686400 | tf_op jit(solution)/shard_map/all_gather | solution.py:529
  11.5 102.6 %all-gather.6.cloned.1.call-start = ((), (), s32[]{:S(2)}) async-start(), calls=%async_computation.7 | async-start | bytes 7372800 | tf_op jit(solution)/shard_map/all_gather | solution.py:529
  15.6 152.2 %all-gather.8.cloned.1.call-start = ((), (), s32[]{:S(2)}) async-start(), calls=%async_computation.8 | async-start | bytes 11059200 | tf_op jit(solution)/shard_map/all_gather | solution.py:529
  19.9 591.1 %reduce-scatter.11.cloned.1.call-start = ((), (), s32[]{:S(2)}) async-start(), calls=%async_computation.11 | async-start | bytes 3686400 | tf_op jit(solution)/shard_map/reduce_scatter | solution.py:563
  69.7 13.5 %collective-permute-start.1 = (bf16[192,1280]{1,0:T(8,128)(2,1)S(1)}, bf16[192,1280]{1,0:T(8,128)(2,1)S(1)}, u32[]{:S(2)}, u32[]{:S(2)}) collective-permute-start(bf16[192,1280]{1,0:T(8,128)(2,1)S(1)} %get-tuple-element.450.refs_0_), channel_id=1, source_target_pairs={{0,1},{3,2},{4,5},{7,6},{8,9},{11,10},{12,13},{15,14},{16,17},{19,... | collective-permute-start | bytes 1474568 | tf_op jit(solution)/shard_map/ppermute | solution.py:454
  77.8 15.9 %collective-permute-start.2 = (bf16[192,1280]{1,0:T(8,128)(2,1)S(1)}, bf16[192,1280]{1,0:T(8,128)(2,1)S(1)}, u32[]{:S(2)}, u32[]{:S(2)}) collective-permute-start(bf16[192,1280]{1,0:T(8,128)(2,1)S(1)} %get-tuple-element.455.refs_0_), channel_id=1, source_target_pairs={{0,1},{3,2},{4,5},{7,6},{8,9},{11,10},{12,13},{15,14},{16,17},{19,... | collective-permute-start | bytes 1474568 | tf_op jit(solution)/shard_map/ppermute | solution.py:454
  83.2 10.5 %collective-permute-start.3 = (bf16[192,1280]{1,0:T(8,128)(2,1)S(1)}, bf16[192,1280]{1,0:T(8,128)(2,1)S(1)}, u32[]{:S(2)}, u32[]{:S(2)}) collective-permute-start(bf16[192,1280]{1,0:T(8,128)(2,1)S(1)} %turn.35.refs_2_), channel_id=1, source_target_pairs={{1,2},{2,1},{5,6},{6,5},{9,10},{10,9},{13,14},{14,13},{17,18},{18,... | collective-permute-start | bytes 1474568 | tf_op jit(solution)/shard_map/ppermute | solution.py:450
  93.9 13.8 %collective-permute-start.4 = (bf16[192,1280]{1,0:T(8,128)(2,1)S(1)}, bf16[192,1280]{1,0:T(8,128)(2,1)S(1)}, u32[]{:S(2)}, u32[]{:S(2)}) collective-permute-start(bf16[192,1280]{1,0:T(8,128)(2,1)S(1)} %get-tuple-element.470.refs_2_), channel_id=1, source_target_pairs={{0,1},{3,2},{1,0},{2,3},{4,5},{7,6},{5,4},{6,7},{8,9},{11,10},{9,8... | collective-permute-start | bytes 1474568 | tf_op jit(solution)/shard_map/ppermute | solution.py:454
  108.8 17.5 %collective-permute-start.6 = (bf16[192,1280]{1,0:T(8,128)(2,1)}, bf16[192,1280]{1,0:T(8,128)(2,1)}, u32[]{:S(2)}, u32[]{:S(2)}) collective-permute-start(bf16[192,1280]{1,0:T(8,128)(2,1)} %get-tuple-element.476.refs_2_), channel_id=1, source_target_pairs={{0,1},{3,2},{1,0},{2,3},{4,5},{7,6},{5,4},{6,7},{8,9},{11,10},{9,8... | collective-permute-start | bytes 1474568 | tf_op jit(solution)/shard_map/ppermute | solution.py:454
  112.0 14.4 %collective-permute-start.7 = (bf16[192,1280]{1,0:T(8,128)(2,1)}, bf16[192,1280]{1,0:T(8,128)(2,1)}, u32[]{:S(2)}, u32[]{:S(2)}) collective-permute-start(bf16[192,1280]{1,0:T(8,128)(2,1)} %get-tuple-element.471.refs_2_), channel_id=1, source_target_pairs={{1,2},{2,1},{5,6},{6,5},{9,10},{10,9},{13,14},{14,13},{17,18},{18,... | collective-permute-start | bytes 1474568 | tf_op jit(solution)/shard_map/ppermute | solution.py:450
  128.3 10.5 %collective-permute-start.8 = (bf16[192,1280]{1,0:T(8,128)(2,1)S(1)}, bf16[192,1280]{1,0:T(8,128)(2,1)S(1)}, u32[]{:S(2)}, u32[]{:S(2)}) collective-permute-start(bf16[192,1280]{1,0:T(8,128)(2,1)S(1)} %get-tuple-element.484.refs_2_), channel_id=1, source_target_pairs={{0,1},{3,2},{1,0},{2,3},{4,5},{7,6},{5,4},{6,7},{8,9},{11,10},{9,8... | collective-permute-start | bytes 1474568 | tf_op jit(solution)/shard_map/ppermute | solution.py:454
  139.1 10.5 %collective-permute-start.10 = (bf16[192,1280]{1,0:T(8,128)(2,1)S(1)}, bf16[192,1280]{1,0:T(8,128)(2,1)S(1)}, u32[]{:S(2)}, u32[]{:S(2)}) collective-permute-start(bf16[192,1280]{1,0:T(8,128)(2,1)S(1)} %get-tuple-element.492.refs_2_), channel_id=1, source_target_pairs={{0,1},{3,2},{1,0},{2,3},{4,5},{7,6},{5,4},{6,7},{8,9},{11,10},{9,8... | collective-permute-start | bytes 1474568 | tf_op jit(solution)/shard_map/ppermute | solution.py:454
  150.2 12.4 %collective-permute-start.12 = (bf16[192,1280]{1,0:T(8,128)(2,1)S(1)}, bf16[192,1280]{1,0:T(8,128)(2,1)S(1)}, u32[]{:S(2)}, u32[]{:S(2)}) collective-permute-start(bf16[192,1280]{1,0:T(8,128)(2,1)S(1)} %get-tuple-element.501.refs_2_), channel_id=1, source_target_pairs={{0,1},{3,2},{1,0},{2,3},{4,5},{7,6},{5,4},{6,7},{8,9},{11,10},{9,8... | collective-permute-start | bytes 1474568 | tf_op jit(solution)/shard_map/ppermute | solution.py:454
  164.4 13.2 %collective-permute-start.14 = (bf16[192,1280]{1,0:T(8,128)(2,1)}, bf16[192,1280]{1,0:T(8,128)(2,1)}, u32[]{:S(2)}, u32[]{:S(2)}) collective-permute-start(bf16[192,1280]{1,0:T(8,128)(2,1)} %get-tuple-element.507.refs_2_), channel_id=1, source_target_pairs={{0,1},{3,2},{1,0},{2,3},{4,5},{7,6},{5,4},{6,7},{8,9},{11,10},{9,8... | collective-permute-start | bytes 1474568 | tf_op jit(solution)/shard_map/ppermute | solution.py:454
  165.7 12.0 %collective-permute-start.15 = (bf16[192,1280]{1,0:T(8,128)(2,1)}, bf16[192,1280]{1,0:T(8,128)(2,1)}, u32[]{:S(2)}, u32[]{:S(2)}) collective-permute-start(bf16[192,1280]{1,0:T(8,128)(2,1)} %get-tuple-element.502.refs_2_), channel_id=1, source_target_pairs={{1,2},{2,1},{5,6},{6,5},{9,10},{10,9},{13,14},{14,13},{17,18},{18,... | collective-permute-start | bytes 1474568 | tf_op jit(solution)/shard_map/ppermute | solution.py:450
  180.3 10.9 %collective-permute-start.17 = (bf16[192,1280]{1,0:T(8,128)(2,1)S(1)}, bf16[192,1280]{1,0:T(8,128)(2,1)S(1)}, u32[]{:S(2)}, u32[]{:S(2)}) collective-permute-start(bf16[192,1280]{1,0:T(8,128)(2,1)S(1)} %get-tuple-element.516.refs_2_), channel_id=1, source_target_pairs={{1,0},{2,3},{5,4},{6,7},{9,8},{10,11},{13,12},{14,15},{17,16},{18,... | collective-permute-start | bytes 1474568 | tf_op jit(solution)/shard_map/ppermute | solution.py:454
  184.5 19.8 %collective-permute-start.18 = (bf16[192,1280]{1,0:T(8,128)(2,1)S(1)}, bf16[192,1280]{1,0:T(8,128)(2,1)S(1)}, u32[]{:S(2)}, u32[]{:S(2)}) collective-permute-start(bf16[192,1280]{1,0:T(8,128)(2,1)S(1)} %turn.43.refs_2_), channel_id=1, source_target_pairs={{1,0},{2,3},{5,4},{6,7},{9,8},{10,11},{13,12},{14,15},{17,16},{18,... | collective-permute-start | bytes 1474568 | tf_op jit(solution)/shard_map/ppermute | solution.py:454
  218.1 11.7 %collective-permute-start.20 = (bf16[192,1280]{1,0:T(8,128)(2,1)S(1)}, bf16[192,1280]{1,0:T(8,128)(2,1)S(1)}, u32[]{:S(2)}, u32[]{:S(2)}) collective-permute-start(bf16[192,1280]{1,0:T(8,128)(2,1)S(1)} %get-tuple-element.528.refs_0_), channel_id=1, source_target_pairs={{0,1},{3,2},{4,5},{7,6},{8,9},{11,10},{12,13},{15,14},{16,17},{19,... | collective-permute-start | bytes 1474568 | tf_op jit(solution)/shard_map/ppermute | solution.py:454
  224.5 15.9 %collective-permute-start.21 = (bf16[192,1280]{1,0:T(8,128)(2,1)S(1)}, bf16[192,1280]{1,0:T(8,128)(2,1)S(1)}, u32[]{:S(2)}, u32[]{:S(2)}) collective-permute-start(bf16[192,1280]{1,0:T(8,128)(2,1)S(1)} %get-tuple-element.533.refs_0_), channel_id=1, source_target_pairs={{0,1},{3,2},{4,5},{7,6},{8,9},{11,10},{12,13},{15,14},{16,17},{19,... | collective-permute-start | bytes 1474568 | tf_op jit(solution)/shard_map/ppermute | solution.py:454
  229.9 10.5 %collective-permute-start.22 = (bf16[192,1280]{1,0:T(8,128)(2,1)S(1)}, bf16[192,1280]{1,0:T(8,128)(2,1)S(1)}, u32[]{:S(2)}, u32[]{:S(2)}) collective-permute-start(bf16[192,1280]{1,0:T(8,128)(2,1)S(1)} %turn.44.refs_2_), channel_id=1, source_target_pairs={{1,2},{2,1},{5,6},{6,5},{9,10},{10,9},{13,14},{14,13},{17,18},{18,... | collective-permute-start | bytes 1474568 | tf_op jit(solution)/shard_map/ppermute | solution.py:450
  240.5 13.6 %collective-permute-start.23 = (bf16[192,1280]{1,0:T(8,128)(2,1)S(1)}, bf16[192,1280]{1,0:T(8,128)(2,1)S(1)}, u32[]{:S(2)}, u32[]{:S(2)}) collective-permute-start(bf16[192,1280]{1,0:T(8,128)(2,1)S(1)} %get-tuple-element.548.refs_2_), channel_id=1, source_target_pairs={{0,1},{3,2},{1,0},{2,3},{4,5},{7,6},{5,4},{6,7},{8,9},{11,10},{9,8... | collective-permute-start | bytes 1474568 | tf_op jit(solution)/shard_map/ppermute | solution.py:454
  254.3 14.2 %collective-permute-start.25 = (bf16[192,1280]{1,0:T(8,128)(2,1)S(1)}, bf16[192,1280]{1,0:T(8,128)(2,1)S(1)}, u32[]{:S(2)}, u32[]{:S(2)}) collective-permute-start(bf16[192,1280]{1,0:T(8,128)(2,1)S(1)} %get-tuple-element.554.refs_2_), channel_id=1, source_target_pairs={{0,1},{3,2},{1,0},{2,3},{4,5},{7,6},{5,4},{6,7},{8,9},{11,10},{9,8... | collective-permute-start | bytes 1474568 | tf_op jit(solution)/shard_map/ppermute | solution.py:454
  257.4 11.1 %collective-permute-start.26 = (bf16[192,1280]{1,0:T(8,128)(2,1)S(1)}, bf16[192,1280]{1,0:T(8,128)(2,1)S(1)}, u32[]{:S(2)}, u32[]{:S(2)}) collective-permute-start(bf16[192,1280]{1,0:T(8,128)(2,1)S(1)} %get-tuple-element.549.refs_2_), channel_id=1, source_target_pairs={{1,2},{2,1},{5,6},{6,5},{9,10},{10,9},{13,14},{14,13},{17,18},{18,... | collective-permute-start | bytes 1474568 | tf_op jit(solution)/shard_map/ppermute | solution.py:450
  268.7 12.2 %collective-permute-start.27 = (bf16[192,1280]{1,0:T(8,128)(2,1)S(1)}, bf16[192,1280]{1,0:T(8,128)(2,1)S(1)}, u32[]{:S(2)}, u32[]{:S(2)}) collective-permute-start(bf16[192,1280]{1,0:T(8,128)(2,1)S(1)} %get-tuple-element.565.refs_2_), channel_id=1, source_target_pairs={{0,1},{3,2},{1,0},{2,3},{4,5},{7,6},{5,4},{6,7},{8,9},{11,10},{9,8... | collective-permute-start | bytes 1474568 | tf_op jit(solution)/shard_map/ppermute | solution.py:454
  281.1 11.8 %collective-permute-start.29 = (bf16[192,1280]{1,0:T(8,128)(2,1)S(1)}, bf16[192,1280]{1,0:T(8,128)(2,1)S(1)}, u32[]{:S(2)}, u32[]{:S(2)}) collective-permute-start(bf16[192,1280]{1,0:T(8,128)(2,1)S(1)} %get-tuple-element.576.refs_2_), channel_id=1, source_target_pairs={{0,1},{3,2},{1,0},{2,3},{4,5},{7,6},{5,4},{6,7},{8,9},{11,10},{9,8... | collective-permute-start | bytes 1474568 | tf_op jit(solution)/shard_map/ppermute | solution.py:454
  283.0 10.0 %collective-permute-start.30 = (bf16[192,1280]{1,0:T(8,128)(2,1)S(1)}, bf16[192,1280]{1,0:T(8,128)(2,1)S(1)}, u32[]{:S(2)}, u32[]{:S(2)}) collective-permute-start(bf16[192,1280]{1,0:T(8,128)(2,1)S(1)} %get-tuple-element.566.refs_2_), channel_id=1, source_target_pairs={{1,2},{2,1},{5,6},{6,5},{9,10},{10,9},{13,14},{14,13},{17,18},{18,... | collective-permute-start | bytes 1474568 | tf_op jit(solution)/shard_map/ppermute | solution.py:450
  293.2 15.1 %collective-permute-start.31 = (bf16[192,1280]{1,0:T(8,128)(2,1)S(1)}, bf16[192,1280]{1,0:T(8,128)(2,1)S(1)}, u32[]{:S(2)}, u32[]{:S(2)}) collective-permute-start(bf16[192,1280]{1,0:T(8,128)(2,1)S(1)} %get-tuple-element.589.refs_2_), channel_id=1, source_target_pairs={{0,1},{3,2},{1,0},{2,3},{4,5},{7,6},{5,4},{6,7},{8,9},{11,10},{9,8... | collective-permute-start | bytes 1474568 | tf_op jit(solution)/shard_map/ppermute | solution.py:454
  295.4 12.9 %collective-permute-start.32 = (bf16[192,1280]{1,0:T(8,128)(2,1)S(1)}, bf16[192,1280]{1,0:T(8,128)(2,1)S(1)}, u32[]{:S(2)}, u32[]{:S(2)}) collective-permute-start(bf16[192,1280]{1,0:T(8,128)(2,1)S(1)} %get-tuple-element.577.refs_2_), channel_id=1, source_target_pairs={{1,2},{2,1},{5,6},{6,5},{9,10},{10,9},{13,14},{14,13},{17,18},{18,... | collective-permute-start | bytes 1474568 | tf_op jit(solution)/shard_map/ppermute | solution.py:450
  318.8 313.6 %reduce-scatter.9.cloned.1.call-start = ((), (), s32[]{:S(2)}) async-start(), calls=%async_computation.10 | async-start | bytes 3686400 | tf_op jit(solution)/shard_map/reduce_scatter | solution.py:563
  332.0 26.8 %collective-permute-start.36 = (bf16[192,1280]{1,0:T(8,128)(2,1)}, bf16[192,1280]{1,0:T(8,128)(2,1)}, u32[]{:S(2)}, u32[]{:S(2)}) collective-permute-start(bf16[192,1280]{1,0:T(8,128)(2,1)} %get-tuple-element.601.refs_2_), channel_id=1, source_target_pairs={{1,2},{2,1},{5,6},{6,5},{9,10},{10,9},{13,14},{14,13},{17,18},{18,... | collective-permute-start | bytes 1474568 | tf_op jit(solution)/shard_map/ppermute | solution.py:450
  348.0 10.8 %collective-permute-start.35 = (bf16[192,1280]{1,0:T(8,128)(2,1)}, bf16[192,1280]{1,0:T(8,128)(2,1)}, u32[]{:S(2)}, u32[]{:S(2)}) collective-permute-start(bf16[192,1280]{1,0:T(8,128)(2,1)} %get-tuple-element.611.refs_2_), channel_id=1, source_target_pairs={{0,1},{3,2},{1,0},{2,3},{4,5},{7,6},{5,4},{6,7},{8,9},{11,10},{9,8... | collective-permute-start | bytes 1474568 | tf_op jit(solution)/shard_map/ppermute | solution.py:454
  356.5 276.4 %reduce-scatter.7.cloned.1.call-start = ((), (), s32[]{:S(2)}) async-start(), calls=%async_computation.9 | async-start | bytes 3686400 | tf_op jit(solution)/shard_map/reduce_scatter | solution.py:563
  362.7 17.8 %collective-permute-start.37 = (bf16[192,1280]{1,0:T(8,128)(2,1)S(1)}, bf16[192,1280]{1,0:T(8,128)(2,1)S(1)}, u32[]{:S(2)}, u32[]{:S(2)}) collective-permute-start(bf16[192,1280]{1,0:T(8,128)(2,1)S(1)} %get-tuple-element.625.refs_2_), channel_id=1, source_target_pairs={{0,1},{3,2},{1,0},{2,3},{4,5},{7,6},{5,4},{6,7},{8,9},{11,10},{9,8... | collective-permute-start | bytes 1474568 | tf_op jit(solution)/shard_map/ppermute | solution.py:454
  364.3 16.2 %collective-permute-start.38 = (bf16[192,1280]{1,0:T(8,128)(2,1)S(1)}, bf16[192,1280]{1,0:T(8,128)(2,1)S(1)}, u32[]{:S(2)}, u32[]{:S(2)}) collective-permute-start(bf16[192,1280]{1,0:T(8,128)(2,1)S(1)} %get-tuple-element.613.refs_2_), channel_id=1, source_target_pairs={{1,2},{2,1},{5,6},{6,5},{9,10},{10,9},{13,14},{14,13},{17,18},{18,... | collective-permute-start | bytes 1474568 | tf_op jit(solution)/shard_map/ppermute | solution.py:450
  392.8 11.4 %collective-permute-start.39 = (bf16[2,768,512]{2,1,0:T(8,128)(2,1)S(1)}, bf16[2,768,512]{2,1,0:T(8,128)(2,1)S(1)}, u32[]{:S(2)}, u32[]{:S(2)}) collective-permute-start(bf16[2,768,512]{2,1,0:T(8,128)(2,1)S(1)} %get-tuple-element.644), channel_id=1, source_target_pairs={{0,4},{4,0},{1,5},{5,1},{2,6},{6,2},{3,7},{7,3},{8,12},{12,8},{9,1... | collective-permute-start | bytes 4718600 | tf_op jit(solution)/shard_map/ppermute | solution.py:746
  401.2 13.4 %collective-permute-start.40 = (bf16[192,1280]{1,0:T(8,128)(2,1)S(1)}, bf16[192,1280]{1,0:T(8,128)(2,1)S(1)}, u32[]{:S(2)}, u32[]{:S(2)}) collective-permute-start(bf16[192,1280]{1,0:T(8,128)(2,1)S(1)} %get-tuple-element.648.refs_2_), channel_id=1, source_target_pairs={{0,1},{3,2},{1,0},{2,3},{4,5},{7,6},{5,4},{6,7},{8,9},{11,10},{9,8... | collective-permute-start | bytes 1474568 | tf_op jit(solution)/shard_map/ppermute | solution.py:454
  403.0 11.5 %collective-permute-start.41 = (bf16[192,1280]{1,0:T(8,128)(2,1)S(1)}, bf16[192,1280]{1,0:T(8,128)(2,1)S(1)}, u32[]{:S(2)}, u32[]{:S(2)}) collective-permute-start(bf16[192,1280]{1,0:T(8,128)(2,1)S(1)} %get-tuple-element.627.refs_2_), channel_id=1, source_target_pairs={{1,2},{2,1},{5,6},{6,5},{9,10},{10,9},{13,14},{14,13},{17,18},{18,... | collective-permute-start | bytes 1474568 | tf_op jit(solution)/shard_map/ppermute | solution.py:450
  414.7 14.2 %collective-permute-start.42 = (bf16[192,1280]{1,0:T(8,128)(2,1)S(1)}, bf16[192,1280]{1,0:T(8,128)(2,1)S(1)}, u32[]{:S(2)}, u32[]{:S(2)}) collective-permute-start(bf16[192,1280]{1,0:T(8,128)(2,1)S(1)} %get-tuple-element.657.refs_2_), channel_id=1, source_target_pairs={{0,1},{3,2},{1,0},{2,3},{4,5},{7,6},{5,4},{6,7},{8,9},{11,10},{9,8... | collective-permute-start | bytes 1474568 | tf_op jit(solution)/shard_map/ppermute | solution.py:454
  418.0 10.8 %collective-permute-start.43 = (bf16[192,1280]{1,0:T(8,128)(2,1)S(1)}, bf16[192,1280]{1,0:T(8,128)(2,1)S(1)}, u32[]{:S(2)}, u32[]{:S(2)}) collective-permute-start(bf16[192,1280]{1,0:T(8,128)(2,1)S(1)} %get-tuple-element.649.refs_2_), channel_id=1, source_target_pairs={{1,2},{2,1},{5,6},{6,5},{9,10},{10,9},{13,14},{14,13},{17,18},{18,... | collective-permute-start | bytes 1474568 | tf_op jit(solution)/shard_map/ppermute | solution.py:450
  429.0 13.0 %collective-permute-start.44 = (bf16[192,1280]{1,0:T(8,128)(2,1)S(1)}, bf16[192,1280]{1,0:T(8,128)(2,1)S(1)}, u32[]{:S(2)}, u32[]{:S(2)}) collective-permute-start(bf16[192,1280]{1,0:T(8,128)(2,1)S(1)} %get-tuple-element.666.refs_2_), channel_id=1, source_target_pairs={{0,1},{3,2},{1,0},{2,3},{4,5},{7,6},{5,4},{6,7},{8,9},{11,10},{9,8... | collective-permute-start | bytes 1474568 | tf_op jit(solution)/shard_map/ppermute | solution.py:454
  442.2 15.2 %collective-permute-start.47 = (bf16[192,1280]{1,0:T(8,128)(2,1)S(1)}, bf16[192,1280]{1,0:T(8,128)(2,1)S(1)}, u32[]{:S(2)}, u32[]{:S(2)}) collective-permute-start(bf16[192,1280]{1,0:T(8,128)(2,1)S(1)} %get-tuple-element.667.refs_2_), channel_id=1, source_target_pairs={{1,2},{2,1},{5,6},{6,5},{9,10},{10,9},{13,14},{14,13},{17,18},{18,... | collective-permute-start | bytes 1474568 | tf_op jit(solution)/shard_map/ppermute | solution.py:450
  443.5 13.9 %collective-permute-start.46 = (bf16[192,1280]{1,0:T(8,128)(2,1)S(1)}, bf16[192,1280]{1,0:T(8,128)(2,1)S(1)}, u32[]{:S(2)}, u32[]{:S(2)}) collective-permute-start(bf16[192,1280]{1,0:T(8,128)(2,1)S(1)} %get-tuple-element.675.refs_2_), channel_id=1, source_target_pairs={{0,1},{3,2},{1,0},{2,3},{4,5},{7,6},{5,4},{6,7},{8,9},{11,10},{9,8... | collective-permute-start | bytes 1474568 | tf_op jit(solution)/shard_map/ppermute | solution.py:454
  462.3 257.7 %reduce-scatter.17.cloned.1.call-start = ((), (), s32[]{:S(2)}) async-start(), calls=%async_computation.14 | async-start | bytes 3686400 | tf_op jit(solution)/shard_map/reduce_scatter | solution.py:563
  462.4 16.1 %collective-permute-start.48 = (bf16[192,1280]{1,0:T(8,128)(2,1)}, bf16[192,1280]{1,0:T(8,128)(2,1)S(1)}, u32[]{:S(2)}, u32[]{:S(2)}) collective-permute-start(bf16[192,1280]{1,0:T(8,128)(2,1)} %copy-done.192), channel_id=1, source_target_pairs={{0,1},{3,2},{1,0},{2,3},{4,5},{7,6},{5,4},{6,7},{8,9},{11,10},{9,8... | collective-permute-start | bytes 1474568 | tf_op jit(solution)/shard_map/ppermute | solution.py:454
  463.6 14.9 %collective-permute-start.49 = (bf16[192,1280]{1,0:T(8,128)(2,1)}, bf16[192,1280]{1,0:T(8,128)(2,1)S(1)}, u32[]{:S(2)}, u32[]{:S(2)}) collective-permute-start(bf16[192,1280]{1,0:T(8,128)(2,1)} %copy-done.198), channel_id=1, source_target_pairs={{1,2},{2,1},{5,6},{6,5},{9,10},{10,9},{13,14},{14,13},{17,18},{18,... | collective-permute-start | bytes 1474568 | tf_op jit(solution)/shard_map/ppermute | solution.py:450
  488.4 10.2 %collective-permute-start.52 = (bf16[192,1280]{1,0:T(8,128)(2,1)S(1)}, bf16[192,1280]{1,0:T(8,128)(2,1)S(1)}, u32[]{:S(2)}, u32[]{:S(2)}) collective-permute-start(bf16[192,1280]{1,0:T(8,128)(2,1)S(1)} %get-tuple-element.715.refs_2_), channel_id=1, source_target_pairs={{0,1},{3,2},{1,0},{2,3},{4,5},{7,6},{5,4},{6,7},{8,9},{11,10},{9,8... | collective-permute-start | bytes 1474568 | tf_op jit(solution)/shard_map/ppermute | solution.py:454
  519.4 201.3 %reduce-scatter.15.cloned.1.call-start = ((), (), s32[]{:S(2)}) async-start(), calls=%async_computation.13 | async-start | bytes 3686400 | tf_op jit(solution)/shard_map/reduce_scatter | solution.py:563
  532.9 21.5 %collective-permute-start.59 = (bf16[192,1280]{1,0:T(8,128)(2,1)}, bf16[192,1280]{1,0:T(8,128)(2,1)}, u32[]{:S(2)}, u32[]{:S(2)}) collective-permute-start(bf16[192,1280]{1,0:T(8,128)(2,1)} %get-tuple-element.742.refs_2_), channel_id=1, source_target_pairs={{1,2},{2,1},{5,6},{6,5},{9,10},{10,9},{13,14},{14,13},{17,18},{18,... | collective-permute-start | bytes 1474568 | tf_op jit(solution)/shard_map/ppermute | solution.py:450
  542.6 11.8 %collective-permute-start.58 = (bf16[192,1280]{1,0:T(8,128)(2,1)}, bf16[192,1280]{1,0:T(8,128)(2,1)}, u32[]{:S(2)}, u32[]{:S(2)}) collective-permute-start(bf16[192,1280]{1,0:T(8,128)(2,1)} %get-tuple-element.753.refs_2_), channel_id=1, source_target_pairs={{0,1},{3,2},{1,0},{2,3},{4,5},{7,6},{5,4},{6,7},{8,9},{11,10},{9,8... | collective-permute-start | bytes 1474568 | tf_op jit(solution)/shard_map/ppermute | solution.py:454
  557.0 19.2 %collective-permute-start.60 = (bf16[192,1280]{1,0:T(8,128)(2,1)S(1)}, bf16[192,1280]{1,0:T(8,128)(2,1)S(1)}, u32[]{:S(2)}, u32[]{:S(2)}) collective-permute-start(bf16[192,1280]{1,0:T(8,128)(2,1)S(1)} %get-tuple-element.754.refs_0_), channel_id=1, source_target_pairs={{1,2},{2,1},{5,6},{6,5},{9,10},{10,9},{13,14},{14,13},{17,18},{18,... | collective-permute-start | bytes 1474568 | tf_op jit(solution)/shard_map/ppermute | solution.py:450
  557.7 19.3 %collective-permute-start.61 = (bf16[192,1280]{1,0:T(8,128)(2,1)S(1)}, bf16[192,1280]{1,0:T(8,128)(2,1)S(1)}, u32[]{:S(2)}, u32[]{:S(2)}) collective-permute-start(bf16[192,1280]{1,0:T(8,128)(2,1)S(1)} %get-tuple-element.768.refs_2_), channel_id=1, source_target_pairs={{1,0},{2,3},{5,4},{6,7},{9,8},{10,11},{13,12},{14,15},{17,16},{18,... | collective-permute-start | bytes 1474568 | tf_op jit(solution)/shard_map/ppermute | solution.py:454
  589.1 11.7 %collective-permute-start.62 = (bf16[2,768,512]{2,1,0:T(8,128)(2,1)S(1)}, bf16[2,768,512]{2,1,0:T(8,128)(2,1)S(1)}, u32[]{:S(2)}, u32[]{:S(2)}) collective-permute-start(bf16[2,768,512]{2,1,0:T(8,128)(2,1)S(1)} %get-tuple-element.784), channel_id=1, source_target_pairs={{0,4},{4,0},{1,5},{5,1},{2,6},{6,2},{3,7},{7,3},{8,12},{12,8},{9,1... | collective-permute-start | bytes 4718600 | tf_op jit(solution)/shard_map/ppermute | solution.py:746
  597.7 17.0 %collective-permute-start.63 = (bf16[192,1280]{1,0:T(8,128)(2,1)}, bf16[192,1280]{1,0:T(8,128)(2,1)}, u32[]{:S(2)}, u32[]{:S(2)}) collective-permute-start(bf16[192,1280]{1,0:T(8,128)(2,1)} %turn.64.refs_2_), channel_id=1, source_target_pairs={{1,0},{2,3},{5,4},{6,7},{9,8},{10,11},{13,12},{14,15},{17,16},{18,... | collective-permute-start | bytes 1474568 | tf_op jit(solution)/shard_map/ppermute | solution.py:454
  604.3 24.7 %collective-permute-start.65 = (bf16[192,1280]{1,0:T(8,128)(2,1)}, bf16[192,1280]{1,0:T(8,128)(2,1)}, u32[]{:S(2)}, u32[]{:S(2)}) collective-permute-start(bf16[192,1280]{1,0:T(8,128)(2,1)} %get-tuple-element.786.refs_0_), channel_id=1, source_target_pairs={{0,1},{3,2},{4,5},{7,6},{8,9},{11,10},{12,13},{15,14},{16,17},{19,... | collective-permute-start | bytes 1474568 | tf_op jit(solution)/shard_map/ppermute | solution.py:454
  611.6 111.5 %reduce-scatter.13.cloned.1.call-start = ((), (), s32[]{:S(2)}) async-start(), calls=%async_computation.12 | async-start | bytes 2048000 | tf_op jit(solution)/shard_map/reduce_scatter | solution.py:561
  626.9 16.8 %collective-permute-start.67 = (bf16[192,1280]{1,0:T(8,128)(2,1)}, bf16[192,1280]{1,0:T(8,128)(2,1)}, u32[]{:S(2)}, u32[]{:S(2)}) collective-permute-start(bf16[192,1280]{1,0:T(8,128)(2,1)} %get-tuple-element.794.refs_0_), channel_id=1, source_target_pairs={{0,1},{3,2},{4,5},{7,6},{8,9},{11,10},{12,13},{15,14},{16,17},{19,... | collective-permute-start | bytes 1474568 | tf_op jit(solution)/shard_map/ppermute | solution.py:454
  631.0 12.7 %collective-permute-start.68 = (bf16[192,1280]{1,0:T(8,128)(2,1)}, bf16[192,1280]{1,0:T(8,128)(2,1)}, u32[]{:S(2)}, u32[]{:S(2)}) collective-permute-start(bf16[192,1280]{1,0:T(8,128)(2,1)} %turn.65.refs_2_), channel_id=1, source_target_pairs={{1,2},{2,1},{5,6},{6,5},{9,10},{10,9},{13,14},{14,13},{17,18},{18,... | collective-permute-start | bytes 1474568 | tf_op jit(solution)/shard_map/ppermute | solution.py:450
  632.9 15.5 %collective-permute-start.69 = (bf16[160,1280]{1,0:T(8,128)(2,1)}, bf16[160,1280]{1,0:T(8,128)(2,1)}, u32[]{:S(2)}, u32[]{:S(2)}) collective-permute-start(bf16[160,1280]{1,0:T(8,128)(2,1)} %reduce-scatter.7.cloned.1.call-done), channel_id=1, source_target_pairs={{0,4},{4,0},{1,5},{5,1},{2,6},{6,2},{3,7},{7,3},{8,12},{12,8},{9,1... | collective-permute-start | bytes 1228808 | tf_op jit(solution)/shard_map/ppermute | solution.py:567
  645.5 12.8 %collective-permute-start.71 = (bf16[192,1280]{1,0:T(8,128)(2,1)S(1)}, bf16[192,1280]{1,0:T(8,128)(2,1)S(1)}, u32[]{:S(2)}, u32[]{:S(2)}) collective-permute-start(bf16[192,1280]{1,0:T(8,128)(2,1)S(1)} %get-tuple-element.802.refs_2_), channel_id=1, source_target_pairs={{1,2},{2,1},{5,6},{6,5},{9,10},{10,9},{13,14},{14,13},{17,18},{18,... | collective-permute-start | bytes 1474568 | tf_op jit(solution)/shard_map/ppermute | solution.py:450
  646.4 11.8 %collective-permute-start.70 = (bf16[192,1280]{1,0:T(8,128)(2,1)S(1)}, bf16[192,1280]{1,0:T(8,128)(2,1)S(1)}, u32[]{:S(2)}, u32[]{:S(2)}) collective-permute-start(bf16[192,1280]{1,0:T(8,128)(2,1)S(1)} %get-tuple-element.810.refs_2_), channel_id=1, source_target_pairs={{0,1},{3,2},{1,0},{2,3},{4,5},{7,6},{5,4},{6,7},{8,9},{11,10},{9,8... | collective-permute-start | bytes 1474568 | tf_op jit(solution)/shard_map/ppermute | solution.py:454
  673.0 12.8 %collective-permute-start.72 = (bf16[192,1280]{1,0:T(8,128)(2,1)}, bf16[192,1280]{1,0:T(8,128)(2,1)S(1)}, u32[]{:S(2)}, u32[]{:S(2)}) collective-permute-start(bf16[192,1280]{1,0:T(8,128)(2,1)} %copy-done.210), channel_id=1, source_target_pairs={{0,1},{3,2},{1,0},{2,3},{4,5},{7,6},{5,4},{6,7},{8,9},{11,10},{9,8... | collective-permute-start | bytes 1474568 | tf_op jit(solution)/shard_map/ppermute | solution.py:454
  674.5 11.3 %collective-permute-start.73 = (bf16[192,1280]{1,0:T(8,128)(2,1)S(1)}, bf16[192,1280]{1,0:T(8,128)(2,1)S(1)}, u32[]{:S(2)}, u32[]{:S(2)}) collective-permute-start(bf16[192,1280]{1,0:T(8,128)(2,1)S(1)} %get-tuple-element.811.refs_2_), channel_id=1, source_target_pairs={{1,2},{2,1},{5,6},{6,5},{9,10},{10,9},{13,14},{14,13},{17,18},{18,... | collective-permute-start | bytes 1474568 | tf_op jit(solution)/shard_map/ppermute | solution.py:450
  686.6 15.9 %collective-permute-start.75 = (bf16[192,1280]{1,0:T(8,128)(2,1)S(1)}, bf16[192,1280]{1,0:T(8,128)(2,1)S(1)}, u32[]{:S(2)}, u32[]{:S(2)}) collective-permute-start(bf16[192,1280]{1,0:T(8,128)(2,1)S(1)} %get-tuple-element.833.refs_2_), channel_id=1, source_target_pairs={{1,0},{2,3},{5,4},{6,7},{9,8},{10,11},{13,12},{14,15},{17,16},{18,... | collective-permute-start | bytes 1474568 | tf_op jit(solution)/shard_map/ppermute | solution.py:454
  689.9 23.0 %collective-permute-start.76 = (bf16[192,1280]{1,0:T(8,128)(2,1)S(1)}, bf16[192,1280]{1,0:T(8,128)(2,1)S(1)}, u32[]{:S(2)}, u32[]{:S(2)}) collective-permute-start(bf16[192,1280]{1,0:T(8,128)(2,1)S(1)} %turn.69.refs_2_), channel_id=1, source_target_pairs={{1,0},{2,3},{5,4},{6,7},{9,8},{10,11},{13,12},{14,15},{17,16},{18,... | collective-permute-start | bytes 1474568 | tf_op jit(solution)/shard_map/ppermute | solution.py:454
  (336 other events, 1983.4 us)
Sparse Core Ops, SparseCore 0:
  11.6 35.3 all-gather.3
  48.9 46.7 all-gather.5
  98.1 60.4 all-gather.7
  318.9 50.2 reduce-scatter.10
  373.0 46.8 reduce-scatter.8
  462.4 48.2 reduce-scatter.6
  519.5 53.0 reduce-scatter.16
  611.8 44.9 reduce-scatter.14
  673.1 29.6 reduce-scatter.12
